TPU v7x, 32 devices: a whole 2x2x4 slice. The times are simulated.
32 devices in a mesh: dp: 16 (over z, y, x), tensor: 2 (over core).
Axes of the slice: x: 2, y: 2, z: 4, core: 2. Of those that a mesh axis runs over, the one named last changes fastest.
Arguments:
- tokens: bfloat16 [128, 197, 384], P(('dp', 'tensor')), may hold values from -6 to 6
- norm1_gain: float32 [384], replicated, may hold values from 0.5 to 1.5
- norm1_bias: float32 [384], replicated, may hold values from -3 to 3
- qkv_weight: bfloat16 [384, 1152], P('dp', 'tensor'), may hold values from -0.3125 to 0.3125
- mix_pre: float32 [6, 6], replicated, may hold values from -3 to 3
- mix_post: float32 [6, 6], replicated, may hold values from -3 to 3
- proj_weight: bfloat16 [384, 384], P('dp', 'tensor'), may hold values from -1.25 to 1.25
- proj_bias: float32 [384], replicated, may hold values from -3 to 3
- norm2_gain: float32 [384], replicated, may hold values from 0.5 to 1.5
- norm2_bias: float32 [384], replicated, may hold values from -3 to 3
- fc1_weight: bfloat16 [384, 1536], P(None, 'tensor'), may hold values from -0.3125 to 0.3125
- fc1_bias: bfloat16 [1536], P('tensor'), may hold values from -3 to 3
- conv_weight: bfloat16 [49, 1536], P(None, 'tensor'), may hold values from -0.875 to 0.875
- fc2_weight: bfloat16 [1536, 384], P('tensor'), may hold values from -0.15625 to 0.15625
- fc2_bias: float32 [384], replicated, may hold values from -3 to 3
- cotangent: bfloat16 [128, 197, 384], P(('dp', 'tensor')), may hold values from -6 to 6
Outputs:
- block_out: bfloat16 [128, 197, 384], P(('dp', 'tensor'))
- grad_tokens: float32 [128, 197, 384], P(('dp', 'tensor'))
- grad_norm1_gain: float32 [384], replicated
- grad_norm1_bias: float32 [384], replicated
- grad_qkv: float32 [384, 1152], P('dp', 'tensor')
- grad_mix_pre: float32 [6, 6], replicated
- grad_mix_post: float32 [6, 6], replicated
- grad_proj: float32 [384, 384], P('dp', 'tensor')
- grad_proj_bias: float32 [384], replicated
- grad_norm2_gain: float32 [384], replicated
- grad_norm2_bias: float32 [384], replicated
- grad_fc1: float32 [384, 1536], P(None, 'tensor')
- grad_fc1_bias: float32 [1536], P('tensor')
- grad_conv: float32 [49, 1536], P(None, 'tensor')
- grad_fc2: float32 [1536, 384], P('tensor')
- grad_fc2_bias: float32 [384], replicated
All inputs are finite; a program needn't handle non-finite values.
Results may differ from a plain program's by a relative error of at most 0.014.
The roundings to bfloat16 on the way count: a program that leaves them out, or rounds other values in their place, can miss the bound.
Values may be sent and summed in bfloat16 or wider, within the bound.
A program may use at most 448 MiB of HBM per device.

v0:
```python
import jax
import jax.numpy as jnp
from jax import lax
from jax.sharding import PartitionSpec as P

HEADS = 6
HEAD_DIM = 64
KS = 7
GRID = 14


highest = lax.Precision.HIGHEST


def layer_norm(values, norm_gain, norm_bias):
    centred = values - jnp.mean(values, axis=-1, keepdims=True)
    spread = jnp.mean(centred * centred, axis=-1, keepdims=True)
    return centred * lax.rsqrt(spread + 1e-05) * norm_gain + norm_bias


def depthwise(hidden, kernel):
    images = hidden.shape[0]
    width = hidden.shape[2]
    patches = hidden[:, 1:].reshape(images, GRID, GRID, width)
    radius = KS // 2
    padded = jnp.pad(patches, ((0, 0), (radius, radius), (radius, radius), (0, 0)))
    summed = jnp.zeros_like(patches)
    for tap_row in range(KS):
        for tap_col in range(KS):
            summed = (
                summed
                + kernel[tap_row * KS + tap_col]
                * padded[:, tap_row : tap_row + GRID, tap_col : tap_col + GRID]
            )
    return jnp.concatenate([hidden[:, :1], summed.reshape(images, GRID * GRID, width)], axis=1)


def gelu_conv(hidden, kernel):
    return depthwise(jax.nn.gelu(hidden, approximate=False), kernel)


def mixed_of(query_rows, key_rows, mix_pre, scaling):
    scores = (
        jnp.einsum("bqhe,bkhe->bhqk", query_rows, key_rows, preferred_element_type=jnp.float32)
        * scaling
    )
    mixed_scores = jnp.einsum("gh,bhqk->bgqk", mix_pre, scores, precision=highest)
    return (scores, mixed_scores)


def shards(
    tokens,
    norm1_gain,
    norm1_bias,
    qkv_weight,
    mix_pre,
    mix_post,
    proj_weight,
    proj_bias,
    norm2_gain,
    norm2_bias,
    fc1_weight,
    fc1_bias,
    conv_weight,
    fc2_weight,
    fc2_bias,
    cotangent,
):
    scaling = HEAD_DIM ** (-0.5)
    images = tokens.shape[0]
    seq_len = tokens.shape[1]
    width = tokens.shape[2]
    qkv_rows, proj_rows = (
        lax.all_gather(qkv_weight, "dp", axis=0, tiled=True),
        lax.all_gather(proj_weight, "dp", axis=0, tiled=True),
    )
    qkv_full, proj_full = (
        lax.all_gather(qkv_rows, "tensor", axis=1, tiled=True),
        lax.all_gather(proj_rows, "tensor", axis=1, tiled=True),
    )
    inputs = tokens.astype(jnp.float32)
    normed, norm1_back = jax.vjp(layer_norm, inputs, norm1_gain, norm1_bias)
    normed_low = normed.astype(jnp.bfloat16)
    packed = jnp.einsum(
        "bsd,dc->bsc", normed_low, qkv_full, preferred_element_type=jnp.float32
    ).astype(jnp.bfloat16)
    packed = packed.reshape(images, seq_len, 3, HEADS, HEAD_DIM)
    query_rows = packed[:, :, 0]
    key_rows = packed[:, :, 1]
    value_rows = packed[:, :, 2]
    scores, mixed_scores = mixed_of(query_rows, key_rows, mix_pre, scaling)
    row_top = jnp.max(mixed_scores, axis=-1, keepdims=True)
    log_total = row_top + jnp.log(jnp.sum(jnp.exp(mixed_scores - row_top), axis=-1, keepdims=True))
    probabilities = jnp.exp(mixed_scores - log_total)
    attn_weights = jnp.einsum("gh,bhqk->bgqk", mix_post, probabilities, precision=highest).astype(
        jnp.bfloat16
    )
    attended = jnp.einsum(
        "bhqk,bkhe->bqhe", attn_weights, value_rows, preferred_element_type=jnp.float32
    ).astype(jnp.bfloat16)
    attended = attended.reshape(images, seq_len, width)
    branch = (
        jnp.einsum("bsd,de->bse", attended, proj_full, preferred_element_type=jnp.float32)
        + proj_bias
    )
    middle = inputs + branch
    normed_two, norm2_back = jax.vjp(layer_norm, middle, norm2_gain, norm2_bias)
    normed_two_low = normed_two.astype(jnp.bfloat16)
    grad_output = cotangent.astype(jnp.float32)
    pair_rows = lax.all_gather(normed_two_low, "tensor", axis=0, tiled=True)
    hidden = jnp.einsum(
        "bsd,df->bsf", pair_rows, fc1_weight, preferred_element_type=jnp.float32
    ) + fc1_bias.astype(jnp.float32)
    convolved, conv_back = jax.vjp(gelu_conv, hidden, conv_weight.astype(jnp.float32))
    convolved_low = convolved.astype(jnp.bfloat16)
    piece = convolved_low
    output = (
        lax.psum_scatter(
            jnp.einsum("bsf,fd->bsd", piece, fc2_weight, preferred_element_type=jnp.float32).astype(
                jnp.bfloat16
            ),
            "tensor",
            scatter_dimension=0,
            tiled=True,
        ).astype(jnp.float32)
        + fc2_bias
    )
    block_out = (middle + output).astype(jnp.bfloat16)
    pair_grads = lax.all_gather(cotangent, "tensor", axis=0, tiled=True)
    grad_fc2 = jnp.einsum(
        "bsf,bsd->fd", convolved_low, pair_grads, preferred_element_type=jnp.float32
    )
    grad_convolved = jnp.einsum(
        "bsd,fd->bsf", pair_grads, fc2_weight, preferred_element_type=jnp.float32
    )
    grad_hidden, grad_conv = conv_back(grad_convolved)
    grad_hidden_low = grad_hidden.astype(jnp.bfloat16)
    grad_fc1 = jnp.einsum(
        "bsd,bsf->df", pair_rows, grad_hidden_low, preferred_element_type=jnp.float32
    )
    grad_fc1_bias = jnp.sum(grad_hidden_low.astype(jnp.float32), axis=(0, 1))
    piece = grad_hidden_low
    grad_normed_two = lax.psum_scatter(
        jnp.einsum("bsf,df->bsd", piece, fc1_weight, preferred_element_type=jnp.float32).astype(
            jnp.bfloat16
        ),
        "tensor",
        scatter_dimension=0,
        tiled=True,
    ).astype(jnp.float32)
    grad_fc1, grad_conv, grad_fc2, grad_fc1_bias = lax.psum(
        (grad_fc1, grad_conv, grad_fc2, grad_fc1_bias), "dp"
    )
    grad_fc2_bias = jnp.sum(grad_output, axis=(0, 1))
    from_norm_two, grad_norm2_gain, grad_norm2_bias = norm2_back(grad_normed_two)
    grad_middle = grad_output + from_norm_two
    grad_middle_low = grad_middle.astype(jnp.bfloat16)
    grad_proj = jnp.einsum(
        "bsd,bse->de", attended, grad_middle_low, preferred_element_type=jnp.float32
    )
    grad_proj_bias = jnp.sum(grad_middle_low.astype(jnp.float32), axis=(0, 1))
    grad_attended = jnp.einsum(
        "bse,de->bsd", grad_middle_low, proj_full, preferred_element_type=jnp.float32
    ).astype(jnp.bfloat16)
    grad_attended = grad_attended.reshape(images, seq_len, HEADS, HEAD_DIM)
    scores, mixed_scores = mixed_of(query_rows, key_rows, mix_pre, scaling)
    probabilities = jnp.exp(mixed_scores - log_total)
    attn_weights = jnp.einsum("gh,bhqk->bgqk", mix_post, probabilities, precision=highest).astype(
        jnp.bfloat16
    )
    grad_value = jnp.einsum(
        "bhqk,bqhe->bkhe", attn_weights, grad_attended, preferred_element_type=jnp.float32
    )
    grad_weights = jnp.einsum(
        "bqhe,bkhe->bhqk", grad_attended, value_rows, preferred_element_type=jnp.float32
    )
    grad_mix_post = jnp.einsum("bgqk,bhqk->gh", grad_weights, probabilities, precision=highest)
    grad_probs = jnp.einsum("gh,bgqk->bhqk", mix_post, grad_weights, precision=highest)
    grad_mixed = probabilities * (
        grad_probs - jnp.sum(probabilities * grad_probs, axis=-1, keepdims=True)
    )
    grad_mix_pre = jnp.einsum("bgqk,bhqk->gh", grad_mixed, scores, precision=highest)
    grad_scores = jnp.einsum("gh,bgqk->bhqk", mix_pre, grad_mixed, precision=highest).astype(
        jnp.bfloat16
    )
    grad_query = (
        jnp.einsum("bhqk,bkhe->bqhe", grad_scores, key_rows, preferred_element_type=jnp.float32)
        * scaling
    )
    grad_key = (
        jnp.einsum("bhqk,bqhe->bkhe", grad_scores, query_rows, preferred_element_type=jnp.float32)
        * scaling
    )
    grad_packed = jnp.stack([grad_query, grad_key, grad_value], axis=2).astype(jnp.bfloat16)
    grad_packed = grad_packed.reshape(images, seq_len, 3 * width)
    grad_qkv = jnp.einsum(
        "bsd,bsc->dc", normed_low, grad_packed, preferred_element_type=jnp.float32
    )
    grad_normed = jnp.einsum(
        "bsc,dc->bsd", grad_packed, qkv_full, preferred_element_type=jnp.float32
    )
    from_norm_one, grad_norm1_gain, grad_norm1_bias = norm1_back(grad_normed)
    grad_tokens = grad_middle + from_norm_one
    grad_qkv, grad_proj = (
        lax.psum_scatter(
            grad_qkv.astype(jnp.bfloat16), "tensor", scatter_dimension=1, tiled=True
        ).astype(jnp.float32),
        lax.psum_scatter(
            grad_proj.astype(jnp.bfloat16), "tensor", scatter_dimension=1, tiled=True
        ).astype(jnp.float32),
    )
    grad_qkv, grad_proj = (
        lax.psum_scatter(grad_qkv, "dp", scatter_dimension=0, tiled=True),
        lax.psum_scatter(grad_proj, "dp", scatter_dimension=0, tiled=True),
    )
    small_sums = lax.psum(
        (
            grad_norm1_gain,
            grad_norm1_bias,
            grad_mix_pre,
            grad_mix_post,
            grad_proj_bias,
            grad_norm2_gain,
            grad_norm2_bias,
            grad_fc2_bias,
        ),
        ("dp", "tensor"),
    )
    return (
        block_out,
        grad_tokens,
        small_sums[0],
        small_sums[1],
        grad_qkv,
        small_sums[2],
        small_sums[3],
        grad_proj,
        small_sums[4],
        small_sums[5],
        small_sums[6],
        grad_fc1,
        grad_fc1_bias,
        grad_conv,
        grad_fc2,
        small_sums[7],
    )


def solution(mesh):
    in_specs = (
        P(("dp", "tensor"), None, None),
        P(),
        P(),
        P("dp", "tensor"),
        P(),
        P(),
        P("dp", "tensor"),
        P(),
        P(),
        P(),
        P(None, "tensor"),
        P("tensor"),
        P(None, "tensor"),
        P("tensor", None),
        P(),
        P(("dp", "tensor"), None, None),
    )
    out_specs = (
        P(("dp", "tensor"), None, None),
        P(("dp", "tensor"), None, None),
        P(),
        P(),
        P("dp", "tensor"),
        P(),
        P(),
        P("dp", "tensor"),
        P(),
        P(),
        P(),
        P(None, "tensor"),
        P("tensor"),
        P(None, "tensor"),
        P("tensor", None),
        P(),
    )
    return jax.shard_map(shards, mesh=mesh, in_specs=in_specs, out_specs=out_specs, check_vma=False)
```

profile of v0, /device:TPU:0, one launch (start us, length us, event | category | flops | bytes accessed | tf_op | source)
XLA Modules:
  0.0 794.7 jit_solution(16847367628613943019)
XLA Ops:
  7.3 2.1 copy.107
  9.4 1.3 convert_reduce_fusion.2
  10.7 45.3 %all_gather.18 = bf16[384,576]{1,0:T(8,128)(2,1)S(1)} all-gather(bf16[24,576]{1,0:T(8,128)(2,1)} %param.19), channel_id=1, replica_groups=mesh['dp'=16,'tensor'=2] {'dp'}, dimensions={0}, use_global_device_ids=true | all-gather | bytes 470016 | tf_op jit(solution)/shard_map/all_gather | solution.py:74
  56.3 2.4 all_gather.19
  60.4 2.6 convolution_convert_fusion
  63.0 2.9 copy.97
  66.8 8.1 %bitcast_reduce_fusion = (f32[4,6,197]{1,2,0:T(8,128)S(1)}, f32[4,197,197,6]{2,3,1,0:T(8,128)S(1)}) fusion(f32[6,6]{1,0:T(8,128)S(1)} %copy-done.91, f32[4,6,197,197]{3,2,1,0:T(8,128)S(1)} %broadcast_multiply_fusion), kind=kOutput, calls=%fused_computation.64 | convolution fusion | flops 67988640 | bytes 7470384 | tf_op jit(solution)/shard_map/gh,bhqk->bgqk/dot_general | solution.py:47
  74.9 2.0 fusion.11
  77.1 7.2 convert_bitcast_fusion.1
  84.3 1.9 fusion.49
  86.3 36.6 %all_gather.20 = bf16[384,192]{1,0:T(8,128)(2,1)S(1)} all-gather(bf16[24,192]{1,0:T(8,128)(2,1)S(1)} %copy-done.126), channel_id=1, replica_groups=mesh['dp'=16,'tensor'=2] {'dp'}, dimensions={0}, use_global_device_ids=true | all-gather | bytes 156672 | tf_op jit(solution)/shard_map/all_gather | solution.py:75
  123.1 2.0 all_gather.21
  125.1 2.0 fusion.116
  128.8 1.1 add_convert_fusion.3
  132.5 2.8 fusion.91
  135.8 1.9 copy-done.9
  137.6 1.5 copy.109
  139.3 20.9 %broadcast_multiply_fusion.3 = (f32[8,14,14,768]{3,0,2,1:T(8,128)}, f32[8,14,14,768]{3,0,2,1:T(8,128)}, f32[8,14,14,768]{3,0,2,1:T(8,128)}, f32[8,14,14,768]{3,0...) fusion(f32[8,14,14,768]{3,0,2,1:T(8,128)S(1)} %bitcast.167, ...), kind=kLoop, calls=%fused_computation.153 | loop fusion | flops 15654912 | bytes 67476480 | tf_op jit(solution)/shard_map/transpose(jvp())/mul | solution.py:32
  160.5 28.6 %broadcast_multiply_fusion.1 = (f32[8,14,14,768]{3,0,2,1:T(8,128)}, f32[8,14,14,768]{3,0,2,1:T(8,128)}, f32[8,14,14,768]{3,0,2,1:T(8,128)}, f32[8,14,14,768]{3,0...) fusion(f32[8,14,14,768]{3,0,2,1:T(8,128)} %bitcast.168, ...), kind=kLoop, calls=%fused_computation.151 | loop fusion | flops 21676032 | bytes 91576320 | tf_op jit(solution)/shard_map/transpose(jvp())/mul | solution.py:32
  189.1 28.6 %broadcast_multiply_fusion.2 = (f32[8,14,14,768]{3,0,2,1:T(8,128)}, f32[8,14,14,768]{3,0,2,1:T(8,128)}, f32[8,14,14,768]{3,0,2,1:T(8,128)}, f32[8,14,14,768]{3,0...) fusion(f32[8,14,14,768]{3,0,2,1:T(8,128)} %bitcast.169, ...), kind=kLoop, calls=%fused_computation.152 | loop fusion | flops 21676032 | bytes 91576320 | tf_op jit(solution)/shard_map/transpose(jvp())/mul | solution.py:32
  217.7 72.5 %pad_add_fusion = f32[8,20,20,768]{3,0,2,1:T(8,128)S(1)} fusion(f32[8,14,14,768]{3,0,2,1:T(8,128)} %get-tuple-element.196, f32[8,14,14,768]{3,0,2,1:T(8,128)} %get-tuple-element.197, f32[8,14,14,768]{3,0,2,1:T(8,128)} %get-tuple-element.198, f32[8,14,14,768]{3,0,2,1:T(8,128)} %get-tuple-element.199, f32[8,14,14,768]{3,0,2,1:T(8,128)} %get-tuple-element.200, ...), kind=kLoop, calls=%fused_computation.48 | loop fusion | flops 103219200 | bytes 216956928 | tf_op jit(solution)/shard_map/transpose(jvp())/add_any | solution.py:33
  290.2 7.0 pad_add_fusion.1
  297.2 3.8 copy.110
  301.1 17.6 %convert_reduce_fusion = (f32[768]{0:T(1024)}, bf16[8,197,768]{2,1,0:T(8,128)(2,1)S(1)}, f32[8,197,768]{2,1,0:T(8,128)}, f32[8,197,768]{2,1,0:T(8,128)}) fusion(f32[8,196,768]{2,1,0:T(8,128)} %copy.110, f32[8,197,768]{2,1,0:T(8,128)} %copy-done.9, pred[197]{0:T(512)(128)(4,1)S(1)} %copy-done.142, f32[768]{0:T(1024)S(1)} %copy-done.94, ...), kind=kOutput, calls=%fused_computation.70 | convolution fusion | flops 1022760192 | bytes 23568580 | tf_op jit(solution)/shard_map/bsd,df->bsf/dot_general | solution.py:111
  318.6 1.5 copy-done.143
  320.1 2.5 convolution_convert_fusion.1
  322.7 4.8 multiply_multiply_fusion.5
  328.2 1.6 multiply_reduce_fusion
  330.8 1.6 copy.105
  332.5 42.9 %add_convert_fusion.1 = bf16[8,14,14,768]{3,0,2,1:T(8,128)(2,1)} fusion(f32[8,14,14,768]{3,0,2,1:T(8,128)S(1)} %bitcast.175, f32[768]{0:T(1024)S(1)} %get-tuple-element.121, f32[768]{0:T(1024)S(1)} %get-tuple-element.122, f32[768]{0:T(1024)S(1)} %copy-done.51, f32[768]{0:T(1024)S(1)} %copy-done.53, f32[768]{0:T(1024)S(1)} %copy-done.55, ...), kind=kLoop, calls=%fused_computation.139 | loop fusion | flops 118013952 | bytes 7375872 | tf_op jit(solution)/shard_map/convert.11
  375.5 12.8 %multiply_reduce_fusion.48 = (f32[768]{0:T(1024)S(1)}, f32[768]{0:T(1024)}, f32[768]{0:T(1024)}, f32[768]{0:T(1024)}, f32[768]{0:T(1024)}, /*index=5*/f32[768]{0...) fusion(f32[8,14,14,768]{3,0,2,1:T(8,128)S(1)} %bitcast.174, ...), kind=kLoop, calls=%fused_computation.138 | loop fusion | flops 43338240 | bytes 9689088 | tf_op jit(solution)/shard_map/transpose(jvp())/reduce_sum | solution.py:32
  388.3 2.2 convert_reduce_fusion.1
  390.5 2.4 fusion.74
  392.9 2.5 convert_reduce_fusion.4
  395.4 1.3 fusion.75
  396.8 32.2 %multiply_reduce_fusion.47 = (f32[768]{0:T(1024)S(1)}, f32[768]{0:T(1024)S(1)}, f32[768]{0:T(1024)S(1)}, f32[768]{0:T(1024)S(1)}, f32[768]{0:T(1024)S(1)}, /*ind...) fusion(f32[8,14,14,768]{3,0,2,1:T(8,128)} %bitcast.170, ...), kind=kLoop, calls=%fused_computation.137 | loop fusion | flops 43338240 | bytes 9689088 | tf_op jit(solution)/shard_map/transpose(jvp())/reduce_sum | solution.py:32
  429.2 1.0 slice.766
  449.2 2.5 fusion.41
  452.3 1.4 convolution_convert_fusion.2
  453.7 2.2 copy.111
  455.9 2.4 fusion.90
  458.4 12.0 %fusion.8 = (f32[4,6,197]{1,2,0:T(8,128)S(1)}, f32[4,197,197,6]{2,3,1,0:T(8,128)S(1)}) fusion(f32[4,197,197,6]{2,3,1,0:T(8,128)} %copy-done.1, f32[4,6,197]{1,2,0:T(8,128)S(1)} %copy-done.16, f32[6,6]{1,0:T(8,128)S(1)} %copy-done.90, f32[4,6,197,197]{3,2,1,0:T(8,128)S(1)} %fusion.90), kind=kOutput, calls=%fused_computation.60 | convolution fusion | flops 69851472 | bytes 11214960 | tf_op jit(solution)/shard_map/gh,bgqk->bhqk/dot_general | solution.py:178
  471.1 8.8 %convert_bitcast_fusion = bf16[4,6,197,197]{3,1,2,0:T(8,128)(2,1)S(1)} fusion(f32[4,197,197,6]{2,3,1,0:T(8,128)S(1)} %get-tuple-element.247, f32[4,197,197,6]{2,3,1,0:T(8,128)S(1)} %bitcast.164, f32[4,6,197]{1,2,0:T(8,128)S(1)} %get-tuple-element.246, f32[4,6,197]{1,2,0:T(8,128)S(1)} %copy-done.16, f32[6,6]{1,0:T(8,128)S(1)} %copy-done.92), kind=kOutput, calls=%fused_computation.143 | convolution fusion | flops 70787616 | bytes 9352128 | tf_op jit(solution)/shard_map/gh,bgqk->bhqk/dot_general | solution.py:183
  479.9 0.9 fusion.60
  482.4 1.4 copy-done.30
  483.8 2.5 fusion.24
  486.8 20.2 %multiply_reduce_fusion.46 = (f32[768]{0:T(1024)S(1)}, f32[768]{0:T(1024)S(1)}, f32[768]{0:T(1024)S(1)}, f32[768]{0:T(1024)S(1)}, f32[768]{0:T(1024)S(1)}, /*ind...) fusion(f32[8,14,14,768]{3,0,2,1:T(8,128)} %bitcast.171, ...), kind=kLoop, calls=%fused_computation.136 | loop fusion | flops 28892160 | bytes 9670656 | tf_op jit(solution)/shard_map/transpose(jvp())/reduce_sum | solution.py:32
  507.4 1.0 pad_add_fusion.7
  508.5 2.6 fusion.48
  511.1 2.3 convolution_bitcast_fusion.1
  513.7 3.4 fusion.113
  517.2 1.0 copy-done.22
  518.9 18.7 %fusion.81 = f32[6,6]{1,0:T(8,128)S(1)} fusion(f32[4,197,197,6]{2,3,1,0:T(8,128)} %copy-done.1, f32[4,6,197]{1,2,0:T(8,128)S(1)} %copy-done.16, f32[4,6,197,197]{3,2,1,0:T(8,128)} %copy-done.5), kind=kOutput, calls=%fused_computation.257 | convolution fusion | flops 67993368 | bytes 7470384 | tf_op jit(solution)/shard_map/bgqk,bhqk->gh/dot_general | solution.py:177
  537.7 17.7 %fusion.76 = f32[6,6]{1,0:T(8,128)S(1)} fusion(f32[4,6,197,197]{3,2,1,0:T(8,128)S(1)} %bitcast.180, f32[4,197,197,6]{2,3,1,0:T(8,128)} %copy-done.8, f32[4,197,197,6]{2,3,1,0:T(8,128)S(1)} %bitcast.166, f32[4,6,197]{1,2,0:T(8,128)S(1)} %copy-done.24, f32[4,6,197]{1,2,0:T(8,128)S(1)} %copy-done.16), kind=kOutput, calls=%fused_computation.256 | convolution fusion | flops 69856200 | bytes 11214960 | tf_op jit(solution)/shard_map/bgqk,bhqk->gh/dot_general | solution.py:182
  555.5 1.8 copy.142
  557.5 2.6 add_add_fusion.2
  560.1 1.1 copy.124
  561.2 1.3 copy.125
  562.5 37.8 %all-reduce.101 = (f32[384]{0:T(512)}, f32[384]{0:T(512)}, f32[6,6]{1,0:T(8,128)}, f32[6,6]{1,0:T(8,128)}, f32[384]{0:T(512)}, /*index=5*/f32[384]{0:T(512)}, f32[384]{0:T(512)}, f32[384]{0:T(512)}) all-reduce(f32[384]{0:T(512)S(1)} %get-tuple-element.114, ...), channel_id=1, replica_groups=mesh['dp'=16,'tensor'=2] {'dp','tensor'}, use_global_device_ids=true, to_apply=%region_14.15 | all-reduce | flops 2376 | bytes 19008 | tf_op jit(solution)/shard_map/psum | solution.py:216
  600.3 94.3 %all-reduce.108 = (f32[384,576]{0,1:T(8,128)S(1)}, f32[768]{0:T(1024)}) all-reduce(bf16[384,576]{0,1:T(8,128)(2,1)} %reduce-scatter.13.cloned.1.call-done, f32[768]{0:T(1024)S(1)} %copy-done.134), channel_id=5, replica_groups=mesh['dp'=16,'tensor'=2] {'dp'}, use_global_device_ids=true, to_apply=%region_18.19.clone | all-reduce | flops 221952 | bytes 1333248
  695.6 85.8 %reduce-scatter.17.cloned.1.call-done = f32[24,192]{1,0:T(8,128)} async-done(((f32[384,192]{1,0:T(8,128)}), f32[24,192]{1,0:T(8,128)}) %reduce-scatter.17.cloned.1.call-update) | async-done | bytes 18448
  781.3 2.4 copy.210
  783.7 1.6 copy.211
  785.3 2.4 copy.212
  (417 shorter events, 33.0 us)
Async XLA Ops:
  7.2 293.9 %copy-start = (bf16[384,768]{1,0:T(8,128)(2,1)S(1)}, bf16[384,768]{1,0:T(8,128)(2,1)}, u32[]{:S(2)}) copy-start(bf16[384,768]{1,0:T(8,128)(2,1)} %param.26) | copy-start | bytes 1769476
  7.2 51.5 %copy-start.13 = (bf16[4,197,384]{2,0,1:T(4,128)(2,1)S(1)}, bf16[4,197,384]{2,0,1:T(4,128)(2,1)}, u32[]{:S(2)}) copy-start(bf16[4,197,384]{2,0,1:T(4,128)(2,1)} %param.16) | copy-start | bytes 1815556
  7.2 53.2 %copy-start.129 = (f32[384]{0:T(512)S(1)}, f32[384]{0:T(512)}, u32[]{:S(2)}) copy-start(f32[384]{0:T(512)} %param.17) | copy-start | bytes 4612
  7.2 53.1 %copy-start.139 = (f32[384]{0:T(512)S(1)}, f32[384]{0:T(512)}, u32[]{:S(2)}) copy-start(f32[384]{0:T(512)} %param.18) | copy-start | bytes 4612
  7.2 125.2 %all-gather.5.cloned.1.call-start = ((), (), s32[]{:S(2)}) async-start(), calls=%async_computation.7 | async-start | bytes 1843200 | tf_op jit(solution)/shard_map/all_gather | solution.py:129
  9.4 291.7 %all-gather.3.cloned.1.call-start = ((), (), s32[]{:S(2)}) async-start(), calls=%async_computation.5 | async-start | bytes 1843200 | tf_op jit(solution)/shard_map/all_gather | solution.py:110
  10.7 48.5 %copy-start.40 = (f32[4,197]{1,0:T(4,128)}, f32[4,197]{1,0:T(4,128)S(1)}, u32[]{:S(2)}) copy-start(f32[4,197]{1,0:T(4,128)S(1)} %broadcast_multiply_fusion.51) | copy-start | bytes 9460
  86.3 42.5 %copy-start.42 = (f32[384]{0:T(512)S(1)}, f32[384]{0:T(512)}, u32[]{:S(2)}) copy-start(f32[384]{0:T(512)} %param.24) | copy-start | bytes 4612
  86.3 42.5 %copy-start.135 = (f32[384]{0:T(512)S(1)}, f32[384]{0:T(512)}, u32[]{:S(2)}) copy-start(f32[384]{0:T(512)} %param.25) | copy-start | bytes 4612
  86.3 43.7 %copy-start.39 = (bf16[49,768]{1,0:T(8,128)(2,1)S(1)}, bf16[49,768]{1,0:T(8,128)(2,1)}, u32[]{:S(2)}) copy-start(bf16[49,768]{1,0:T(8,128)(2,1)} %param.28) | copy-start | bytes 225796
  86.3 44.3 %copy-start.137 = (bf16[768]{0:T(1024)(128)(2,1)S(1)}, bf16[768]{0:T(1024)(128)(2,1)}, u32[]{:S(2)}) copy-start(bf16[768]{0:T(1024)(128)(2,1)} %param.27) | copy-start | bytes 4612
  86.3 44.9 %copy-start.141 = (u32[32]{0:T(128)S(1)}, u32[32]{0:T(128)}, u32[]{:S(2)}) copy-start(u32[32]{0:T(128)} %constant.294) | copy-start | bytes 388
  86.3 46.1 %copy-start.33 = (bf16[768,384]{1,0:T(8,128)(2,1)S(1)}, bf16[768,384]{1,0:T(8,128)(2,1)}, u32[]{:S(2)}) copy-start(bf16[768,384]{1,0:T(8,128)(2,1)} %param.29) | copy-start | bytes 1769476
  129.9 258.3 %reduce-scatter.11.cloned.1.call-start = ((), (), s32[]{:S(2)}) async-start(), calls=%async_computation.8 | async-start | bytes 1843200 | tf_op jit(solution)/shard_map/reduce_scatter | solution.py:143
  139.2 21.3 %copy-start.2 = (f32[8,196,768]{2,0,1:T(8,128)}, f32[8,196,768]{2,0,1:T(8,128)S(1)}, u32[]{:S(2)}) copy-start(f32[8,196,768]{2,0,1:T(8,128)S(1)} %copy.109) | copy-start | bytes 14450692
  189.1 101.1 %slice-start.10 = ((s8[4816896]{0:T(1024)(128)(4,1)}), s8[622592]{0:T(1024)(128)(4,1)S(1)}, s32[]{:S(2)}) async-start(s8[4816896]{0:T(1024)(128)(4,1)} %bitcast.183), calls=%async_computation.23 | async-start | bytes 1245184
  217.7 72.5 %slice-start.11 = ((s8[4816896]{0:T(1024)(128)(4,1)}), s8[4194304]{0:T(1024)(128)(4,1)S(1)}, s32[]{:S(2)}) async-start(s8[4816896]{0:T(1024)(128)(4,1)} %bitcast.183), calls=%async_computation.24 | async-start | bytes 8388608
  322.7 232.8 %reduce-scatter.15.cloned.1.call-start = ((), (), s32[]{:S(2)}) async-start(), calls=%async_computation.10 | async-start | bytes 442368 | tf_op jit(solution)/shard_map/reduce_scatter | solution.py:208
  328.2 47.2 %slice-start.4 = ((s8[4816896]{0:T(1024)(128)(4,1)}), s8[4194304]{0:T(1024)(128)(4,1)S(1)}, s32[]{:S(2)}) async-start(s8[4816896]{0:T(1024)(128)(4,1)} %bitcast.172), calls=%async_computation.17 | async-start | bytes 8388608
  330.8 44.6 %slice-start.5 = ((s8[4816896]{0:T(1024)(128)(4,1)}), s8[622592]{0:T(1024)(128)(4,1)S(1)}, s32[]{:S(2)}) async-start(s8[4816896]{0:T(1024)(128)(4,1)} %bitcast.172), calls=%async_computation.18 | async-start | bytes 1245184
  332.4 43.0 %copy-start.3 = (f32[8,196,768]{2,0,1:T(8,128)}, f32[8,196,768]{2,0,1:T(8,128)S(1)}, u32[]{:S(2)}) copy-start(f32[8,196,768]{2,0,1:T(8,128)S(1)} %copy.105) | copy-start | bytes 14450692
  396.7 160.7 %reduce-scatter.9.cloned.1.call-start = ((), (), s32[]{:S(2)}) async-start(), calls=%async_computation.6 | async-start | bytes 1843200 | tf_op jit(solution)/shard_map/reduce_scatter | solution.py:118
  396.8 33.4 %copy-start.20 = (bf16[8,14,14,768]{3,0,2,1:T(8,128)(2,1)S(1)}, bf16[8,14,14,768]{3,0,2,1:T(8,128)(2,1)}, u32[]{:S(2)}) copy-start(bf16[8,14,14,768]{3,0,2,1:T(8,128)(2,1)} %add_convert_fusion.1) | copy-start | bytes 7225348
  429.2 20.0 %copy-start.34 = (bf16[768,384]{1,0:T(8,128)(2,1)S(1)}, bf16[768,384]{1,0:T(8,128)(2,1)}, u32[]{:S(2)}) copy-start(bf16[768,384]{1,0:T(8,128)(2,1)} %param.29) | copy-start | bytes 1769476
  430.7 21.6 %copy-start.27 = (bf16[384,384]{0,1:T(8,128)(2,1)S(1)}, bf16[384,384]{0,1:T(8,128)(2,1)}, u32[]{:S(2)}) copy-start(bf16[384,384]{0,1:T(8,128)(2,1)} %copy-done.26) | copy-start | bytes 884740
  451.7 148.6 %reduce-scatter.13.cloned.1.call-start = ((), (), s32[]{:S(2)}) async-start(), calls=%async_computation.9 | async-start | bytes 1327104 | tf_op jit(solution)/shard_map/reduce_scatter | solution.py:205
  486.4 20.8 %copy-start.95 = (f32[1,768]{1,0:T(1,128)S(1)}, f32[1,768]{1,0:T(1,128)}, u32[]{:S(2)}) copy-start(f32[1,768]{1,0:T(1,128)} %broadcast_in_dim.225) | copy-start | bytes 9220
  486.4 20.7 %copy-start.96 = (f32[1,768]{1,0:T(1,128)S(1)}, f32[1,768]{1,0:T(1,128)}, u32[]{:S(2)}) copy-start(f32[1,768]{1,0:T(1,128)} %broadcast_in_dim.224) | copy-start | bytes 9220
  486.4 20.7 %copy-start.97 = (f32[1,768]{1,0:T(1,128)S(1)}, f32[1,768]{1,0:T(1,128)}, u32[]{:S(2)}) copy-start(f32[1,768]{1,0:T(1,128)} %broadcast_in_dim.223) | copy-start | bytes 9220
  486.4 20.7 %copy-start.98 = (f32[1,768]{1,0:T(1,128)S(1)}, f32[1,768]{1,0:T(1,128)}, u32[]{:S(2)}) copy-start(f32[1,768]{1,0:T(1,128)} %broadcast_in_dim.222) | copy-start | bytes 9220
  486.4 20.7 %copy-start.99 = (f32[1,768]{1,0:T(1,128)S(1)}, f32[1,768]{1,0:T(1,128)}, u32[]{:S(2)}) copy-start(f32[1,768]{1,0:T(1,128)} %broadcast_in_dim.221) | copy-start | bytes 9220
  486.4 20.7 %copy-start.100 = (f32[1,768]{1,0:T(1,128)S(1)}, f32[1,768]{1,0:T(1,128)}, u32[]{:S(2)}) copy-start(f32[1,768]{1,0:T(1,128)} %broadcast_in_dim.220) | copy-start | bytes 9220
  486.5 20.7 %copy-start.101 = (f32[1,768]{1,0:T(1,128)S(1)}, f32[1,768]{1,0:T(1,128)}, u32[]{:S(2)}) copy-start(f32[1,768]{1,0:T(1,128)} %broadcast_in_dim.219) | copy-start | bytes 9220
  486.5 20.7 %copy-start.102 = (f32[1,768]{1,0:T(1,128)S(1)}, f32[1,768]{1,0:T(1,128)}, u32[]{:S(2)}) copy-start(f32[1,768]{1,0:T(1,128)} %broadcast_in_dim.218) | copy-start | bytes 9220
  486.5 20.7 %copy-start.103 = (f32[1,768]{1,0:T(1,128)S(1)}, f32[1,768]{1,0:T(1,128)}, u32[]{:S(2)}) copy-start(f32[1,768]{1,0:T(1,128)} %broadcast_in_dim.217) | copy-start | bytes 9220
  486.5 20.7 %copy-start.104 = (f32[1,768]{1,0:T(1,128)S(1)}, f32[1,768]{1,0:T(1,128)}, u32[]{:S(2)}) copy-start(f32[1,768]{1,0:T(1,128)} %broadcast_in_dim.216) | copy-start | bytes 9220
  486.5 20.7 %copy-start.105 = (f32[1,768]{1,0:T(1,128)S(1)}, f32[1,768]{1,0:T(1,128)}, u32[]{:S(2)}) copy-start(f32[1,768]{1,0:T(1,128)} %broadcast_in_dim.215) | copy-start | bytes 9220
  486.5 20.7 %copy-start.106 = (f32[1,768]{1,0:T(1,128)S(1)}, f32[1,768]{1,0:T(1,128)}, u32[]{:S(2)}) copy-start(f32[1,768]{1,0:T(1,128)} %broadcast_in_dim.214) | copy-start | bytes 9220
  486.5 20.7 %copy-start.107 = (f32[1,768]{1,0:T(1,128)S(1)}, f32[1,768]{1,0:T(1,128)}, u32[]{:S(2)}) copy-start(f32[1,768]{1,0:T(1,128)} %broadcast_in_dim.213) | copy-start | bytes 9220
  486.5 20.7 %copy-start.108 = (f32[1,768]{1,0:T(1,128)S(1)}, f32[1,768]{1,0:T(1,128)}, u32[]{:S(2)}) copy-start(f32[1,768]{1,0:T(1,128)} %broadcast_in_dim.212) | copy-start | bytes 9220
  486.5 20.7 %copy-start.109 = (f32[1,768]{1,0:T(1,128)S(1)}, f32[1,768]{1,0:T(1,128)}, u32[]{:S(2)}) copy-start(f32[1,768]{1,0:T(1,128)} %broadcast_in_dim.207) | copy-start | bytes 9220
  486.5 20.7 %copy-start.110 = (f32[1,768]{1,0:T(1,128)S(1)}, f32[1,768]{1,0:T(1,128)}, u32[]{:S(2)}) copy-start(f32[1,768]{1,0:T(1,128)} %broadcast_in_dim.206) | copy-start | bytes 9220
  486.6 20.7 %copy-start.111 = (f32[1,768]{1,0:T(1,128)S(1)}, f32[1,768]{1,0:T(1,128)}, u32[]{:S(2)}) copy-start(f32[1,768]{1,0:T(1,128)} %broadcast_in_dim.205) | copy-start | bytes 9220
  486.6 20.7 %copy-start.112 = (f32[1,768]{1,0:T(1,128)S(1)}, f32[1,768]{1,0:T(1,128)}, u32[]{:S(2)}) copy-start(f32[1,768]{1,0:T(1,128)} %broadcast_in_dim.204) | copy-start | bytes 9220
  486.6 20.7 %copy-start.113 = (f32[1,768]{1,0:T(1,128)S(1)}, f32[1,768]{1,0:T(1,128)}, u32[]{:S(2)}) copy-start(f32[1,768]{1,0:T(1,128)} %broadcast_in_dim.203) | copy-start | bytes 9220
  486.6 20.7 %copy-start.114 = (f32[1,768]{1,0:T(1,128)S(1)}, f32[1,768]{1,0:T(1,128)}, u32[]{:S(2)}) copy-start(f32[1,768]{1,0:T(1,128)} %broadcast_in_dim.202) | copy-start | bytes 9220
  486.6 20.7 %copy-start.115 = (f32[1,768]{1,0:T(1,128)S(1)}, f32[1,768]{1,0:T(1,128)}, u32[]{:S(2)}) copy-start(f32[1,768]{1,0:T(1,128)} %broadcast_in_dim.201) | copy-start | bytes 9220
  486.6 20.7 %copy-start.116 = (f32[1,768]{1,0:T(1,128)S(1)}, f32[1,768]{1,0:T(1,128)}, u32[]{:S(2)}) copy-start(f32[1,768]{1,0:T(1,128)} %broadcast_in_dim.200) | copy-start | bytes 9220
  486.6 20.7 %copy-start.117 = (f32[1,768]{1,0:T(1,128)S(1)}, f32[1,768]{1,0:T(1,128)}, u32[]{:S(2)}) copy-start(f32[1,768]{1,0:T(1,128)} %broadcast_in_dim.199) | copy-start | bytes 9220
  486.6 20.7 %copy-start.118 = (f32[1,768]{1,0:T(1,128)S(1)}, f32[1,768]{1,0:T(1,128)}, u32[]{:S(2)}) copy-start(f32[1,768]{1,0:T(1,128)} %broadcast_in_dim.198) | copy-start | bytes 9220
  486.6 20.7 %copy-start.119 = (f32[1,768]{1,0:T(1,128)S(1)}, f32[1,768]{1,0:T(1,128)}, u32[]{:S(2)}) copy-start(f32[1,768]{1,0:T(1,128)} %broadcast_in_dim.197) | copy-start | bytes 9220
  486.6 20.7 %copy-start.120 = (f32[1,768]{1,0:T(1,128)S(1)}, f32[1,768]{1,0:T(1,128)}, u32[]{:S(2)}) copy-start(f32[1,768]{1,0:T(1,128)} %broadcast_in_dim.196) | copy-start | bytes 9220
  486.7 20.7 %copy-start.121 = (f32[1,768]{1,0:T(1,128)S(1)}, f32[1,768]{1,0:T(1,128)}, u32[]{:S(2)}) copy-start(f32[1,768]{1,0:T(1,128)} %broadcast_in_dim.195) | copy-start | bytes 9220
  486.7 20.7 %copy-start.122 = (f32[1,768]{1,0:T(1,128)S(1)}, f32[1,768]{1,0:T(1,128)}, u32[]{:S(2)}) copy-start(f32[1,768]{1,0:T(1,128)} %broadcast_in_dim.194) | copy-start | bytes 9220
  486.7 20.7 %copy-start.123 = (f32[1,768]{1,0:T(1,128)S(1)}, f32[1,768]{1,0:T(1,128)}, u32[]{:S(2)}) copy-start(f32[1,768]{1,0:T(1,128)} %broadcast_in_dim.193) | copy-start | bytes 9220
  486.7 20.7 %copy-start.124 = (f32[1,768]{1,0:T(1,128)S(1)}, f32[1,768]{1,0:T(1,128)}, u32[]{:S(2)}) copy-start(f32[1,768]{1,0:T(1,128)} %broadcast_in_dim.192) | copy-start | bytes 9220
  486.7 20.7 %copy-start.125 = (f32[1,768]{1,0:T(1,128)S(1)}, f32[1,768]{1,0:T(1,128)}, u32[]{:S(2)}) copy-start(f32[1,768]{1,0:T(1,128)} %broadcast_in_dim.191) | copy-start | bytes 9220
  486.7 208.8 %all-reduce.107.cloned.1.call-start = ((), (), s32[]{:S(2)}) async-start(), calls=%async_computation.12 | async-start | bytes 5062656 | tf_op jit(solution)/shard_map/psum | solution.py:151
  486.8 21.7 %copy-start.29 = (bf16[8,196,768]{2,1,0:T(8,128)(2,1)S(1)}, bf16[8,196,768]{2,1,0:T(8,128)(2,1)}, u32[]{:S(2)}) copy-start(bf16[8,196,768]{2,1,0:T(8,128)(2,1)} %copy-done.28) | copy-start | bytes 7225348
  486.8 21.7 %copy-start.31 = (bf16[8,197,384]{2,1,0:T(8,128)(2,1)S(1)}, bf16[8,197,384]{2,1,0:T(8,128)(2,1)}, u32[]{:S(2)}) copy-start(bf16[8,197,384]{2,1,0:T(8,128)(2,1)} %all-gather.5.cloned.1.call-done) | copy-start | bytes 3631108
  513.5 267.8 %reduce-scatter.17.cloned.1.call-start = ((), (), s32[]{:S(2)}) async-start(), calls=%async_computation.11 | async-start | bytes 417792
  513.7 24.0 %slice-start.2 = ((s8[6455296]{0:T(1024)(128)(4,1)}), s8[4194304]{0:T(1024)(128)(4,1)S(1)}, s32[]{:S(2)}) async-start(s8[6455296]{0:T(1024)(128)(4,1)} %bitcast.165), calls=%async_computation.15 | async-start | bytes 8388608
  513.7 24.0 %slice-start.6 = ((s8[4915200]{0:T(1024)(128)(4,1)}), s8[4194304]{0:T(1024)(128)(4,1)S(1)}, s32[]{:S(2)}) async-start(s8[4915200]{0:T(1024)(128)(4,1)} %bitcast.179), calls=%async_computation.19 | async-start | bytes 8388608
  557.4 42.9 %copy-start.134 = (f32[768]{0:T(1024)S(1)}, f32[768]{0:T(1024)}, u32[]{:S(2)}) copy-start(f32[768]{0:T(1024)} %get-tuple-element.182) | copy-start | bytes 9220
  (101 other events, 691.0 us)
Sparse Core Ops, SparseCore 0:
  10.2 11.9 all-gather.4
  130.1 7.0 all-gather.2
  322.8 6.5 reduce-scatter.10
  396.8 5.5 reduce-scatter.14
  451.8 6.5 reduce-scatter.8
  486.5 6.2 reduce-scatter.12
  513.6 138.8 all-reduce.106
  658.4 122.8 reduce-scatter.16
where the time goes:
time: 798 us; the launch traced here: 795 us
  other arithmetic  290 us (36%)
  blocking collectives  219 us (27%)
  matrix products  124 us (16%)
  waiting for transfers between devices  85.9 us (11%)
  local copies, waits for them, and re-layouts  58.2 us (7%)
  between operations  17.4 us (2%)
    unnamed x1, blocking collectives  94.3 us
    unnamed x9, waiting for transfers between devices  85.9 us
    add_any x2, other arithmetic, depthwise(): padded[:, tap_row:tap_row + GRID, tap_col:tap_col + GRID]  79.4 us
    mul x3, other arithmetic, depthwise(): kernel[tap_row * KS + tap_col]  78.1 us
    reduce_sum x4, other arithmetic, depthwise(): kernel[tap_row * KS + tap_col]  66.8 us
    all_gather x1, blocking collectives, shards(): lax.all_gather(qkv_weight, 'dp', axis=0, tiled=True)  45.3 us
    another operation x1, other arithmetic  42.9 us
    psum x1, blocking collectives, shards(): lax.psum((grad_norm1_gain, grad_norm1_bias, grad_mix_pre, grad_mix_post,...  37.8 us
  transfers between devices with their start and end apart: 8, of which 1 were waited for; matrix products, arithmetic and copies ran while one was open for 53% of the time, Pallas kernels for 0%

commit v1 on v0

v1 whole, which is shorter than its diff:
```python
import functools

import jax
import jax.numpy as jnp
import numpy as np
from jax import lax
from jax.experimental import pallas as pl
from jax.experimental.pallas import tpu as pltpu
from jax.sharding import PartitionSpec as P

HEADS = 6
HEAD_DIM = 64
KS = 7
GRID = 14
POINTS = 17
SEQ = 197
ROWS = 208
KEYS = 256
WIDTH = 384
HALF = 152
COEFS = 2 * HALF
CLASS_ROW = 145
CHUNK = 256
VMEM = 60 * 1024 * 1024

f32 = jnp.float32
bf16 = jnp.bfloat16


def fourier():
    pairs = [(0, 0)]
    for k in range(POINTS):
        for m in range(POINTS):
            other = ((-k) % POINTS, (-m) % POINTS)
            if (k, m) != (0, 0) and (k, m) < other:
                pairs.append((k, m))
    freq = np.array(pairs, np.float64)
    unit = 2.0 * np.pi / POINTS
    spots = np.array([(y, x) for y in range(GRID) for x in range(GRID)], np.float64)
    taps = np.array([(a - 3, c - 3) for a in range(KS) for c in range(KS)], np.float64)
    count = len(pairs)
    angle = unit * freq @ spots.T
    forward = np.zeros((COEFS, ROWS))
    forward[:count, 1:SEQ] = np.cos(angle)
    forward[HALF : HALF + count, 1:SEQ] = -np.sin(angle)
    forward[CLASS_ROW, 0] = 1.0
    weight = np.full((count, 1), 2.0)
    weight[0] = 1.0
    weight = weight / POINTS**2
    inverse = np.zeros((COEFS, ROWS))
    inverse[:count, 1:SEQ] = weight * np.cos(angle)
    inverse[HALF : HALF + count, 1:SEQ] = -weight * np.sin(angle)
    inverse[CLASS_ROW, 0] = 1.0
    turn = unit * freq @ taps.T
    kernel = np.zeros((COEFS, KS * KS))
    kernel[:count] = np.cos(turn)
    kernel[HALF : HALF + count] = np.sin(turn)
    back = np.zeros((COEFS, KS * KS))
    back[:count] = weight * np.cos(turn)
    back[HALF : HALF + count] = -weight * np.sin(turn)
    one = np.zeros((COEFS, 1))
    one[CLASS_ROW] = 1.0
    return forward, inverse.T, kernel, back.T, one


def split(matrix):
    high = np.asarray(matrix, np.float32).astype(bf16)
    low = (np.asarray(matrix, np.float32) - high.astype(np.float32)).astype(bf16)
    return high, low


def dot(a, b):
    return lax.dot_general(a, b, (((1,), (0,)), ((), ())), preferred_element_type=f32)


def dot_t(a, b):
    return lax.dot_general(a, b, (((1,), (1,)), ((), ())), preferred_element_type=f32)


def t_dot(a, b):
    return lax.dot_general(a, b, (((0,), (0,)), ((), ())), preferred_element_type=f32)


def centre(values):
    centred = values - jnp.mean(values, axis=-1, keepdims=True)
    spread = jnp.mean(centred * centred, axis=-1, keepdims=True)
    return centred, lax.rsqrt(spread + 1e-05)


def norm_back(centred, r, gain, grad):
    scaled = grad * gain
    moment = jnp.mean(scaled * centred, axis=-1, keepdims=True)
    back = r * (scaled - jnp.mean(scaled, axis=-1, keepdims=True) - centred * (r * r * moment))
    return back, grad * (centred * r)


def add_rows(values):
    return jnp.sum(values, axis=0, keepdims=True)


def row_mask(shape):
    return lax.broadcasted_iota(jnp.int32, shape, 0) < SEQ


def attention_forward(
    pre, post, tok, wqkv, wproj, gain1, bias1, pbias, gain2, bias2,
    n1_out, packed_out, probs_out, attn_out, att_out, mid_out, n2_out, pad, score, keys,
):
    pad[SEQ - 5 :] = jnp.zeros((ROWS - SEQ + 5, WIDTH), f32)
    pad[:SEQ] = tok[0].astype(f32)
    inputs = pad[...]
    centred, r = centre(inputs)
    inside = row_mask((ROWS, WIDTH))
    n1 = jnp.where(inside, centred * r * gain1[...] + bias1[...], 0.0).astype(bf16)
    n1_out[0] = n1
    packed = dot(n1, wqkv[...]).astype(bf16)
    packed_out[0, :ROWS] = packed
    packed_out[0, ROWS:] = jnp.zeros((KEYS - ROWS, 3 * WIDTH), bf16)
    low_half = lax.broadcasted_iota(jnp.int32, (ROWS, 128), 1) < HEAD_DIM
    zero = jnp.zeros((ROWS, 128), bf16)
    for p in range(HEADS // 2):
        query = packed_out[0, :ROWS, 128 * p : 128 * p + 128]
        key = packed_out[0, :, WIDTH + 128 * p : WIDTH + 128 * p + 128]
        score[2 * p] = dot_t(jnp.where(low_half, query, zero), key)
        score[2 * p + 1] = dot_t(jnp.where(low_half, zero, query), key)
    valid = lax.broadcasted_iota(jnp.int32, (16, KEYS), 1) < SEQ

    def rows_step(step, carry):
        rows = pl.ds(pl.multiple_of(step * 16, 16), 16)
        scores = [score[h, rows, :] for h in range(HEADS)]
        probs = []
        for g in range(HEADS):
            mixed = scores[0] * (pre[g, 0] * 0.125)
            for h in range(1, HEADS):
                mixed = mixed + scores[h] * (pre[g, h] * 0.125)
            mixed = jnp.where(valid, mixed, -1e30)
            top = jnp.max(mixed, axis=-1, keepdims=True)
            raised = jnp.exp(mixed - top)
            prob = raised * (1.0 / jnp.sum(raised, axis=-1, keepdims=True))
            probs_out[0, g, rows, :] = prob
            probs.append(prob)
        for g in range(HEADS):
            mixed = probs[0] * post[g, 0]
            for h in range(1, HEADS):
                mixed = mixed + probs[h] * post[g, h]
            attn_out[0, g, rows, :] = mixed.astype(bf16)
        return carry

    lax.fori_loop(0, ROWS // 16, rows_step, 0)
    pieces = []
    for p in range(HEADS // 2):
        value = packed_out[0, :, 2 * WIDTH + 128 * p : 2 * WIDTH + 128 * p + 128]
        pieces.append(
            jnp.where(low_half, dot(attn_out[0, 2 * p], value), dot(attn_out[0, 2 * p + 1], value))
        )
    attended = jnp.concatenate(pieces, axis=1).astype(bf16)
    att_out[0] = attended
    middle = inputs + (dot(attended, wproj[...]) + pbias[...])
    mid_out[0] = middle
    centred, r = centre(middle)
    n2_out[0] = jnp.where(inside, centred * r * gain2[...] + bias2[...], 0.0).astype(bf16)


def gelu_parts(hidden):
    size = jnp.abs(hidden) * np.float32(np.sqrt(0.5))
    t = 1.0 / (1.0 + 0.3275911 * size)
    raised = jnp.exp(-(size * size))
    series = t * (
        0.254829592
        + t * (-0.284496736 + t * (1.421413741 + t * (-1.453152027 + t * 1.061405429)))
    )
    tail = 0.5 * series * raised
    cdf = jnp.where(hidden < 0.0, tail, 1.0 - tail)
    return hidden * cdf, cdf + hidden * (raised * np.float32(1.0 / np.sqrt(2.0 * np.pi)))


def mlp(
    n2, cot, mid, fc1, fc1b, conv, fc2, fc2b, fwd, inv, kh, kl, bh, bl, one,
    block_out, gn2_out, gfc1_out, gb1_out, gconv_out, gfc2_out, gb2_out,
    cot_pad, pad, hid, grad, out_acc, conv_low, ghid_low,
):
    step = pl.program_id(0)
    images = n2.shape[0]

    @pl.when(step == 0)
    def _():
        total = jnp.zeros((1, WIDTH), f32)
        for b in range(images):
            pad[SEQ - 5 :] = jnp.zeros((ROWS - SEQ + 5, WIDTH), f32)
            pad[:SEQ] = cot[b].astype(f32)
            values = pad[...]
            total = total + add_rows(values)
            cot_pad[b * ROWS : (b + 1) * ROWS] = values.astype(bf16)
        gb2_out[...] = total

    w1 = fc1[...]
    w2 = fc2[...]
    taps = conv[...]
    turned = dot(kh[...], taps) + dot(kl[...], taps) + one[...]
    kr, ki = turned[:HALF], turned[HALF:]
    rows_all = n2[...].reshape(images * ROWS, WIDTH)
    hid[...] = dot(rows_all, w1) + fc1b[...].astype(f32)
    grad[...] = dot_t(cot_pad[...], w2)
    cross_r = jnp.zeros((HALF, CHUNK), f32)
    cross_i = jnp.zeros((HALF, CHUNK), f32)
    bias_sum = jnp.zeros((1, CHUNK), f32)
    for b in range(images):
        span = slice(b * ROWS, (b + 1) * ROWS)
        act, slope = gelu_parts(hid[span, :])
        x = dot(fwd[...], act.astype(bf16))
        y = dot(fwd[...], grad[span, :].astype(bf16))
        xr, xi = x[:HALF], x[HALF:]
        yr, yi = y[:HALF], y[HALF:]
        made = jnp.concatenate([xr * kr - xi * ki, xr * ki + xi * kr], axis=0).astype(bf16)
        back = jnp.concatenate([yr * kr + yi * ki, yi * kr - yr * ki], axis=0).astype(bf16)
        cross_r = cross_r + (xr * yr + xi * yi)
        cross_i = cross_i + (xi * yr - xr * yi)
        conv_low[span, :] = dot(inv[...], made).astype(bf16)
        ghid = (dot(inv[...], back) * slope).astype(bf16)
        bias_sum = bias_sum + add_rows(ghid.astype(f32))
        ghid_low[span, :] = ghid
    gb1_out[...] = bias_sum
    cross = jnp.concatenate([cross_r, cross_i], axis=0)
    high = cross.astype(bf16)
    low = (cross - high.astype(f32)).astype(bf16)
    gconv_out[...] = dot(bh[...], high) + dot(bl[...], high) + dot(bh[...], low)
    convolved = conv_low[...]
    ghid_all = ghid_low[...]
    part = dot(convolved, w2).reshape(images, ROWS, WIDTH)
    part_grad = dot_t(ghid_all, w1).reshape(images, ROWS, WIDTH)
    gfc2_out[...] = t_dot(convolved, cot_pad[...])
    gfc1_out[...] = t_dot(rows_all, ghid_all)

    @pl.when(step == 0)
    def _():
        out_acc[...] = part
        gn2_out[...] = part_grad

    @pl.when(step > 0)
    def _():
        out_acc[...] += part
        gn2_out[...] += part_grad

    @pl.when(step == pl.num_programs(0) - 1)
    def _():
        for b in range(images):
            result = mid[b] + (out_acc[b] + fc2b[...])
            block_out[b] = result[:SEQ].astype(bf16)


def attention_backward(
    pre, post, tok, cot, n1, packed, probs, attn, att, mid, gn2, wqkv, wproj, gain1, gain2,
    gtok_out, gqkv_out, gproj_out, rows_out, mix_out,
    pad, score, weight, low, mix,
):
    step = pl.program_id(0)

    @pl.when(step == 0)
    def _():
        gqkv_out[...] = jnp.zeros_like(gqkv_out)
        gproj_out[...] = jnp.zeros_like(gproj_out)
        rows_out[...] = jnp.zeros_like(rows_out)
        mix[...] = jnp.zeros_like(mix)

    pad[SEQ - 5 :] = jnp.zeros((ROWS - SEQ + 5, WIDTH), f32)
    pad[:SEQ] = cot[0].astype(f32)
    centred, r = centre(mid[0])
    grad = gn2[0]
    back, gain_rows = norm_back(centred, r, gain2[...], grad)
    rows_out[3:4] += add_rows(gain_rows)
    rows_out[4:5] += add_rows(grad)
    gmid = pad[...] + back
    gmid_low = gmid.astype(bf16)
    rows_out[2:3] += add_rows(gmid_low.astype(f32))
    gproj_out[...] += t_dot(att[0], gmid_low)
    gatt = dot_t(gmid_low, wproj[...]).astype(bf16)
    low_half = lax.broadcasted_iota(jnp.int32, (ROWS, 128), 1) < HEAD_DIM
    key_half = lax.broadcasted_iota(jnp.int32, (KEYS, 128), 1) < HEAD_DIM
    zero = jnp.zeros((ROWS, 128), bf16)
    for p in range(HEADS // 2):
        query = packed[0, :ROWS, 128 * p : 128 * p + 128]
        key = packed[0, :, WIDTH + 128 * p : WIDTH + 128 * p + 128]
        value = packed[0, :, 2 * WIDTH + 128 * p : 2 * WIDTH + 128 * p + 128]
        ahead = gatt[:, 128 * p : 128 * p + 128]
        score[2 * p] = dot_t(jnp.where(low_half, query, zero), key)
        score[2 * p + 1] = dot_t(jnp.where(low_half, zero, query), key)
        weight[2 * p] = dot_t(jnp.where(low_half, ahead, zero), value)
        weight[2 * p + 1] = dot_t(jnp.where(low_half, zero, ahead), value)

    def fold(values):
        values = values[:, :128] + values[:, 128:]
        return values[:8] + values[8:]

    def rows_step(index, carry):
        rows = pl.ds(pl.multiple_of(index * 16, 16), 16)
        weights = [weight[g, rows, :] for g in range(HEADS)]
        mixed = []
        for h in range(HEADS):
            prob = probs[0, h, rows, :]
            ahead = weights[0] * post[0, h]
            for g in range(1, HEADS):
                ahead = ahead + weights[g] * post[g, h]
            for g in range(HEADS):
                mix[HEADS * HEADS + g * HEADS + h] += fold(weights[g] * prob)
            inner = jnp.sum(prob * ahead, axis=-1, keepdims=True)
            mixed.append(prob * (ahead - inner))
        for h in range(HEADS):
            scores = score[h, rows, :]
            total = mixed[0] * pre[0, h]
            for g in range(1, HEADS):
                total = total + mixed[g] * pre[g, h]
            low[h, rows, :] = total.astype(bf16)
            for g in range(HEADS):
                mix[g * HEADS + h] += fold(mixed[g] * scores)
        return carry

    lax.fori_loop(0, ROWS // 16, rows_step, 0)
    queries, keys, values = [], [], []
    for p in range(HEADS // 2):
        query = packed[0, :ROWS, 128 * p : 128 * p + 128]
        key = packed[0, :, WIDTH + 128 * p : WIDTH + 128 * p + 128]
        ahead = gatt[:, 128 * p : 128 * p + 128]
        even, odd = low[2 * p], low[2 * p + 1]
        queries.append(jnp.where(low_half, dot(even, key), dot(odd, key)) * 0.125)
        keys.append(jnp.where(key_half, t_dot(even, query), t_dot(odd, query))[:ROWS] * 0.125)
        values.append(
            jnp.where(key_half, t_dot(attn[0, 2 * p], ahead), t_dot(attn[0, 2 * p + 1], ahead))[
                :ROWS
            ]
        )
    gpacked = jnp.concatenate(queries + keys + values, axis=1).astype(bf16)
    gqkv_out[...] += t_dot(n1[0], gpacked)
    gnormed = dot_t(gpacked, wqkv[...])
    pad[:SEQ] = tok[0].astype(f32)
    centred, r = centre(pad[...])
    back, gain_rows = norm_back(centred, r, gain1[...], gnormed)
    rows_out[0:1] += add_rows(gain_rows)
    rows_out[1:2] += add_rows(gnormed)
    gtok_out[0] = (gmid + back)[:SEQ]

    @pl.when(step == pl.num_programs(0) - 1)
    def _():
        mix_out[...] = jnp.sum(mix[...], axis=1)


def whole(shape):
    return pl.BlockSpec(shape, lambda *_: (0,) * len(shape))


def image(shape):
    return pl.BlockSpec((1,) + shape, lambda i: (i,) + (0,) * len(shape))


def params():
    return pltpu.CompilerParams(vmem_limit_bytes=VMEM, dimension_semantics=("arbitrary",))


def call_forward(tokens, wqkv, wproj, pre, post, gain1, bias1, pbias, gain2, bias2):
    images = tokens.shape[0]
    smem = pl.BlockSpec(memory_space=pltpu.SMEM)
    row = whole((1, WIDTH))
    return pl.pallas_call(
        attention_forward,
        grid=(images,),
        in_specs=[
            smem, smem, image((SEQ, WIDTH)), whole((WIDTH, 3 * WIDTH)), whole((WIDTH, WIDTH)),
            row, row, row, row, row,
        ],
        out_specs=[
            image((ROWS, WIDTH)), image((KEYS, 3 * WIDTH)), image((HEADS, ROWS, KEYS)),
            image((HEADS, ROWS, KEYS)), image((ROWS, WIDTH)), image((ROWS, WIDTH)),
            image((ROWS, WIDTH)),
        ],
        out_shape=[
            jax.ShapeDtypeStruct((images, ROWS, WIDTH), bf16),
            jax.ShapeDtypeStruct((images, KEYS, 3 * WIDTH), bf16),
            jax.ShapeDtypeStruct((images, HEADS, ROWS, KEYS), f32),
            jax.ShapeDtypeStruct((images, HEADS, ROWS, KEYS), bf16),
            jax.ShapeDtypeStruct((images, ROWS, WIDTH), bf16),
            jax.ShapeDtypeStruct((images, ROWS, WIDTH), f32),
            jax.ShapeDtypeStruct((images, ROWS, WIDTH), bf16),
        ],
        scratch_shapes=[
            pltpu.VMEM((ROWS, WIDTH), f32),
            pltpu.VMEM((HEADS, ROWS, KEYS), f32),
            pltpu.VMEM((8, 128), f32),
        ],
        compiler_params=params(),
        name="attention_forward",
    )(pre, post, tokens, wqkv, wproj, gain1, bias1, pbias, gain2, bias2)


def call_mlp(n2, cotangent, middle, fc1, fc1_bias, conv, fc2, fc2_bias):
    images = n2.shape[0]
    units = fc1.shape[1]
    steps = units // CHUNK
    forward, inverse, kernel, back, one = fourier()
    kernel_high, kernel_low = split(kernel)
    back_high, back_low = split(back)
    consts = [
        jnp.asarray(forward.astype(np.float32).astype(bf16)),
        jnp.asarray(inverse.astype(np.float32).astype(bf16)),
        jnp.asarray(kernel_high), jnp.asarray(kernel_low),
        jnp.asarray(back_high), jnp.asarray(back_low),
        jnp.asarray(one.astype(np.float32)),
    ]
    columns = lambda rows: pl.BlockSpec((rows, CHUNK), lambda i: (0, i))
    taps = KS * KS
    total = images * ROWS
    return pl.pallas_call(
        mlp,
        grid=(steps,),
        in_specs=[
            whole((images, ROWS, WIDTH)), whole((images, SEQ, WIDTH)), whole((images, ROWS, WIDTH)),
            columns(WIDTH), columns(1), columns(taps),
            pl.BlockSpec((CHUNK, WIDTH), lambda i: (i, 0)), whole((1, WIDTH)),
        ]
        + [whole(c.shape) for c in consts],
        out_specs=[
            whole((images, SEQ, WIDTH)), whole((images, ROWS, WIDTH)),
            columns(WIDTH), columns(1), columns(taps),
            pl.BlockSpec((CHUNK, WIDTH), lambda i: (i, 0)), whole((1, WIDTH)),
        ],
        out_shape=[
            jax.ShapeDtypeStruct((images, SEQ, WIDTH), bf16),
            jax.ShapeDtypeStruct((images, ROWS, WIDTH), f32),
            jax.ShapeDtypeStruct((WIDTH, units), f32),
            jax.ShapeDtypeStruct((1, units), f32),
            jax.ShapeDtypeStruct((taps, units), f32),
            jax.ShapeDtypeStruct((units, WIDTH), f32),
            jax.ShapeDtypeStruct((1, WIDTH), f32),
        ],
        scratch_shapes=[
            pltpu.VMEM((total, WIDTH), bf16),
            pltpu.VMEM((ROWS, WIDTH), f32),
            pltpu.VMEM((total, CHUNK), f32),
            pltpu.VMEM((total, CHUNK), f32),
            pltpu.VMEM((images, ROWS, WIDTH), f32),
            pltpu.VMEM((total, CHUNK), bf16),
            pltpu.VMEM((total, CHUNK), bf16),
        ],
        compiler_params=params(),
        name="mlp",
    )(n2, cotangent, middle, fc1, fc1_bias, conv, fc2, fc2_bias, *consts)


def call_backward(
    tokens, cotangent, n1, packed, probs, attn, att, mid, gn2, wqkv, wproj, pre, post, gain1, gain2
):
    images = tokens.shape[0]
    smem = pl.BlockSpec(memory_space=pltpu.SMEM)
    row = whole((1, WIDTH))
    return pl.pallas_call(
        attention_backward,
        grid=(images,),
        in_specs=[
            smem, smem, image((SEQ, WIDTH)), image((SEQ, WIDTH)), image((ROWS, WIDTH)),
            image((KEYS, 3 * WIDTH)), image((HEADS, ROWS, KEYS)), image((HEADS, ROWS, KEYS)),
            image((ROWS, WIDTH)), image((ROWS, WIDTH)), image((ROWS, WIDTH)),
            whole((WIDTH, 3 * WIDTH)), whole((WIDTH, WIDTH)), row, row,
        ],
        out_specs=[
            image((SEQ, WIDTH)), whole((WIDTH, 3 * WIDTH)), whole((WIDTH, WIDTH)),
            whole((8, WIDTH)), whole((2 * HEADS * HEADS, 128)),
        ],
        out_shape=[
            jax.ShapeDtypeStruct((images, SEQ, WIDTH), f32),
            jax.ShapeDtypeStruct((WIDTH, 3 * WIDTH), f32),
            jax.ShapeDtypeStruct((WIDTH, WIDTH), f32),
            jax.ShapeDtypeStruct((8, WIDTH), f32),
            jax.ShapeDtypeStruct((2 * HEADS * HEADS, 128), f32),
        ],
        scratch_shapes=[
            pltpu.VMEM((ROWS, WIDTH), f32),
            pltpu.VMEM((HEADS, ROWS, KEYS), f32),
            pltpu.VMEM((HEADS, ROWS, KEYS), f32),
            pltpu.VMEM((HEADS, ROWS, KEYS), bf16),
            pltpu.VMEM((2 * HEADS * HEADS, 8, 128), f32),
        ],
        compiler_params=params(),
        name="attention_backward",
    )(
        pre, post, tokens, cotangent, n1, packed, probs, attn, att, mid, gn2, wqkv, wproj,
        gain1, gain2,
    )


def local_block(
    tokens, norm1_gain, norm1_bias, wqkv, mix_pre, mix_post, wproj, proj_bias, norm2_gain,
    norm2_bias, fc1, fc1_bias, conv, fc2, fc2_bias, cotangent,
):
    row = lambda v: v.reshape(1, -1)
    gain1, gain2 = row(norm1_gain), row(norm2_gain)
    n1, packed, probs, attn, att, mid, n2 = call_forward(
        tokens, wqkv, wproj, mix_pre, mix_post, gain1, row(norm1_bias), row(proj_bias), gain2,
        row(norm2_bias),
    )
    block_out, gn2, gfc1, gb1, gconv, gfc2, gb2 = call_mlp(
        n2, cotangent, mid, fc1, row(fc1_bias), conv, fc2, row(fc2_bias)
    )
    gtok, gqkv, gproj, rows, mix = call_backward(
        tokens, cotangent, n1, packed, probs, attn, att, mid, gn2, wqkv, wproj, mix_pre, mix_post,
        gain1, gain2,
    )
    return block_out, gtok, gqkv, gproj, gfc1, gb1, gconv, gfc2, gb2, rows, mix


def shards(
    tokens, norm1_gain, norm1_bias, qkv_weight, mix_pre, mix_post, proj_weight, proj_bias,
    norm2_gain, norm2_bias, fc1_weight, fc1_bias, conv_weight, fc2_weight, fc2_bias, cotangent,
):
    gather = lambda v, axis, dim: lax.all_gather(v, axis, axis=dim, tiled=True)
    both = jnp.concatenate([qkv_weight, proj_weight], axis=1)
    rows = gather(both, "dp", 0)
    pair = lax.all_gather(rows, "tensor", axis=0)
    columns = qkv_weight.shape[1]
    wqkv = jnp.concatenate([pair[0, :, :columns], pair[1, :, :columns]], axis=1)
    wproj = jnp.concatenate([pair[0, :, columns:], pair[1, :, columns:]], axis=1)
    fc1 = gather(fc1_weight, "tensor", 1)
    fc1b = gather(fc1_bias, "tensor", 0)
    conv = gather(conv_weight, "tensor", 1)
    fc2 = gather(fc2_weight, "tensor", 0)
    block_out, gtok, gqkv, gproj, gfc1, gb1, gconv, gfc2, gb2, rows, mix = local_block(
        tokens, norm1_gain, norm1_bias, wqkv, mix_pre, mix_post, wproj, proj_bias, norm2_gain,
        norm2_bias, fc1, fc1b, conv, fc2, fc2_bias, cotangent,
    )
    scatter = lambda v, axis, dim: lax.psum_scatter(v, axis, scatter_dimension=dim, tiled=True)
    gqkv = scatter(scatter(gqkv.astype(bf16), "tensor", 1).astype(f32), "dp", 0)
    gproj = scatter(scatter(gproj.astype(bf16), "tensor", 1).astype(f32), "dp", 0)
    gfc1 = lax.psum(scatter(gfc1.astype(bf16), "tensor", 1).astype(f32), "dp")
    gfc2 = lax.psum(scatter(gfc2.astype(bf16), "tensor", 0).astype(f32), "dp")
    gconv = lax.psum(scatter(gconv, "tensor", 1), "dp")
    gb1 = lax.psum(scatter(gb1[0], "tensor", 0), "dp")
    mixes = jnp.sum(mix, axis=1).reshape(2, HEADS, HEADS)
    rows, gb2, mixes = lax.psum((rows, gb2, mixes), ("dp", "tensor"))
    return (
        block_out, gtok, rows[0], rows[1], gqkv, mixes[0] * 0.125, mixes[1], gproj, rows[2],
        rows[3], rows[4], gfc1, gb1, gconv, gfc2, gb2[0],
    )


def solution(mesh):
    spec = P(("dp", "tensor"), None, None)
    in_specs = (
        spec, P(), P(), P("dp", "tensor"), P(), P(), P("dp", "tensor"), P(), P(), P(),
        P(None, "tensor"), P("tensor"), P(None, "tensor"), P("tensor", None), P(), spec,
    )
    out_specs = (
        spec, spec, P(), P(), P("dp", "tensor"), P(), P(), P("dp", "tensor"), P(), P(), P(),
        P(None, "tensor"), P("tensor"), P(None, "tensor"), P("tensor", None), P(),
    )
    return jax.shard_map(shards, mesh=mesh, in_specs=in_specs, out_specs=out_specs, check_vma=False)
```

time: 798 us -> 566 us (0.71)
  other arithmetic: 290 us -> 11 us
  waiting for transfers between devices: 85.9 us -> 241 us
  matrix products: 124 us -> 0 us
  Pallas kernels: 0 us -> 72.9 us
  local copies, waits for them, and re-layouts: 58.2 us -> 16.6 us
  blocking collectives: 219 us -> 209 us
    dot_general x24 -> x0, matrix products: 124 us -> none  [the longest x1 18.7 us: shards(): jnp.einsum('bgqk,bhqk->gh', grad_weights, probabilities, precision=highest)]
    psum x1 -> x2, blocking collectives: 37.8 us -> 154 us  [the longest x1 113 us: shards(): gfc1 = lax.psum(scatter(gfc1.astype(bf16), 'tensor', 1).astype(f32), 'dp')]
    reduce_scatter x4, waiting for transfers between devices: 0.03 us -> 104 us  [shards(): lax.psum_scatter(v, axis, scatter_dimension=dim, tiled=True)]
    unnamed x1, blocking collectives: 94.3 us -> 2.5 us
    mul x4 -> x0, other arithmetic: 82.9 us -> none  [the longest x3 78.1 us: depthwise(): kernel[tap_row * KS + tap_col]]
    add_any x3 -> x0, other arithmetic: 80.5 us -> none  [the longest x2 79.4 us: depthwise(): padded[:, tap_row:tap_row + GRID, tap_col:tap_col + GRID]]
    reduce_sum x12 -> x1, other arithmetic: 78.7 us -> 0.1 us  [shards(): mixes = jnp.sum(mix, axis=1).reshape(2, HEADS, HEADS)]
    pallas_call x0 -> x3, Pallas kernels: none -> 72.9 us  [the longest x1 28 us: call_mlp(): pl.pallas_call(mlp, grid=(steps,), in_specs=[whole((images, ROWS, WIDTH))...]
  transfers between devices with their start and end apart: 8 -> 11, of which waited for: 1 -> 3; matrix products, arithmetic and copies ran while one was open for 53% -> 4% of each run, Pallas kernels for 0% -> 8%
where the time goes in v1:
time: 566 us
  waiting for transfers between devices  241 us (43%)
  blocking collectives  209 us (37%)
  Pallas kernels  72.9 us (13%)
  local copies, waits for them, and re-layouts  16.6 us (3%)
  between operations  14.8 us (3%)
  other arithmetic  11 us (2%)
    unnamed x14, waiting for transfers between devices  137 us
    psum x1, blocking collectives, shards(): gfc1 = lax.psum(scatter(gfc1.astype(bf16), 'tensor', 1).astype(f32), 'dp')  113 us
    reduce_scatter x4, waiting for transfers between devices, shards(): lax.psum_scatter(v, axis, scatter_dimension=dim, tiled=True)  104 us
    all_gather x3, blocking collectives, shards(): gather = lambda v, axis, dim: lax.all_gather(v, axis, axis=dim, tiled=True)  52.2 us
    psum x1, blocking collectives, shards(): rows, gb2, mixes = lax.psum((rows, gb2, mixes), ('dp', 'tensor'))  41.1 us
    pallas_call x1, Pallas kernels, call_mlp(): pl.pallas_call(mlp, grid=(steps,), in_specs=[whole((images, ROWS, WIDTH))...  28 us
    pallas_call x1, Pallas kernels, call_backward(): pl.pallas_call(attention_backward, grid=(images,), in_specs=[smem, smem,...  24.5 us
    pallas_call x1, Pallas kernels, call_forward(): pl.pallas_call(attention_forward, grid=(images,), in_specs=[smem, smem, i...  20.4 us
  transfers between devices with their start and end apart: 11, of which 3 were waited for; matrix products, arithmetic and copies ran while one was open for 4% of the time, Pallas kernels for 8%

profile of v1, /device:TPU:0, one launch (start us, length us, event | category | flops | bytes accessed | tf_op | source)
XLA Modules:
  0.0 565.6 jit_solution(11542950111323582027)
XLA Ops:
  7.2 0.0 all-gather.10.cloned.1.call-start
  7.2 0.9 pad_maximum_fusion.2
  8.1 48.3 %all_gather.21 = bf16[384,768]{1,0:T(8,128)(2,1)} all-gather(bf16[24,768]{1,0:T(8,128)(2,1)S(1)} %pad_maximum_fusion.2), channel_id=1, replica_groups=mesh['dp'=16,'tensor'=2] {'dp'}, dimensions={0}, use_global_device_ids=true | all-gather | bytes 626688 | tf_op jit(solution)/shard_map/all_gather | solution.py:512
  56.4 0.0 all-gather.10.cloned.1.call-update
  56.5 0.0 all-gather.6.cloned.1.call-start
  56.5 0.7 all-gather.6.cloned.1.call-update
  57.2 0.0 all-gather.8.cloned.1.call-start
  57.3 0.7 all-gather.8.cloned.1.call-update
  58.0 0.0 reduce-scatter.18.cloned.1.call-start
  58.1 0.9 copy.51.tok
  59.0 0.6 reshape.58.gain1
  59.6 0.6 reshape.59.bias1
  60.1 0.6 reshape.60.pbias
  60.7 0.6 reshape.61.gain2
  61.3 0.6 reshape.62.bias2
  61.8 0.9 copy.52.cot
  62.8 0.6 reshape.64.fc2b
  63.3 1.9 all-gather.1
  65.2 2.1 all_gather.26.conv
  67.3 1.3 slice_bitcast_fusion.3
  68.6 0.9 pad_maximum_fusion.1.wproj
  69.5 0.1 slice_bitcast_fusion.1
  69.6 1.2 pad_maximum_fusion.wqkv
  70.7 20.4 %attention_forward.1 = (bf16[4,208,384]{2,1,0:T(8,128)(2,1)}, bf16[4,256,1152]{2,1,0:T(8,128)(2,1)}, f32[4,6,208,256]{3,2,1,0:T(8,128)}, bf16[4,6,208,256]{3,2,1...) custom-call(f32[6,6]{1,0:T(8,128)} %pre.3, f32[6,6]{1,0:T(8,128)} %post.3, ...), custom_call_target="tpu_custom_call" | custom-call | tf_op jit(solution)/shard_map/attention_forward/pallas_call | solution.py:362
  91.1 0.0 all-gather.6.cloned.1.call-done.fc1
  91.1 0.0 all-gather.8.cloned.1.call-done.fc2
  91.2 28.0 %mlp.1 = (bf16[4,197,384]{2,1,0:T(8,128)(2,1)}, f32[4,208,384]{2,1,0:T(8,128)}, f32[384,1536]{1,0:T(8,128)}, f32[1,1536]{1,0:T(1,128)}, f32[49,1536]{1,0:T(8,128...) custom-call(bf16[4,208,384]{2,1,0:T(8,128)(2,1)} %get-tuple-element.35.n2, bf16[4,197,384]{2,1,0:T(8,128)(2,1)} %copy.52.cot, ...), custom_call_target="tpu_custom_call" | custom-call | tf_op jit(solution)/shard_map/mlp/pallas_call | solution.py:410
  119.2 0.0 reduce-scatter.18.cloned.1.call-update
  119.2 0.0 reduce-scatter.24.cloned.1.call-start
  119.2 24.5 %attention_backward.1 = (f32[4,197,384]{2,1,0:T(8,128)}, f32[384,1152]{1,0:T(8,128)}, f32[384,384]{1,0:T(8,128)}, f32[8,384]{1,0:T(8,128)}, f32[72,128]{1,0:T(8,128)}) custom-call(f32[6,6]{1,0:T(8,128)} %pre.3, f32[6,6]{1,0:T(8,128)} %post.3, bf16[4,197,384]{2,1,0:T(8,128)(2,1)} %copy.51.tok, bf16[4,197,384]{2,1,0:T(8,128)(2,1)} %copy.52.cot, ...), custom_call_target="tpu_custom_call" | custom-call | tf_op jit(solution)/shard_map/attention_backward/pallas_call | solution.py:453
  143.8 1.2 convert_element_type.26
  145.0 0.9 copy.59
  145.9 0.0 reduce-scatter.22.cloned.1.call-start
  146.0 0.1 convert_element_type.24
  146.1 1.3 copy.57
  147.5 0.0 reduce-scatter.16.cloned.1.call-start
  147.5 3.0 convert_element_type.28
  150.5 0.0 reduce-scatter.20.cloned.1.call-start
  150.6 1.1 convert_element_type.30
  151.7 0.0 all-reduce.7.cloned.1.call-start
  151.8 0.0 reduce-scatter.18.cloned.1.call-done
  151.8 0.7 all-reduce.7.cloned.1.call-update
  152.5 0.0 reduce-scatter.14.cloned.1.call-start
  152.5 0.0 reduce-scatter.24.cloned.1.call-done
  152.5 1.0 copy.60
  153.6 0.8 convert_element_type.27
  154.4 0.2 reduce-scatter.26.cloned.1.call-start
  154.6 7.4 %reduce-scatter.22.cloned.1.call-done = bf16[576,384]{1,0:T(8,128)(2,1)} async-done(((bf16[1152,384]{1,0:T(8,128)(2,1)}), bf16[576,384]{1,0:T(8,128)(2,1)}) %reduce-scatter.22.cloned.1.call-update) | async-done | bytes 442384
  162.0 1.3 copy.58
  163.3 1.0 convert_element_type.25
  164.4 0.6 dynamic-slice.2
  165.6 1.1 copy.55
  166.7 1.3 copy.56
  168.0 0.1 reduce_sum.9
  168.1 0.1 reshape.65
  168.3 2.5 all-reduce.1
  170.8 0.1 dynamic-slice.3
  170.9 41.1 %all-reduce.2 = (f32[8,384]{1,0:T(8,128)S(1)}, f32[2,6,6]{2,1,0:T(8,128)S(1)}, f32[384]{0:T(512)}) all-reduce(f32[8,384]{1,0:T(8,128)S(1)} %copy-done.9, f32[2,6,6]{2,1,0:T(8,128)S(1)} %reshape.65, f32[384]{0:T(512)S(1)} %reduce.6), channel_id=1, replica_groups=mesh['dp'=16,'tensor'=2] {'dp','tensor'}, use_global_device_ids=true, to_apply=%region_0.0 | all-reduce | flops 3528 | bytes 28224 | tf_op jit(solution)/shard_map/psum | solution.py:535
  212.0 0.6 slice_reduce_fusion
  212.6 0.6 slice_bitcast_fusion.4
  213.2 112.7 %all-reduce.8 = (f32[384,768]{1,0:T(8,128)}, f32[768]{0:T(1024)}, f32[768,384]{1,0:T(8,128)}) all-reduce(bf16[384,768]{1,0:T(8,128)(2,1)} %reduce-scatter.16.cloned.1.call-done, f32[768]{0:T(1024)S(1)} %dynamic-slice.3, bf16[768,384]{1,0:T(8,128)(2,1)} %reduce-scatter.20.cloned.1.call-done), channel_id=1, replica_groups=mesh['dp'=16,'tensor'=2] {'dp'}, use_global_device_ids=true, to_apply=%region_8.0 | all-reduce | flops 590592 | bytes 3545088 | tf_op jit(solution)/shard_map/psum | solution.py:530
  325.9 103.7 %reduce-scatter.14.cloned.1.call-done = f32[24,192]{1,0:T(8,128)} async-done(((f32[384,192]{1,0:T(8,128)}), f32[24,192]{1,0:T(8,128)}) %reduce-scatter.14.cloned.1.call-update) | async-done | bytes 18448 | tf_op jit(solution)/shard_map/reduce_scatter | solution.py:527
  429.7 127.8 %reduce-scatter.26.cloned.1.call-done = f32[24,576]{1,0:T(8,128)} async-done(((f32[384,576]{1,0:T(8,128)}), f32[24,576]{1,0:T(8,128)}) %reduce-scatter.26.cloned.1.call-update) | async-done | bytes 55312
  557.4 1.6 copy.67
  (53 shorter events, 0.3 us)
Async XLA Ops:
  7.2 50.9 %copy-start.5 = (bf16[4,197,384]{2,0,1:T(4,128)(2,1)S(1)}, bf16[4,197,384]{2,0,1:T(4,128)(2,1)}, u32[]{:S(2)}) copy-start(bf16[4,197,384]{2,0,1:T(4,128)(2,1)} %param.23) | copy-start | bytes 1815556
  7.2 60.1 %all-gather.10.cloned.1.call-start = ((), (), s32[]{:S(2)}) async-start(), calls=%async_computation.14 | async-start | bytes 1769472 | tf_op jit(solution)/shard_map/all_gather | solution.py:515
  56.4 2.6 copy-start.11
  56.4 3.1 copy-start.12
  56.4 3.7 copy-start.13
  56.5 4.2 copy-start.14
  56.5 4.8 copy-start.15
  56.5 5.4 copy-start.6
  56.5 34.6 %all-gather.6.cloned.1.call-start = ((), (), s32[]{:S(2)}) async-start(), calls=%async_computation.7 | async-start | bytes 1769472 | tf_op jit(solution)/shard_map/all_gather | solution.py:512
  57.2 33.9 %all-gather.8.cloned.1.call-start = ((), (), s32[]{:S(2)}) async-start(), calls=%async_computation.8 | async-start | bytes 1769472 | tf_op jit(solution)/shard_map/all_gather | solution.py:512
  58.0 4.8 copy-start.17
  58.0 4.8 copy-start.16
  58.0 7.2 %copy-start.7 = (bf16[49,768]{1,0:T(8,128)(2,1)S(1)}, bf16[49,768]{1,0:T(8,128)(2,1)}, u32[]{:S(2)}) copy-start(bf16[49,768]{1,0:T(8,128)(2,1)} %param.35) | copy-start | bytes 225796
  58.0 93.8 %reduce-scatter.18.cloned.1.call-start = ((), (), s32[]{:S(2)}) async-start(), calls=%async_computation.11 | async-start | bytes 516096 | tf_op jit(solution)/shard_map/reduce_scatter | solution.py:527
  67.3 2.2 copy-start.2
  119.2 33.4 %reduce-scatter.24.cloned.1.call-start = ((), (), s32[]{:S(2)}) async-start(), calls=%async_computation.16 | async-start | bytes 442368
  143.8 2.2 copy-start.1
  145.9 16.1 %reduce-scatter.22.cloned.1.call-start = ((), (), s32[]{:S(2)}) async-start(), calls=%async_computation.15 | async-start | bytes 1327104
  147.5 65.7 %reduce-scatter.16.cloned.1.call-start = ((), (), s32[]{:S(2)}) async-start(), calls=%async_computation.10 | async-start | bytes 1769472 | tf_op jit(solution)/shard_map/reduce_scatter | solution.py:527
  147.5 3.1 copy-start
  150.5 62.7 %reduce-scatter.20.cloned.1.call-start = ((), (), s32[]{:S(2)}) async-start(), calls=%async_computation.13 | async-start | bytes 1769472 | tf_op jit(solution)/shard_map/reduce_scatter | solution.py:527
  151.7 174.2 %all-reduce.7.cloned.1.call-start = ((), (), s32[]{:S(2)}) async-start(), calls=%async_computation.12 | async-start | bytes 344064 | tf_op jit(solution)/shard_map/psum | solution.py:532
  152.5 277.2 %reduce-scatter.14.cloned.1.call-start = ((), (), s32[]{:S(2)}) async-start(), calls=%async_computation.9 | async-start | bytes 417792 | tf_op jit(solution)/shard_map/reduce_scatter | solution.py:527
  154.4 403.0 %reduce-scatter.26.cloned.1.call-start = ((), (), s32[]{:S(2)}) async-start(), calls=%async_computation.17 | async-start | bytes 1044480
  163.3 1.1 copy-start.19
  163.3 2.3 copy-start.4
  164.3 2.4 copy-start.3
  166.7 1.4 copy-start.8
  166.7 1.5 copy-start.18
  166.7 1.6 copy-start.10
  166.7 4.2 copy-start.9
Sparse Core Ops, SparseCore 0:
  56.5 5.0 all-gather.9
  63.2 10.5 all-gather.5
  75.3 10.4 all-gather.7
  119.3 3.7 reduce-scatter.17
  146.1 3.6 reduce-scatter.23
  152.5 9.4 reduce-scatter.21
  164.8 9.8 reduce-scatter.15
  177.6 9.8 reduce-scatter.19
  192.8 110.2 all-reduce.6
  308.8 120.7 reduce-scatter.13
  435.0 122.4 reduce-scatter.25

commit v2 on v1

--- a/solution.py
+++ b/solution.py
@@ -15,12 +15,14 @@
 POINTS = 17
 SEQ = 197
 ROWS = 208
+TAPS = 64
 KEYS = 256
 WIDTH = 384
 HALF = 152
 COEFS = 2 * HALF
 CLASS_ROW = 145
 CHUNK = 256
+SMALL = 32
 VMEM = 60 * 1024 * 1024
 
 f32 = jnp.float32
@@ -52,12 +54,12 @@
     inverse[HALF : HALF + count, 1:SEQ] = -weight * np.sin(angle)
     inverse[CLASS_ROW, 0] = 1.0
     turn = unit * freq @ taps.T
-    kernel = np.zeros((COEFS, KS * KS))
-    kernel[:count] = np.cos(turn)
-    kernel[HALF : HALF + count] = np.sin(turn)
-    back = np.zeros((COEFS, KS * KS))
-    back[:count] = weight * np.cos(turn)
-    back[HALF : HALF + count] = -weight * np.sin(turn)
+    kernel = np.zeros((COEFS, TAPS))
+    kernel[:count, : KS * KS] = np.cos(turn)
+    kernel[HALF : HALF + count, : KS * KS] = np.sin(turn)
+    back = np.zeros((COEFS, TAPS))
+    back[:count, : KS * KS] = weight * np.cos(turn)
+    back[HALF : HALF + count, : KS * KS] = -weight * np.sin(turn)
     one = np.zeros((COEFS, 1))
     one[CLASS_ROW] = 1.0
     return forward, inverse.T, kernel, back.T, one
@@ -92,6 +94,10 @@
     moment = jnp.mean(scaled * centred, axis=-1, keepdims=True)
     back = r * (scaled - jnp.mean(scaled, axis=-1, keepdims=True) - centred * (r * r * moment))
     return back, grad * (centred * r)
+
+
+def row(ref):
+    return ref[...].reshape(1, ref.shape[0])
 
 
 def add_rows(values):
@@ -111,7 +117,7 @@
     inputs = pad[...]
     centred, r = centre(inputs)
     inside = row_mask((ROWS, WIDTH))
-    n1 = jnp.where(inside, centred * r * gain1[...] + bias1[...], 0.0).astype(bf16)
+    n1 = jnp.where(inside, centred * r * row(gain1) + row(bias1), 0.0).astype(bf16)
     n1_out[0] = n1
     packed = dot(n1, wqkv[...]).astype(bf16)
     packed_out[0, :ROWS] = packed
@@ -155,10 +161,10 @@
         )
     attended = jnp.concatenate(pieces, axis=1).astype(bf16)
     att_out[0] = attended
-    middle = inputs + (dot(attended, wproj[...]) + pbias[...])
+    middle = inputs + (dot(attended, wproj[...]) + row(pbias))
     mid_out[0] = middle
     centred, r = centre(middle)
-    n2_out[0] = jnp.where(inside, centred * r * gain2[...] + bias2[...], 0.0).astype(bf16)
+    n2_out[0] = jnp.where(inside, centred * r * row(gain2) + row(bias2), 0.0).astype(bf16)
 
 
 def gelu_parts(hidden):
@@ -175,8 +181,8 @@
 
 
 def mlp(
-    n2, cot, mid, fc1, fc1b, conv, fc2, fc2b, fwd, inv, kh, kl, bh, bl, one,
-    block_out, gn2_out, gfc1_out, gb1_out, gconv_out, gfc2_out, gb2_out,
+    n2, cot, mid, fc1, conv, fc2, fc2b, fwd, inv, kh, kl, bh, bl, one,
+    block_out, gn2_out, gfc1_out, gconv_out, gfc2_out, gb2_out,
     cot_pad, pad, hid, grad, out_acc, conv_low, ghid_low,
 ):
     step = pl.program_id(0)
@@ -199,7 +205,7 @@
     turned = dot(kh[...], taps) + dot(kl[...], taps) + one[...]
     kr, ki = turned[:HALF], turned[HALF:]
     rows_all = n2[...].reshape(images * ROWS, WIDTH)
-    hid[...] = dot(rows_all, w1) + fc1b[...].astype(f32)
+    hid[...] = dot(rows_all, w1) + taps.astype(f32)[KS * KS : KS * KS + 1]
     grad[...] = dot_t(cot_pad[...], w2)
     cross_r = jnp.zeros((HALF, CHUNK), f32)
     cross_i = jnp.zeros((HALF, CHUNK), f32)
@@ -219,11 +225,11 @@
         ghid = (dot(inv[...], back) * slope).astype(bf16)
         bias_sum = bias_sum + add_rows(ghid.astype(f32))
         ghid_low[span, :] = ghid
-    gb1_out[...] = bias_sum
     cross = jnp.concatenate([cross_r, cross_i], axis=0)
     high = cross.astype(bf16)
     low = (cross - high.astype(f32)).astype(bf16)
     gconv_out[...] = dot(bh[...], high) + dot(bl[...], high) + dot(bh[...], low)
+    gconv_out[KS * KS : KS * KS + 1] = bias_sum
     convolved = conv_low[...]
     ghid_all = ghid_low[...]
     part = dot(convolved, w2).reshape(images, ROWS, WIDTH)
@@ -244,14 +250,14 @@
     @pl.when(step == pl.num_programs(0) - 1)
     def _():
         for b in range(images):
-            result = mid[b] + (out_acc[b] + fc2b[...])
+            result = mid[b] + (out_acc[b] + row(fc2b))
             block_out[b] = result[:SEQ].astype(bf16)
 
 
 def attention_backward(
-    pre, post, tok, cot, n1, packed, probs, attn, att, mid, gn2, wqkv, wproj, gain1, gain2,
-    gtok_out, gqkv_out, gproj_out, rows_out, mix_out,
-    pad, score, weight, low, mix,
+    pre, post, tok, cot, n1, packed, probs, attn, att, mid, gn2, wqkv, wproj, gain1, gain2, gb2,
+    gtok_out, gqkv_out, gproj_out, small_out,
+    pad, score, weight, low, mix, rows_out, square,
 ):
     step = pl.program_id(0)
 
@@ -266,7 +272,7 @@
     pad[:SEQ] = cot[0].astype(f32)
     centred, r = centre(mid[0])
     grad = gn2[0]
-    back, gain_rows = norm_back(centred, r, gain2[...], grad)
+    back, gain_rows = norm_back(centred, r, row(gain2), grad)
     rows_out[3:4] += add_rows(gain_rows)
     rows_out[4:5] += add_rows(grad)
     gmid = pad[...] + back
@@ -333,14 +339,20 @@
     gnormed = dot_t(gpacked, wqkv[...])
     pad[:SEQ] = tok[0].astype(f32)
     centred, r = centre(pad[...])
-    back, gain_rows = norm_back(centred, r, gain1[...], gnormed)
+    back, gain_rows = norm_back(centred, r, row(gain1), gnormed)
     rows_out[0:1] += add_rows(gain_rows)
     rows_out[1:2] += add_rows(gnormed)
     gtok_out[0] = (gmid + back)[:SEQ]
 
     @pl.when(step == pl.num_programs(0) - 1)
     def _():
-        mix_out[...] = jnp.sum(mix[...], axis=1)
+        rows_out[5:6] = gb2[...]
+        for t in range(WIDTH // 128):
+            small_out[8 * t : 8 * t + 8] = rows_out[:, 128 * t : 128 * t + 128]
+        square[...] = jnp.zeros_like(square)
+        square[: 2 * HEADS * HEADS] = jnp.sum(mix[...], axis=1)
+        sums = add_rows(square[...].T)
+        small_out[24:] = jnp.concatenate([sums, jnp.zeros((SMALL - 25, 128), f32)], axis=0)
 
 
 def whole(shape):
@@ -358,13 +370,13 @@
 def call_forward(tokens, wqkv, wproj, pre, post, gain1, bias1, pbias, gain2, bias2):
     images = tokens.shape[0]
     smem = pl.BlockSpec(memory_space=pltpu.SMEM)
-    row = whole((1, WIDTH))
+    vector = whole((WIDTH,))
     return pl.pallas_call(
         attention_forward,
         grid=(images,),
         in_specs=[
             smem, smem, image((SEQ, WIDTH)), whole((WIDTH, 3 * WIDTH)), whole((WIDTH, WIDTH)),
-            row, row, row, row, row,
+            vector, vector, vector, vector, vector,
         ],
         out_specs=[
             image((ROWS, WIDTH)), image((KEYS, 3 * WIDTH)), image((HEADS, ROWS, KEYS)),
@@ -390,7 +402,7 @@
     )(pre, post, tokens, wqkv, wproj, gain1, bias1, pbias, gain2, bias2)
 
 
-def call_mlp(n2, cotangent, middle, fc1, fc1_bias, conv, fc2, fc2_bias):
+def call_mlp(n2, cotangent, middle, fc1, conv, fc2, fc2_bias):
     images = n2.shape[0]
     units = fc1.shape[1]
     steps = units // CHUNK
@@ -405,28 +417,26 @@
         jnp.asarray(one.astype(np.float32)),
     ]
     columns = lambda rows: pl.BlockSpec((rows, CHUNK), lambda i: (0, i))
-    taps = KS * KS
     total = images * ROWS
     return pl.pallas_call(
         mlp,
         grid=(steps,),
         in_specs=[
             whole((images, ROWS, WIDTH)), whole((images, SEQ, WIDTH)), whole((images, ROWS, WIDTH)),
-            columns(WIDTH), columns(1), columns(taps),
-            pl.BlockSpec((CHUNK, WIDTH), lambda i: (i, 0)), whole((1, WIDTH)),
+            columns(WIDTH), columns(TAPS),
+            pl.BlockSpec((CHUNK, WIDTH), lambda i: (i, 0)), whole((WIDTH,)),
         ]
         + [whole(c.shape) for c in consts],
         out_specs=[
             whole((images, SEQ, WIDTH)), whole((images, ROWS, WIDTH)),
-            columns(WIDTH), columns(1), columns(taps),
+            columns(WIDTH), columns(TAPS),
             pl.BlockSpec((CHUNK, WIDTH), lambda i: (i, 0)), whole((1, WIDTH)),
         ],
         out_shape=[
             jax.ShapeDtypeStruct((images, SEQ, WIDTH), bf16),
             jax.ShapeDtypeStruct((images, ROWS, WIDTH), f32),
             jax.ShapeDtypeStruct((WIDTH, units), f32),
-            jax.ShapeDtypeStruct((1, units), f32),
-            jax.ShapeDtypeStruct((taps, units), f32),
+            jax.ShapeDtypeStruct((TAPS, units), f32),
             jax.ShapeDtypeStruct((units, WIDTH), f32),
             jax.ShapeDtypeStruct((1, WIDTH), f32),
         ],
@@ -441,15 +451,15 @@
         ],
         compiler_params=params(),
         name="mlp",
-    )(n2, cotangent, middle, fc1, fc1_bias, conv, fc2, fc2_bias, *consts)
+    )(n2, cotangent, middle, fc1, conv, fc2, fc2_bias, *consts)
 
 
 def call_backward(
-    tokens, cotangent, n1, packed, probs, attn, att, mid, gn2, wqkv, wproj, pre, post, gain1, gain2
+    tokens, cotangent, n1, packed, probs, attn, att, mid, gn2, wqkv, wproj, pre, post, gain1, gain2, gb2
 ):
     images = tokens.shape[0]
     smem = pl.BlockSpec(memory_space=pltpu.SMEM)
-    row = whole((1, WIDTH))
+    vector = whole((WIDTH,))
     return pl.pallas_call(
         attention_backward,
         grid=(images,),
@@ -457,18 +467,18 @@
             smem, smem, image((SEQ, WIDTH)), image((SEQ, WIDTH)), image((ROWS, WIDTH)),
             image((KEYS, 3 * WIDTH)), image((HEADS, ROWS, KEYS)), image((HEADS, ROWS, KEYS)),
             image((ROWS, WIDTH)), image((ROWS, WIDTH)), image((ROWS, WIDTH)),
-            whole((WIDTH, 3 * WIDTH)), whole((WIDTH, WIDTH)), row, row,
+            whole((WIDTH, 3 * WIDTH)), whole((WIDTH, WIDTH)), vector, vector,
+            whole((1, WIDTH)),
         ],
         out_specs=[
             image((SEQ, WIDTH)), whole((WIDTH, 3 * WIDTH)), whole((WIDTH, WIDTH)),
-            whole((8, WIDTH)), whole((2 * HEADS * HEADS, 128)),
+            whole((SMALL, 128)),
         ],
         out_shape=[
             jax.ShapeDtypeStruct((images, SEQ, WIDTH), f32),
             jax.ShapeDtypeStruct((WIDTH, 3 * WIDTH), f32),
             jax.ShapeDtypeStruct((WIDTH, WIDTH), f32),
-            jax.ShapeDtypeStruct((8, WIDTH), f32),
-            jax.ShapeDtypeStruct((2 * HEADS * HEADS, 128), f32),
+            jax.ShapeDtypeStruct((SMALL, 128), f32),
         ],
         scratch_shapes=[
             pltpu.VMEM((ROWS, WIDTH), f32),
@@ -476,66 +486,492 @@
             pltpu.VMEM((HEADS, ROWS, KEYS), f32),
             pltpu.VMEM((HEADS, ROWS, KEYS), bf16),
             pltpu.VMEM((2 * HEADS * HEADS, 8, 128), f32),
+            pltpu.VMEM((8, WIDTH), f32),
+            pltpu.VMEM((128, 128), f32),
         ],
         compiler_params=params(),
         name="attention_backward",
     )(
         pre, post, tokens, cotangent, n1, packed, probs, attn, att, mid, gn2, wqkv, wproj,
-        gain1, gain2,
+        gain1, gain2, gb2,
     )
 
 
 def local_block(
     tokens, norm1_gain, norm1_bias, wqkv, mix_pre, mix_post, wproj, proj_bias, norm2_gain,
-    norm2_bias, fc1, fc1_bias, conv, fc2, fc2_bias, cotangent,
+    norm2_bias, fc1, taps, fc2, fc2_bias, cotangent,
 ):
-    row = lambda v: v.reshape(1, -1)
-    gain1, gain2 = row(norm1_gain), row(norm2_gain)
     n1, packed, probs, attn, att, mid, n2 = call_forward(
-        tokens, wqkv, wproj, mix_pre, mix_post, gain1, row(norm1_bias), row(proj_bias), gain2,
-        row(norm2_bias),
-    )
-    block_out, gn2, gfc1, gb1, gconv, gfc2, gb2 = call_mlp(
-        n2, cotangent, mid, fc1, row(fc1_bias), conv, fc2, row(fc2_bias)
-    )
-    gtok, gqkv, gproj, rows, mix = call_backward(
+        tokens, wqkv, wproj, mix_pre, mix_post, norm1_gain, norm1_bias, proj_bias, norm2_gain,
+        norm2_bias,
+    )
+    block_out, gn2, gfc1, gconv, gfc2, gb2 = call_mlp(n2, cotangent, mid, fc1, taps, fc2, fc2_bias)
+    gtok, gqkv, gproj, small = call_backward(
         tokens, cotangent, n1, packed, probs, attn, att, mid, gn2, wqkv, wproj, mix_pre, mix_post,
-        gain1, gain2,
-    )
-    return block_out, gtok, gqkv, gproj, gfc1, gb1, gconv, gfc2, gb2, rows, mix
-
-
-def shards(
+        norm1_gain, norm2_gain, gb2,
+    )
+    return block_out, gtok, gqkv, gproj, gfc1, gconv, gfc2, small
+
+
+SIDES = (8, 4, 2, 1)
+ORDERS = ((3, 2, 1, 0), (2, 1, 0, 3), (1, 0, 3, 2))
+MESH_IDS = pl.DeviceIdType.MESH
+PIECE = 144
+BLOCK = 320
+
+
+def place():
+    dp, core = lax.axis_index("dp"), lax.axis_index("tensor")
+    bits = [lax.rem(dp // stride, 2) for stride in SIDES]
+    partners = [(dp + (1 - 2 * bit) * stride, core) for bit, stride in zip(bits, SIDES)]
+    return bits, partners, (dp, 1 - core), core
+
+
+def meet(partners):
+    barrier = pltpu.get_barrier_semaphore()
+    for partner in partners:
+        pl.semaphore_signal(barrier, inc=1, device_id=partner, device_id_type=MESH_IDS)
+    pl.semaphore_wait(barrier, len(partners))
+
+
+def send(src, dst, sems, index, device):
+    copy = pltpu.make_async_remote_copy(
+        src_ref=src, dst_ref=dst, send_sem=sems.at[0, index], recv_sem=sems.at[1, index],
+        device_id=device, device_id_type=MESH_IDS,
+    )
+    copy.start()
+    return copy
+
+
+def region(fixed, rows):
+    return tuple(fixed.get(axis, slice(None)) for axis in range(4)) + (rows,)
+
+
+def combos(count):
+    return [tuple((i >> (count - 1 - j)) & 1 for j in range(count)) for i in range(2**count)]
+
+
+class Halving:
+    def __init__(self, acc, landing, sems, first, parts, bits, partners):
+        self.acc, self.landing, self.sems, self.first = acc, landing, sems, first
+        self.parts, self.bits, self.partners = parts, bits, partners
+        self.copies = {}
+
+    def start(self, part, step):
+        order, rows = ORDERS[part], pl.ds(*self.parts[part])
+        axis = order[step]
+        fixed = {a: self.bits[a] for a in order[:step]}
+        fixed[axis] = 1 - self.bits[axis]
+        dst = self.landing[step].at[(slice(None),) * (3 - step) + (rows,)]
+        self.copies[part, step] = send(
+            self.acc.at[region(fixed, rows)], dst, self.sems,
+            self.first + step * len(self.parts) + part, self.partners[axis],
+        )
+
+    def add(self, part, step):
+        order, rows = ORDERS[part], pl.ds(*self.parts[part])
+        self.copies[part, step].wait_recv()
+        fixed = {a: self.bits[a] for a in order[: step + 1]}
+        free = [a for a in range(4) if a not in fixed]
+        for combo in combos(len(free)):
+            where = region({**fixed, **dict(zip(free, combo))}, rows)
+            came = self.landing[step][combo + (rows,)]
+            self.acc[where] = (self.acc[where].astype(f32) + came.astype(f32)).astype(bf16)
+
+    def finish(self):
+        for copy in self.copies.values():
+            copy.wait_send()
+
+
+class Doubling:
+    def __init__(self, full, sems, first, parts, bits, partners):
+        self.full, self.sems, self.first = full, sems, first
+        self.parts, self.bits, self.partners = parts, bits, partners
+        self.copies = {}
+
+    def held(self, part, step):
+        order, rows = ORDERS[part][::-1], pl.ds(*self.parts[part])
+        return region({a: self.bits[a] for a in order[step:]}, rows)
+
+    def come(self, part, step):
+        order, rows = ORDERS[part][::-1], pl.ds(*self.parts[part])
+        fixed = {a: self.bits[a] for a in order[step + 1 :]}
+        fixed[order[step]] = 1 - self.bits[order[step]]
+        return region(fixed, rows)
+
+    def start(self, part, step):
+        axis = ORDERS[part][::-1][step]
+        where = self.held(part, step)
+        self.copies[part, step] = send(
+            self.full.at[where], self.full.at[where], self.sems,
+            self.first + step * len(self.parts) + part, self.partners[axis],
+        )
+
+    def wait(self, part, step):
+        self.copies[part, step].wait_recv()
+
+    def finish(self):
+        for copy in self.copies.values():
+            copy.wait_send()
+
+
+def tiles(values):
+    return jnp.concatenate(
+        [values[:, 128 * t : 128 * t + 128] for t in range(values.shape[1] // 128)], axis=0
+    )
+
+
+def untiles(values, count):
+    rows = values.shape[0] // count
+    return jnp.concatenate([values[t * rows : (t + 1) * rows] for t in range(count)], axis=1)
+
+
+GATHER_PARTS = ((0, 48), (48, 48), (96, 48))
+
+
+def gather_kernel(
+    qkv, proj, fc1, conv, bias, fc2, wqkv, wproj, fc1_full, conv_full, fc2_full,
+    full, other, taps, sems, pair_sems, local_sems,
+):
+    bits, partners, pair, core = place()
+    half = fc1.shape[1]
+    mine = tuple(bits)
+    cols = pl.ds(pl.multiple_of(core * half, 128), half)
+    both = jnp.concatenate([qkv[...].astype(f32), proj[...].astype(f32)], axis=1)
+    full[mine] = tiles(both).astype(bf16)
+    taps[...] = jnp.zeros(taps.shape, f32)
+    taps[: KS * KS] = conv[...].astype(f32)
+    taps[KS * KS : KS * KS + 1] = bias[...].astype(f32).reshape(1, half)
+    conv_full[:, cols] = taps[...].astype(bf16)
+    meet(partners + [pair])
+    rows = pl.ds(pl.multiple_of(core * half, 128), half)
+    pair_copies = [
+        send(full.at[mine], other.at[mine], pair_sems, 0, pair),
+        send(conv_full.at[:, cols], conv_full.at[:, cols], pair_sems, 1, pair),
+        send(fc1, fc1_full.at[:, cols], pair_sems, 2, pair),
+        send(fc2, fc2_full.at[rows], pair_sems, 3, pair),
+    ]
+    local = [
+        pltpu.make_async_copy(fc1, fc1_full.at[:, cols], local_sems.at[0]),
+        pltpu.make_async_copy(fc2, fc2_full.at[rows], local_sems.at[1]),
+    ]
+    gather = Doubling(full, sems, 0, GATHER_PARTS, bits, partners)
+    parts = range(len(GATHER_PARTS))
+    for part in parts:
+        gather.start(part, 0)
+    for copy in local:
+        copy.start()
+    for step in range(4):
+        for part in parts:
+            gather.wait(part, step)
+            if step < 3:
+                gather.start(part, step + 1)
+            where = gather.come(part, step)
+            pair_copies.append(
+                send(full.at[where], other.at[where], pair_sems, 4 + 3 * step + part, pair)
+            )
+    for copy in pair_copies:
+        copy.wait_recv()
+    width = qkv.shape[1]
+    for d in range(0, 16, 2):
+        blocks = []
+        for ref in (full, other):
+            pair_rows = []
+            for e in (d, d + 1):
+                index = tuple((e // stride) % 2 for stride in SIDES)
+                pair_rows.append(untiles(ref[index].astype(f32), 6))
+            blocks.append(jnp.concatenate(pair_rows, axis=0))
+        flip = core == 1
+        first = jnp.where(flip, blocks[1], blocks[0])
+        second = jnp.where(flip, blocks[0], blocks[1])
+        rows = slice(24 * d, 24 * d + 48)
+        wqkv[rows, :] = jnp.concatenate([first[:, :width], second[:, :width]], axis=1).astype(bf16)
+        wproj[rows, :] = jnp.concatenate([first[:, width:], second[:, width:]], axis=1).astype(bf16)
+    for copy in local:
+        copy.wait()
+    for copy in pair_copies:
+        copy.wait_send()
+    gather.finish()
+
+
+def call_gather(qkv, proj, fc1, conv, bias, fc2):
+    vmem = pl.BlockSpec(memory_space=pltpu.VMEM)
+    half = fc1.shape[1]
+    return pl.pallas_call(
+        gather_kernel,
+        in_specs=[vmem] * 6,
+        out_specs=[vmem] * 5,
+        out_shape=[
+            jax.ShapeDtypeStruct((WIDTH, 3 * WIDTH), bf16),
+            jax.ShapeDtypeStruct((WIDTH, WIDTH), bf16),
+            jax.ShapeDtypeStruct((WIDTH, 2 * half), bf16),
+            jax.ShapeDtypeStruct((64, 2 * half), bf16),
+            jax.ShapeDtypeStruct((2 * half, WIDTH), bf16),
+        ],
+        scratch_shapes=[
+            pltpu.VMEM((2, 2, 2, 2, PIECE, 128), bf16),
+            pltpu.VMEM((2, 2, 2, 2, PIECE, 128), bf16),
+            pltpu.VMEM((64, half), f32),
+            pltpu.SemaphoreType.DMA((2, 12)),
+            pltpu.SemaphoreType.DMA((2, 16)),
+            pltpu.SemaphoreType.DMA((2,)),
+        ],
+        compiler_params=pltpu.CompilerParams(
+            vmem_limit_bytes=VMEM, collective_id=0, has_side_effects=True
+        ),
+        name="gather_weights",
+    )(qkv, proj, fc1, conv, bias, fc2)
+
+
+MLP_PARTS = ((0, 112), (112, 112), (224, 96))
+
+
+def reduce_mlp_kernel(gfc1, gconv, gfc2, total, acc, out, came, l0, l1, l2, l3, full, sems, psems):
+    bits, partners, pair, core = place()
+    half = gfc1.shape[1] // 2
+    mine = tuple(bits)
+
+    def pack(side):
+        start = pl.multiple_of(side * half, 128)
+        taps = tiles(gconv[:, pl.ds(start, half)])
+        for d in range(16):
+            one = tiles(gfc1[24 * d : 24 * d + 24, pl.ds(start, half)])
+            two = tiles(gfc2[pl.ds(pl.multiple_of(start + 48 * d, 16), 48), :])
+            three = taps[24 * d : 24 * d + 24]
+            empty = jnp.zeros((BLOCK - 312, 128), f32)
+            index = tuple((d // stride) % 2 for stride in SIDES)
+            yield index, jnp.concatenate([one, two, three, empty], axis=0)
+
+    for index, values in pack(1 - core):
+        out[index] = values.astype(bf16)
+    meet(partners + [pair])
+    copy = send(out, came, psems, 0, pair)
+    copy.wait_recv()
+    for index, values in pack(core):
+        acc[index] = (values + came[index].astype(f32)).astype(bf16)
+    landing = [l0, l1, l2, l3]
+    halving = Halving(acc, landing, sems, 0, MLP_PARTS, bits, partners)
+    parts = range(3)
+    for part in parts:
+        halving.start(part, 0)
+    for step in range(4):
+        for part in parts:
+            halving.add(part, step)
+            if step < 3:
+                halving.start(part, step + 1)
+    full[mine] = acc[mine]
+    doubling = Doubling(full, sems, 12, MLP_PARTS, bits, partners)
+    for part in parts:
+        doubling.start(part, 0)
+    for step in range(4):
+        for part in parts:
+            doubling.wait(part, step)
+            if step < 3:
+                doubling.start(part, step + 1)
+    total[...] = full[...]
+    copy.wait_send()
+    halving.finish()
+    doubling.finish()
+
+
+def call_reduce_mlp(gfc1, gconv, gfc2):
+    vmem = pl.BlockSpec(memory_space=pltpu.VMEM)
+    buffer = lambda free: pltpu.VMEM((2,) * free + (BLOCK, 128), bf16)
+    return pl.pallas_call(
+        reduce_mlp_kernel,
+        in_specs=[vmem] * 3,
+        out_specs=vmem,
+        out_shape=jax.ShapeDtypeStruct((2, 2, 2, 2, BLOCK, 128), bf16),
+        scratch_shapes=[
+            buffer(4), buffer(4), buffer(4), buffer(3), buffer(2), buffer(1), buffer(0), buffer(4),
+            pltpu.SemaphoreType.DMA((2, 24)),
+            pltpu.SemaphoreType.DMA((2, 1)),
+        ],
+        compiler_params=pltpu.CompilerParams(
+            vmem_limit_bytes=VMEM, collective_id=1, has_side_effects=True
+        ),
+        name="reduce_mlp",
+    )(gfc1, gconv, gfc2)
+
+
+def reduce_attention_kernel(
+    gqkv, gproj, small, total, small_total, acc, own, out, came, l0, l1, l2, l3, sums, landed,
+    sems, psems,
+):
+    bits, partners, pair, core = place()
+    width, proj_width = gqkv.shape[1] // 2, gproj.shape[1] // 2
+    mine = tuple(bits)
+    for side in range(2):
+
+        @pl.when(core == side)
+        def _():
+            for d in range(16):
+                rows = slice(24 * d, 24 * d + 24)
+                index = tuple((d // stride) % 2 for stride in SIDES)
+                for half, ref in ((side, own), (1 - side, out)):
+                    both = jnp.concatenate(
+                        [
+                            gqkv[rows, half * width : (half + 1) * width],
+                            gproj[rows, half * proj_width : (half + 1) * proj_width],
+                        ],
+                        axis=1,
+                    )
+                    ref[index] = tiles(both).astype(ref.dtype)
+
+    sums[0] = small[...]
+    meet(partners + [pair])
+    copy = send(out, came, psems, 0, pair)
+    copies = [send(sums.at[0], landed.at[0], psems, 1, pair)]
+    copy.wait_recv()
+    for d in range(16):
+        index = tuple((d // stride) % 2 for stride in SIDES)
+        acc[index] = (own[index] + came[index].astype(f32)).astype(bf16)
+    halving = Halving(acc, [l0, l1, l2, l3], sems, 0, GATHER_PARTS, bits, partners)
+    parts = range(3)
+    for part in parts:
+        halving.start(part, 0)
+    for step in range(4):
+        copies[step].wait_recv()
+        sums[step + 1] = sums[step] + landed[step]
+        copies.append(
+            send(sums.at[step + 1], landed.at[step + 1], psems, 2 + step, partners[3 - step])
+        )
+        for part in parts:
+            halving.add(part, step)
+            if step < 3:
+                halving.start(part, step + 1)
+    copies[4].wait_recv()
+    small_total[...] = sums[4] + landed[4]
+    total[...] = acc[mine]
+    copy.wait_send()
+    for copy in copies:
+        copy.wait_send()
+    halving.finish()
+
+
+def call_reduce_attention(gqkv, gproj, small):
+    vmem = pl.BlockSpec(memory_space=pltpu.VMEM)
+    buffer = lambda free, dtype=bf16: pltpu.VMEM((2,) * free + (PIECE, 128), dtype)
+    return pl.pallas_call(
+        reduce_attention_kernel,
+        in_specs=[vmem] * 3,
+        out_specs=[vmem] * 2,
+        out_shape=[
+            jax.ShapeDtypeStruct((PIECE, 128), bf16),
+            jax.ShapeDtypeStruct((SMALL, 128), f32),
+        ],
+        scratch_shapes=[
+            buffer(4), buffer(4, f32), buffer(4), buffer(4), buffer(3), buffer(2), buffer(1),
+            buffer(0), pltpu.VMEM((5, SMALL, 128), f32), pltpu.VMEM((5, SMALL, 128), f32),
+            pltpu.SemaphoreType.DMA((2, 12)),
+            pltpu.SemaphoreType.DMA((2, 6)),
+        ],
+        compiler_params=pltpu.CompilerParams(
+            vmem_limit_bytes=VMEM, collective_id=2, has_side_effects=True
+        ),
+        name="reduce_attention",
+    )(gqkv, gproj, small)
+
+
+def finish_kernel(
+    total, piece, small, gfc1, gb1, gconv, gfc2, gqkv, gproj, g1, b1, pb, g2, b2, fb, pre, post,
+    taps, mixes,
+):
+    for d in range(16):
+        index = tuple((d // stride) % 2 for stride in SIDES)
+        block = total[index].astype(f32)
+        gfc1[24 * d : 24 * d + 24, :] = untiles(block[:144], 6)
+        gfc2[48 * d : 48 * d + 48, :] = untiles(block[144:288], 3)
+        taps[24 * d : 24 * d + 24, :] = block[288:312]
+    filters = untiles(taps[...], 6)
+    gconv[...] = filters[: KS * KS]
+    gb1[...] = filters[KS * KS].reshape(gb1.shape)
+    both = untiles(piece[...].astype(f32), 6)
+    width = gqkv.shape[1]
+    gqkv[...] = both[:, :width]
+    gproj[...] = both[:, width:]
+    rows = untiles(small[:24], 3)
+    for index, ref in enumerate((g1, b1, pb, g2, b2, fb)):
+        ref[...] = rows[index].reshape(ref.shape)
+    line = small[24:25]
+    for index, ref in enumerate((pre, post)):
+        for g in range(HEADS):
+            start = HEADS * HEADS * index + HEADS * g
+            mixes[index, g : g + 1, :HEADS] = line[:, start : start + HEADS]
+    pre[...] = mixes[0, :HEADS, :HEADS] * 0.125
+    post[...] = mixes[1, :HEADS, :HEADS]
+
+
+def call_finish(total, piece, small, half):
+    vmem = pl.BlockSpec(memory_space=pltpu.VMEM)
+    shape = lambda *dims: jax.ShapeDtypeStruct(dims, f32)
+    return pl.pallas_call(
+        finish_kernel,
+        in_specs=[vmem] * 3,
+        out_specs=[vmem] * 14,
+        out_shape=[
+            shape(WIDTH, half), shape(half), shape(KS * KS, half), shape(half, WIDTH),
+            shape(24, 3 * WIDTH // 2), shape(24, WIDTH // 2),
+        ]
+        + [shape(WIDTH)] * 6
+        + [shape(HEADS, HEADS)] * 2,
+        scratch_shapes=[pltpu.VMEM((WIDTH, 128), f32), pltpu.VMEM((2, 8, 128), f32)],
+        compiler_params=pltpu.CompilerParams(vmem_limit_bytes=VMEM),
+        name="finish",
+    )(total, piece, small)
+
+
+def shards_any(
     tokens, norm1_gain, norm1_bias, qkv_weight, mix_pre, mix_post, proj_weight, proj_bias,
     norm2_gain, norm2_bias, fc1_weight, fc1_bias, conv_weight, fc2_weight, fc2_bias, cotangent,
 ):
     gather = lambda v, axis, dim: lax.all_gather(v, axis, axis=dim, tiled=True)
     both = jnp.concatenate([qkv_weight, proj_weight], axis=1)
-    rows = gather(both, "dp", 0)
-    pair = lax.all_gather(rows, "tensor", axis=0)
+    pair = lax.all_gather(gather(both, "dp", 0), "tensor", axis=0)
     columns = qkv_weight.shape[1]
     wqkv = jnp.concatenate([pair[0, :, :columns], pair[1, :, :columns]], axis=1)
     wproj = jnp.concatenate([pair[0, :, columns:], pair[1, :, columns:]], axis=1)
     fc1 = gather(fc1_weight, "tensor", 1)
-    fc1b = gather(fc1_bias, "tensor", 0)
-    conv = gather(conv_weight, "tensor", 1)
+    taps = jnp.concatenate([conv_weight, fc1_bias[None]], axis=0)
+    taps = jnp.pad(gather(taps, "tensor", 1), ((0, TAPS - KS * KS - 1), (0, 0)))
     fc2 = gather(fc2_weight, "tensor", 0)
-    block_out, gtok, gqkv, gproj, gfc1, gb1, gconv, gfc2, gb2, rows, mix = local_block(
+    block_out, gtok, gqkv, gproj, gfc1, gconv, gfc2, small = local_block(
         tokens, norm1_gain, norm1_bias, wqkv, mix_pre, mix_post, wproj, proj_bias, norm2_gain,
-        norm2_bias, fc1, fc1b, conv, fc2, fc2_bias, cotangent,
+        norm2_bias, fc1, taps, fc2, fc2_bias, cotangent,
     )
     scatter = lambda v, axis, dim: lax.psum_scatter(v, axis, scatter_dimension=dim, tiled=True)
-    gqkv = scatter(scatter(gqkv.astype(bf16), "tensor", 1).astype(f32), "dp", 0)
-    gproj = scatter(scatter(gproj.astype(bf16), "tensor", 1).astype(f32), "dp", 0)
-    gfc1 = lax.psum(scatter(gfc1.astype(bf16), "tensor", 1).astype(f32), "dp")
-    gfc2 = lax.psum(scatter(gfc2.astype(bf16), "tensor", 0).astype(f32), "dp")
+    gqkv = scatter(scatter(gqkv, "tensor", 1), "dp", 0)
+    gproj = scatter(scatter(gproj, "tensor", 1), "dp", 0)
+    gfc1 = lax.psum(scatter(gfc1, "tensor", 1), "dp")
+    gfc2 = lax.psum(scatter(gfc2, "tensor", 0), "dp")
     gconv = lax.psum(scatter(gconv, "tensor", 1), "dp")
-    gb1 = lax.psum(scatter(gb1[0], "tensor", 0), "dp")
-    mixes = jnp.sum(mix, axis=1).reshape(2, HEADS, HEADS)
-    rows, gb2, mixes = lax.psum((rows, gb2, mixes), ("dp", "tensor"))
+    small = lax.psum(small, ("dp", "tensor"))
+    rows = jnp.concatenate([small[0:8], small[8:16], small[16:24]], axis=1)
+    mixes = small[24, : 2 * HEADS * HEADS].reshape(2, HEADS, HEADS)
     return (
         block_out, gtok, rows[0], rows[1], gqkv, mixes[0] * 0.125, mixes[1], gproj, rows[2],
-        rows[3], rows[4], gfc1, gb1, gconv, gfc2, gb2[0],
+        rows[3], rows[4], gfc1, gconv[KS * KS], gconv[: KS * KS], gfc2, rows[5],
+    )
+
+
+def shards_sixteen(
+    tokens, norm1_gain, norm1_bias, qkv_weight, mix_pre, mix_post, proj_weight, proj_bias,
+    norm2_gain, norm2_bias, fc1_weight, fc1_bias, conv_weight, fc2_weight, fc2_bias, cotangent,
+):
+    wqkv, wproj, fc1, taps, fc2 = call_gather(
+        qkv_weight, proj_weight, fc1_weight, conv_weight, fc1_bias, fc2_weight
+    )
+    block_out, gtok, gqkv, gproj, gfc1, gconv, gfc2, small = local_block(
+        tokens, norm1_gain, norm1_bias, wqkv, mix_pre, mix_post, wproj, proj_bias, norm2_gain,
+        norm2_bias, fc1, taps, fc2, fc2_bias, cotangent,
+    )
+    total = call_reduce_mlp(gfc1, gconv, gfc2)
+    piece, small = call_reduce_attention(gqkv, gproj, small)
+    gfc1, gb1, gconv, gfc2, gqkv, gproj, g1, b1, pb, g2, b2, fb, pre, post = call_finish(
+        total, piece, small, fc1_weight.shape[1]
+    )
+    return (
+        block_out, gtok, g1, b1, gqkv, pre, post, gproj, pb, g2, b2, gfc1, gb1, gconv, gfc2, fb
     )
 
 
@@ -549,4 +985,6 @@
         spec, spec, P(), P(), P("dp", "tensor"), P(), P(), P("dp", "tensor"), P(), P(), P(),
         P(None, "tensor"), P("tensor"), P(None, "tensor"), P("tensor", None), P(),
     )
-    return jax.shard_map(shards, mesh=mesh, in_specs=in_specs, out_specs=out_specs, check_vma=False)
+    sixteen = mesh.shape["dp"] == 16 and mesh.shape["tensor"] == 2
+    body = shards_sixteen if sixteen else shards_any
+    return jax.shard_map(body, mesh=mesh, in_specs=in_specs, out_specs=out_specs, check_vma=False)

time: 566 us -> 180 us (0.32)
  waiting for transfers between devices: 241 us -> 0 us
  blocking collectives: 209 us -> 0 us
  Pallas kernels: 72.9 us -> 171 us
  between operations: 14.8 us -> 0.68 us
  other arithmetic: 11 us -> 0 us
  local copies, waits for them, and re-layouts: 16.6 us -> 7.66 us
    psum x2 -> x0, blocking collectives: 154 us -> none  [the longest x1 113 us: shards(): gfc1 = lax.psum(scatter(gfc1.astype(bf16), 'tensor', 1).astype(f32), 'dp')]
    unnamed x14 -> x0, waiting for transfers between devices: 137 us -> none
    reduce_scatter x4 -> x0, waiting for transfers between devices: 104 us -> none  [shards(): lax.psum_scatter(v, axis, scatter_dimension=dim, tiled=True)]
    pallas_call x0 -> x4, Pallas kernels: none -> 98.4 us  [the longest x1 50.3 us: call_reduce_mlp(): pl.pallas_call(reduce_mlp_kernel, in_specs=[vmem] * 3, out_specs=vmem, ou...]
    all_gather x3 -> x0, blocking collectives: 52.2 us -> none  [shards(): gather = lambda v, axis, dim: lax.all_gather(v, axis, axis=dim, tiled=True)]
    convert_element_type x6 -> x0, other arithmetic: 7.26 us -> none  [the longest x1 2.97 us: shards(): gfc1 = lax.psum(scatter(gfc1.astype(bf16), 'tensor', 1).astype(f32), 'dp')]
  transfers between devices with their start and end apart: 11 -> 0, of which waited for: 3 -> 0; matrix products, arithmetic and copies ran while one was open for 4% -> 0% of each run, Pallas kernels for 8% -> 0%
where the time goes in v2:
time: 180 us
  Pallas kernels  171 us (95%)
  local copies, waits for them, and re-layouts  7.66 us (4%)
    pallas_call x1, Pallas kernels, call_reduce_mlp(): pl.pallas_call(reduce_mlp_kernel, in_specs=[vmem] * 3, out_specs=vmem, ou...  50.3 us
    pallas_call x1, Pallas kernels, call_mlp(): pl.pallas_call(mlp, grid=(steps,), in_specs=[whole((images, ROWS, WIDTH))...  27.9 us
    pallas_call x1, Pallas kernels, call_backward(): pl.pallas_call(attention_backward, grid=(images,), in_specs=[smem, smem,...  24.6 us
    pallas_call x1, Pallas kernels, call_gather(): pl.pallas_call(gather_kernel, in_specs=[vmem] * 6, out_specs=[vmem] * 5,...  24.6 us
    pallas_call x1, Pallas kernels, call_reduce_attention(): pl.pallas_call(reduce_attention_kernel, in_specs=[vmem] * 3, out_specs=[v...  20.6 us
    pallas_call x1, Pallas kernels, call_forward(): pl.pallas_call(attention_forward, grid=(images,), in_specs=[smem, smem, i...  20.3 us
    unnamed x6, local copies, waits for them, and re-layouts  7.66 us

profile of v2, /device:TPU:0, one launch (start us, length us, event | category | flops | bytes accessed | tf_op | source)
XLA Modules:
  0.0 179.6 jit_solution(10759479453011763088)
XLA Ops:
  0.6 2.0 %copy.39.tok = bf16[4,197,384]{2,1,0:T(8,128)(2,1)} copy(bf16[4,197,384]{2,0,1:T(4,128)(2,1)} %param.23) | data formatting | bytes 1210368 | tf_op args[0]
  2.6 0.0 copy-start
  2.6 24.6 %gather_weights.1 = (bf16[384,1152]{1,0:T(8,128)(2,1)}, bf16[384,384]{1,0:T(8,128)(2,1)}, bf16[384,1536]{1,0:T(8,128)(2,1)}, bf16[64,1536]{1,0:T(8,128)(2,1)}, bf16[1536,384]{1,0:T(8,128)(2,1)}) custom-call(bf16[24,576]{1,0:T(8,128)(2,1)} %qkv.1, bf16[24,192]{1,0:T(8,128)(2,1)} %proj.1, bf16[384,768]{1,0:T(8,128)(2,1)} %fc1.1, bf16[49,768]{1,0:T(8,128)(2,1)} %conv.1, ...), custom_call_target="tpu_custom_call" | custom-call | tf_op jit(solution)/shard_map/gather_weights/pallas_call | solution.py:700
  27.2 20.3 %attention_forward.1 = (bf16[4,208,384]{2,1,0:T(8,128)(2,1)}, bf16[4,256,1152]{2,1,0:T(8,128)(2,1)}, f32[4,6,208,256]{3,2,1,0:T(8,128)}, bf16[4,6,208,256]{3,2,1...) custom-call(f32[6,6]{1,0:T(8,128)} %pre.3, f32[6,6]{1,0:T(8,128)} %post.3, ...), custom_call_target="tpu_custom_call" | custom-call | tf_op jit(solution)/shard_map/attention_forward/pallas_call | solution.py:374
  47.5 0.0 copy-done
  47.5 0.9 copy.40.cot
  48.5 27.9 %mlp.1 = (bf16[4,197,384]{2,1,0:T(8,128)(2,1)}, f32[4,208,384]{2,1,0:T(8,128)}, f32[384,1536]{1,0:T(8,128)}, f32[64,1536]{1,0:T(8,128)}, f32[1536,384]{1,0:T(8,128)}, /*index=5*/f32[1,384]{1,0:T(1,128)}) custom-call(bf16[4,208,384]{2,1,0:T(8,128)(2,1)} %get-tuple-element.56.n2, bf16[4,197,384]{2,1,0:T(8,128)(2,1)} %copy.40.cot, ...), custom_call_target="tpu_custom_call" | custom-call | tf_op jit(solution)/shard_map/mlp/pallas_call | solution.py:421
  76.4 2.1 %copy.43 = bf16[4,197,384]{2,0,1:T(4,128)(2,1)} copy(bf16[4,197,384]{2,1,0:T(8,128)(2,1)} %get-tuple-element.92) | data formatting | bytes 1210368
  78.5 24.6 %attention_backward.1 = (f32[4,197,384]{2,1,0:T(8,128)}, f32[384,1152]{1,0:T(8,128)}, f32[384,384]{1,0:T(8,128)}, f32[32,128]{1,0:T(8,128)}) custom-call(f32[6,6]{1,0:T(8,128)} %pre.3, f32[6,6]{1,0:T(8,128)} %post.3, bf16[4,197,384]{2,1,0:T(8,128)(2,1)} %copy.39.tok, bf16[4,197,384]{2,1,0:T(8,128)(2,1)} %copy.40.cot, ...), custom_call_target="tpu_custom_call" | custom-call | tf_op jit(solution)/shard_map/attention_backward/pallas_call | solution.py:463
  103.1 2.6 %copy.44 = f32[4,197,384]{2,0,1:T(4,128)} copy(f32[4,197,384]{2,1,0:T(8,128)} %get-tuple-element.93) | data formatting | bytes 2420736
  105.7 50.3 %reduce_mlp.1.total = bf16[2,2,2,2,320,128]{5,4,3,2,1,0:T(8,128)(2,1)} custom-call(f32[384,1536]{1,0:T(8,128)} %get-tuple-element.70.gfc1, f32[64,1536]{1,0:T(8,128)} %get-tuple-element.71.gconv, f32[1536,384]{1,0:T(8,128)} %get-tuple-element.72.gfc2), custom_call_target="tpu_custom_call" | custom-call | tf_op jit(solution)/shard_map/reduce_mlp/pallas_call | solution.py:780
  156.0 20.6 %reduce_attention.1 = (bf16[144,128]{1,0:T(8,128)(2,1)}, f32[32,128]{1,0:T(8,128)}) custom-call(f32[384,1152]{1,0:T(8,128)} %get-tuple-element.73.gqkv, f32[384,384]{1,0:T(8,128)} %get-tuple-element.74.gproj, f32[32,128]{1,0:T(8,128)} %get-tuple-element.75.small), custom_call_target="tpu_custom_call" | custom-call | tf_op jit(solution)/shard_map/reduce_attention/pallas_call | solution.py:855
  176.6 2.9 %finish.1 = (f32[384,768]{1,0:T(8,128)}, f32[768]{0:T(1024)}, f32[49,768]{1,0:T(8,128)}, f32[768,384]{1,0:T(8,128)}, f32[24,576]{1,0:T(8,128)}, /*index=5*/f32[2...) custom-call(bf16[2,2,2,2,320,128]{5,4,3,2,1,0:T(8,128)(2,1)} %reduce, ...), custom_call_target="tpu_custom_call" | custom-call | tf_op jit(solution)/shard_map/finish/pallas_call | solution.py:908
Async XLA Ops:
  2.6 44.9 %copy-start = (bf16[4,197,384]{2,0,1:T(4,128)(2,1)S(1)}, bf16[4,197,384]{2,0,1:T(4,128)(2,1)}, u32[]{:S(2)}) copy-start(bf16[4,197,384]{2,0,1:T(4,128)(2,1)} %param.38) | copy-start | bytes 1815556

commit v3 on v1

--- a/solution.py
+++ b/solution.py
@@ -15,13 +15,16 @@
 POINTS = 17
 SEQ = 197
 ROWS = 208
+TAPS = 64
 KEYS = 256
 WIDTH = 384
 HALF = 152
 COEFS = 2 * HALF
 CLASS_ROW = 145
-CHUNK = 256
-VMEM = 60 * 1024 * 1024
+CHUNK = 512
+STREAM = 256
+SMALL = 32
+VMEM = 62 * 1024 * 1024
 
 f32 = jnp.float32
 bf16 = jnp.bfloat16
@@ -52,12 +55,12 @@
     inverse[HALF : HALF + count, 1:SEQ] = -weight * np.sin(angle)
     inverse[CLASS_ROW, 0] = 1.0
     turn = unit * freq @ taps.T
-    kernel = np.zeros((COEFS, KS * KS))
-    kernel[:count] = np.cos(turn)
-    kernel[HALF : HALF + count] = np.sin(turn)
-    back = np.zeros((COEFS, KS * KS))
-    back[:count] = weight * np.cos(turn)
-    back[HALF : HALF + count] = -weight * np.sin(turn)
+    kernel = np.zeros((COEFS, TAPS))
+    kernel[:count, : KS * KS] = np.cos(turn)
+    kernel[HALF : HALF + count, : KS * KS] = np.sin(turn)
+    back = np.zeros((COEFS, TAPS))
+    back[:count, : KS * KS] = weight * np.cos(turn)
+    back[HALF : HALF + count, : KS * KS] = -weight * np.sin(turn)
     one = np.zeros((COEFS, 1))
     one[CLASS_ROW] = 1.0
     return forward, inverse.T, kernel, back.T, one
@@ -92,6 +95,10 @@
     moment = jnp.mean(scaled * centred, axis=-1, keepdims=True)
     back = r * (scaled - jnp.mean(scaled, axis=-1, keepdims=True) - centred * (r * r * moment))
     return back, grad * (centred * r)
+
+
+def row(ref):
+    return ref[...].reshape(1, ref.shape[0])
 
 
 def add_rows(values):
@@ -111,7 +118,7 @@
     inputs = pad[...]
     centred, r = centre(inputs)
     inside = row_mask((ROWS, WIDTH))
-    n1 = jnp.where(inside, centred * r * gain1[...] + bias1[...], 0.0).astype(bf16)
+    n1 = jnp.where(inside, centred * r * row(gain1) + row(bias1), 0.0).astype(bf16)
     n1_out[0] = n1
     packed = dot(n1, wqkv[...]).astype(bf16)
     packed_out[0, :ROWS] = packed
@@ -155,10 +162,10 @@
         )
     attended = jnp.concatenate(pieces, axis=1).astype(bf16)
     att_out[0] = attended
-    middle = inputs + (dot(attended, wproj[...]) + pbias[...])
+    middle = inputs + (dot(attended, wproj[...]) + row(pbias))
     mid_out[0] = middle
     centred, r = centre(middle)
-    n2_out[0] = jnp.where(inside, centred * r * gain2[...] + bias2[...], 0.0).astype(bf16)
+    n2_out[0] = jnp.where(inside, centred * r * row(gain2) + row(bias2), 0.0).astype(bf16)
 
 
 def gelu_parts(hidden):
@@ -175,8 +182,8 @@
 
 
 def mlp(
-    n2, cot, mid, fc1, fc1b, conv, fc2, fc2b, fwd, inv, kh, kl, bh, bl, one,
-    block_out, gn2_out, gfc1_out, gb1_out, gconv_out, gfc2_out, gb2_out,
+    n2, cot, mid, fc1, conv, fc2, fc2b, fwd, inv, kh, kl, bh, bl, one,
+    block_out, gn2_out, gfc1_out, gconv_out, gfc2_out, gb2_out,
     cot_pad, pad, hid, grad, out_acc, conv_low, ghid_low,
 ):
     step = pl.program_id(0)
@@ -199,7 +206,7 @@
     turned = dot(kh[...], taps) + dot(kl[...], taps) + one[...]
     kr, ki = turned[:HALF], turned[HALF:]
     rows_all = n2[...].reshape(images * ROWS, WIDTH)
-    hid[...] = dot(rows_all, w1) + fc1b[...].astype(f32)
+    hid[...] = dot(rows_all, w1) + taps.astype(f32)[KS * KS : KS * KS + 1]
     grad[...] = dot_t(cot_pad[...], w2)
     cross_r = jnp.zeros((HALF, CHUNK), f32)
     cross_i = jnp.zeros((HALF, CHUNK), f32)
@@ -219,11 +226,11 @@
         ghid = (dot(inv[...], back) * slope).astype(bf16)
         bias_sum = bias_sum + add_rows(ghid.astype(f32))
         ghid_low[span, :] = ghid
-    gb1_out[...] = bias_sum
     cross = jnp.concatenate([cross_r, cross_i], axis=0)
     high = cross.astype(bf16)
     low = (cross - high.astype(f32)).astype(bf16)
     gconv_out[...] = dot(bh[...], high) + dot(bl[...], high) + dot(bh[...], low)
+    gconv_out[KS * KS : KS * KS + 1] = bias_sum
     convolved = conv_low[...]
     ghid_all = ghid_low[...]
     part = dot(convolved, w2).reshape(images, ROWS, WIDTH)
@@ -244,14 +251,14 @@
     @pl.when(step == pl.num_programs(0) - 1)
     def _():
         for b in range(images):
-            result = mid[b] + (out_acc[b] + fc2b[...])
+            result = mid[b] + (out_acc[b] + row(fc2b))
             block_out[b] = result[:SEQ].astype(bf16)
 
 
 def attention_backward(
-    pre, post, tok, cot, n1, packed, probs, attn, att, mid, gn2, wqkv, wproj, gain1, gain2,
-    gtok_out, gqkv_out, gproj_out, rows_out, mix_out,
-    pad, score, weight, low, mix,
+    pre, post, tok, cot, n1, packed, probs, attn, att, mid, gn2, wqkv, wproj, gain1, gain2, gb2,
+    gtok_out, gqkv_out, gproj_out, small_out,
+    pad, score, weight, low, mix, rows_out, square,
 ):
     step = pl.program_id(0)
 
@@ -266,7 +273,7 @@
     pad[:SEQ] = cot[0].astype(f32)
     centred, r = centre(mid[0])
     grad = gn2[0]
-    back, gain_rows = norm_back(centred, r, gain2[...], grad)
+    back, gain_rows = norm_back(centred, r, row(gain2), grad)
     rows_out[3:4] += add_rows(gain_rows)
     rows_out[4:5] += add_rows(grad)
     gmid = pad[...] + back
@@ -333,14 +340,20 @@
     gnormed = dot_t(gpacked, wqkv[...])
     pad[:SEQ] = tok[0].astype(f32)
     centred, r = centre(pad[...])
-    back, gain_rows = norm_back(centred, r, gain1[...], gnormed)
+    back, gain_rows = norm_back(centred, r, row(gain1), gnormed)
     rows_out[0:1] += add_rows(gain_rows)
     rows_out[1:2] += add_rows(gnormed)
     gtok_out[0] = (gmid + back)[:SEQ]
 
     @pl.when(step == pl.num_programs(0) - 1)
     def _():
-        mix_out[...] = jnp.sum(mix[...], axis=1)
+        rows_out[5:6] = gb2[...]
+        for t in range(WIDTH // 128):
+            small_out[8 * t : 8 * t + 8] = rows_out[:, 128 * t : 128 * t + 128]
+        square[...] = jnp.zeros_like(square)
+        square[: 2 * HEADS * HEADS] = jnp.sum(mix[...], axis=1)
+        sums = add_rows(square[...].T)
+        small_out[24:] = jnp.concatenate([sums, jnp.zeros((SMALL - 25, 128), f32)], axis=0)
 
 
 def whole(shape):
@@ -358,13 +371,13 @@
 def call_forward(tokens, wqkv, wproj, pre, post, gain1, bias1, pbias, gain2, bias2):
     images = tokens.shape[0]
     smem = pl.BlockSpec(memory_space=pltpu.SMEM)
-    row = whole((1, WIDTH))
+    vector = whole((WIDTH,))
     return pl.pallas_call(
         attention_forward,
         grid=(images,),
         in_specs=[
             smem, smem, image((SEQ, WIDTH)), whole((WIDTH, 3 * WIDTH)), whole((WIDTH, WIDTH)),
-            row, row, row, row, row,
+            vector, vector, vector, vector, vector,
         ],
         out_specs=[
             image((ROWS, WIDTH)), image((KEYS, 3 * WIDTH)), image((HEADS, ROWS, KEYS)),
@@ -390,7 +403,7 @@
     )(pre, post, tokens, wqkv, wproj, gain1, bias1, pbias, gain2, bias2)
 
 
-def call_mlp(n2, cotangent, middle, fc1, fc1_bias, conv, fc2, fc2_bias):
+def call_mlp(n2, cotangent, middle, fc1, conv, fc2, fc2_bias):
     images = n2.shape[0]
     units = fc1.shape[1]
     steps = units // CHUNK
@@ -405,28 +418,26 @@
         jnp.asarray(one.astype(np.float32)),
     ]
     columns = lambda rows: pl.BlockSpec((rows, CHUNK), lambda i: (0, i))
-    taps = KS * KS
     total = images * ROWS
     return pl.pallas_call(
         mlp,
         grid=(steps,),
         in_specs=[
             whole((images, ROWS, WIDTH)), whole((images, SEQ, WIDTH)), whole((images, ROWS, WIDTH)),
-            columns(WIDTH), columns(1), columns(taps),
-            pl.BlockSpec((CHUNK, WIDTH), lambda i: (i, 0)), whole((1, WIDTH)),
+            columns(WIDTH), columns(TAPS),
+            pl.BlockSpec((CHUNK, WIDTH), lambda i: (i, 0)), whole((WIDTH,)),
         ]
         + [whole(c.shape) for c in consts],
         out_specs=[
             whole((images, SEQ, WIDTH)), whole((images, ROWS, WIDTH)),
-            columns(WIDTH), columns(1), columns(taps),
+            columns(WIDTH), columns(TAPS),
             pl.BlockSpec((CHUNK, WIDTH), lambda i: (i, 0)), whole((1, WIDTH)),
         ],
         out_shape=[
             jax.ShapeDtypeStruct((images, SEQ, WIDTH), bf16),
             jax.ShapeDtypeStruct((images, ROWS, WIDTH), f32),
             jax.ShapeDtypeStruct((WIDTH, units), f32),
-            jax.ShapeDtypeStruct((1, units), f32),
-            jax.ShapeDtypeStruct((taps, units), f32),
+            jax.ShapeDtypeStruct((TAPS, units), f32),
             jax.ShapeDtypeStruct((units, WIDTH), f32),
             jax.ShapeDtypeStruct((1, WIDTH), f32),
         ],
@@ -441,15 +452,15 @@
         ],
         compiler_params=params(),
         name="mlp",
-    )(n2, cotangent, middle, fc1, fc1_bias, conv, fc2, fc2_bias, *consts)
+    )(n2, cotangent, middle, fc1, conv, fc2, fc2_bias, *consts)
 
 
 def call_backward(
-    tokens, cotangent, n1, packed, probs, attn, att, mid, gn2, wqkv, wproj, pre, post, gain1, gain2
+    tokens, cotangent, n1, packed, probs, attn, att, mid, gn2, wqkv, wproj, pre, post, gain1, gain2, gb2
 ):
     images = tokens.shape[0]
     smem = pl.BlockSpec(memory_space=pltpu.SMEM)
-    row = whole((1, WIDTH))
+    vector = whole((WIDTH,))
     return pl.pallas_call(
         attention_backward,
         grid=(images,),
@@ -457,18 +468,18 @@
             smem, smem, image((SEQ, WIDTH)), image((SEQ, WIDTH)), image((ROWS, WIDTH)),
             image((KEYS, 3 * WIDTH)), image((HEADS, ROWS, KEYS)), image((HEADS, ROWS, KEYS)),
             image((ROWS, WIDTH)), image((ROWS, WIDTH)), image((ROWS, WIDTH)),
-            whole((WIDTH, 3 * WIDTH)), whole((WIDTH, WIDTH)), row, row,
+            whole((WIDTH, 3 * WIDTH)), whole((WIDTH, WIDTH)), vector, vector,
+            whole((1, WIDTH)),
         ],
         out_specs=[
             image((SEQ, WIDTH)), whole((WIDTH, 3 * WIDTH)), whole((WIDTH, WIDTH)),
-            whole((8, WIDTH)), whole((2 * HEADS * HEADS, 128)),
+            whole((SMALL, 128)),
         ],
         out_shape=[
             jax.ShapeDtypeStruct((images, SEQ, WIDTH), f32),
             jax.ShapeDtypeStruct((WIDTH, 3 * WIDTH), f32),
             jax.ShapeDtypeStruct((WIDTH, WIDTH), f32),
-            jax.ShapeDtypeStruct((8, WIDTH), f32),
-            jax.ShapeDtypeStruct((2 * HEADS * HEADS, 128), f32),
+            jax.ShapeDtypeStruct((SMALL, 128), f32),
         ],
         scratch_shapes=[
             pltpu.VMEM((ROWS, WIDTH), f32),
@@ -476,66 +487,826 @@
             pltpu.VMEM((HEADS, ROWS, KEYS), f32),
             pltpu.VMEM((HEADS, ROWS, KEYS), bf16),
             pltpu.VMEM((2 * HEADS * HEADS, 8, 128), f32),
+            pltpu.VMEM((8, WIDTH), f32),
+            pltpu.VMEM((128, 128), f32),
         ],
         compiler_params=params(),
         name="attention_backward",
     )(
         pre, post, tokens, cotangent, n1, packed, probs, attn, att, mid, gn2, wqkv, wproj,
-        gain1, gain2,
+        gain1, gain2, gb2,
     )
 
 
 def local_block(
     tokens, norm1_gain, norm1_bias, wqkv, mix_pre, mix_post, wproj, proj_bias, norm2_gain,
-    norm2_bias, fc1, fc1_bias, conv, fc2, fc2_bias, cotangent,
+    norm2_bias, fc1, taps, fc2, fc2_bias, cotangent,
 ):
-    row = lambda v: v.reshape(1, -1)
-    gain1, gain2 = row(norm1_gain), row(norm2_gain)
     n1, packed, probs, attn, att, mid, n2 = call_forward(
-        tokens, wqkv, wproj, mix_pre, mix_post, gain1, row(norm1_bias), row(proj_bias), gain2,
-        row(norm2_bias),
-    )
-    block_out, gn2, gfc1, gb1, gconv, gfc2, gb2 = call_mlp(
-        n2, cotangent, mid, fc1, row(fc1_bias), conv, fc2, row(fc2_bias)
-    )
-    gtok, gqkv, gproj, rows, mix = call_backward(
+        tokens, wqkv, wproj, mix_pre, mix_post, norm1_gain, norm1_bias, proj_bias, norm2_gain,
+        norm2_bias,
+    )
+    block_out, gn2, gfc1, gconv, gfc2, gb2 = call_mlp(n2, cotangent, mid, fc1, taps, fc2, fc2_bias)
+    gtok, gqkv, gproj, small = call_backward(
         tokens, cotangent, n1, packed, probs, attn, att, mid, gn2, wqkv, wproj, mix_pre, mix_post,
-        gain1, gain2,
-    )
-    return block_out, gtok, gqkv, gproj, gfc1, gb1, gconv, gfc2, gb2, rows, mix
-
-
-def shards(
+        norm1_gain, norm2_gain, gb2,
+    )
+    return block_out, gtok, gqkv, gproj, gfc1, gconv, gfc2, small
+
+
+SIDES = (8, 4, 2, 1)
+ORDERS = ((3, 2, 1, 0), (2, 1, 0, 3), (1, 0, 3, 2))
+MESH_IDS = pl.DeviceIdType.MESH
+PIECE = 144
+PIECE_PARTS = ((0, 48), (48, 48), (96, 48))
+BLOCK = 112
+BLOCK_PARTS = ((0, 48), (48, 32), (80, 32))
+STREAMS = 3
+
+
+def place():
+    dp, core = lax.axis_index("dp"), lax.axis_index("tensor")
+    bits = [lax.rem(dp // stride, 2) for stride in SIDES]
+    partners = [(dp + (1 - 2 * bit) * stride, core) for bit, stride in zip(bits, SIDES)]
+    return bits, partners, (dp, 1 - core), core
+
+
+def meet(partners):
+    barrier = pltpu.get_barrier_semaphore()
+    for partner in partners:
+        pl.semaphore_signal(barrier, inc=1, device_id=partner, device_id_type=MESH_IDS)
+    pl.semaphore_wait(barrier, len(partners))
+
+
+def remote(src, dst, sems, index, device):
+    return pltpu.make_async_remote_copy(
+        src_ref=src, dst_ref=dst, send_sem=sems.at[(0,) + index], recv_sem=sems.at[(1,) + index],
+        device_id=device, device_id_type=MESH_IDS,
+    )
+
+
+def region(fixed, rows):
+    return tuple(fixed.get(axis, slice(None)) for axis in range(4)) + (rows,)
+
+
+def combos(count):
+    return [tuple((i >> (count - 1 - j)) & 1 for j in range(count)) for i in range(2**count)]
+
+
+def index_of(d):
+    return tuple((d // stride) % 2 for stride in SIDES)
+
+
+class Halving:
+    def __init__(self, acc, landing, sems, parts, turn, bits, partners):
+        self.acc, self.landing, self.sems = acc, landing, sems
+        self.parts, self.turn, self.bits, self.partners = parts, turn, bits, partners
+
+    def copy(self, part, step):
+        order, rows = ORDERS[(part + self.turn) % 3], pl.ds(*self.parts[part])
+        axis = order[step]
+        fixed = {a: self.bits[a] for a in order[:step]}
+        fixed[axis] = 1 - self.bits[axis]
+        dst = self.landing[step].at[(slice(None),) * (3 - step) + (rows,)]
+        return remote(
+            self.acc.at[region(fixed, rows)], dst, self.sems, (part, step), self.partners[axis]
+        )
+
+    def start(self, step):
+        for part in range(3):
+            self.copy(part, step).start()
+
+    def act(self, step):
+        for part in range(3):
+            order, rows = ORDERS[(part + self.turn) % 3], pl.ds(*self.parts[part])
+            self.copy(part, step).wait_recv()
+            fixed = {a: self.bits[a] for a in order[: step + 1]}
+            free = [a for a in range(4) if a not in fixed]
+            for combo in combos(len(free)):
+                where = region({**fixed, **dict(zip(free, combo))}, rows)
+                came = self.landing[step][combo + (rows,)]
+                self.acc[where] = (self.acc[where].astype(f32) + came.astype(f32)).astype(bf16)
+            if step < 3:
+                self.copy(part, step + 1).start()
+
+    def finish(self):
+        for step in range(4):
+            for part in range(3):
+                self.copy(part, step).wait_send()
+
+
+class Doubling:
+    def __init__(self, full, sems, parts, turn, bits, partners):
+        self.full, self.sems = full, sems
+        self.parts, self.turn, self.bits, self.partners = parts, turn, bits, partners
+
+    def come(self, part, step):
+        order, rows = ORDERS[(part + self.turn) % 3][::-1], pl.ds(*self.parts[part])
+        fixed = {a: self.bits[a] for a in order[step + 1 :]}
+        fixed[order[step]] = 1 - self.bits[order[step]]
+        return region(fixed, rows)
+
+    def copy(self, part, step):
+        order, rows = ORDERS[(part + self.turn) % 3][::-1], pl.ds(*self.parts[part])
+        held = region({a: self.bits[a] for a in order[step:]}, rows)
+        return remote(
+            self.full.at[held], self.full.at[held], self.sems, (part, step),
+            self.partners[order[step]],
+        )
+
+    def start(self):
+        for part in range(3):
+            self.copy(part, 0).start()
+
+    def act(self, step, then=None):
+        for part in range(3):
+            self.copy(part, step).wait_recv()
+            if step < 3:
+                self.copy(part, step + 1).start()
+            if then is not None:
+                then(part, step)
+
+    def finish(self):
+        for step in range(4):
+            for part in range(3):
+                self.copy(part, step).wait_send()
+
+
+def tiles(values):
+    return jnp.concatenate(
+        [values[:, 128 * t : 128 * t + 128] for t in range(values.shape[1] // 128)], axis=0
+    )
+
+
+def untiles(values, count):
+    rows = values.shape[0] // count
+    return jnp.concatenate([values[t * rows : (t + 1) * rows] for t in range(count)], axis=1)
+
+
+def block_kernel(
+    pre, post, tok, cot, gain1, bias1, pbias, gain2, bias2, fc2b,
+    qkv, proj, fc1, conv, bias, fc2, fwd, inv, kh, kl, bh, bl, one,
+    block_out, gtok_out, *rest,
+):
+    fulls, (piece_out, small_out), rest = rest[:STREAMS], rest[STREAMS : STREAMS + 2], rest[STREAMS + 2 :]
+    (
+        piece_full, piece_other, taps_pad, wqkv, wproj, fc1_full, fc2_full, conv_full,
+        inputs, cot_pad, n1, packed, score, probs, attn, att, mid, n2,
+        turned, ghat, hid, conv_low, ghid_low, gmid, gmid_low, gatt, low, gpacked, mix,
+        rows_out, square, gqkv, gproj, small_sums, small_landed,
+        streams_out, streams_came, streams_acc, streams_landing, gconv, att_bufs,
+        local_sems, gather_sems, gather_pair_sems, stream_pair_sems, stream_sems, att_sems, att_pair_sems,
+    ) = rest
+    images = tok.shape[0]
+    total = images * ROWS
+    half = fc1.shape[1]
+    bits, partners, pair, core = place()
+    mine = tuple(bits)
+    mine_start = pl.multiple_of(core * half, 128)
+    other_start = pl.multiple_of((1 - core) * half, 128)
+    cols, rows_of = pl.ds(mine_start, half), pl.ds(mine_start, half)
+    span = lambda b: slice(b * ROWS, (b + 1) * ROWS)
+    spans = [span(b) for b in range(images)]
+    inside = row_mask((ROWS, WIDTH))
+
+    both = jnp.concatenate([qkv[...].astype(f32), proj[...].astype(f32)], axis=1)
+    piece_full[mine] = tiles(both).astype(bf16)
+    taps_pad[...] = jnp.zeros(taps_pad.shape, f32)
+    taps_pad[: KS * KS] = conv[...].astype(f32)
+    taps_pad[KS * KS : KS * KS + 1] = bias[...].astype(f32).reshape(1, half)
+    conv_full[:, cols] = taps_pad[...].astype(bf16)
+    meet(partners + [pair])
+    gather = Doubling(piece_full, gather_sems, PIECE_PARTS, 0, bits, partners)
+    gather.start()
+    weights_come = [
+        remote(conv_full.at[:, cols], conv_full.at[:, cols], gather_pair_sems, (0,), pair),
+        remote(fc2, fc2_full.at[rows_of], gather_pair_sems, (1,), pair),
+        remote(fc1, fc1_full.at[:, cols], gather_pair_sems, (2,), pair),
+    ]
+    forwards = [
+        remote(piece_full.at[mine], piece_other.at[mine], gather_pair_sems, (3,), pair)
+    ]
+    local = [
+        pltpu.make_async_copy(fc2, fc2_full.at[rows_of], local_sems.at[0]),
+        pltpu.make_async_copy(fc1, fc1_full.at[:, cols], local_sems.at[1]),
+    ]
+    for copy in weights_come + forwards + local:
+        copy.start()
+
+    def forward(part, step):
+        where = gather.come(part, step)
+        copy = remote(
+            piece_full.at[where], piece_other.at[where], gather_pair_sems,
+            (4 + 3 * step + part,), pair,
+        )
+        copy.start()
+        forwards.append(copy)
+
+    cot_sum = jnp.zeros((1, WIDTH), f32)
+    for b in range(images):
+        for source, ref in ((tok, inputs), (cot, gmid)):
+            ref[b * ROWS + SEQ - 5 : (b + 1) * ROWS] = jnp.zeros((ROWS - SEQ + 5, WIDTH), f32)
+            ref[b * ROWS : b * ROWS + SEQ] = source[b].astype(f32)
+        grads = gmid[spans[b], :]
+        cot_sum = cot_sum + add_rows(grads)
+        cot_pad[spans[b], :] = grads.astype(bf16)
+    gather.act(0, forward)
+    for b in range(images):
+        centred, r = centre(inputs[spans[b], :])
+        n1[spans[b], :] = jnp.where(inside, centred * r * row(gain1) + row(bias1), 0.0).astype(bf16)
+
+    def prepare(start):
+        units = pl.ds(start, half)
+        taps = conv_full[:, units]
+        turned[:, units] = dot(kh[...], taps) + dot(kl[...], taps) + one[...]
+        hid[...] = dot_t(cot_pad[...], fc2_full[units, :])
+        for b in range(images):
+            ghat[b, :, units] = dot(fwd[...], hid[spans[b], :].astype(bf16))
+
+    gather.act(1, forward)
+    for copy in local:
+        copy.wait()
+    prepare(mine_start)
+    gather.act(2, forward)
+    for copy in weights_come:
+        copy.wait_recv()
+    prepare(other_start)
+    gather.act(3, forward)
+    for copy in forwards:
+        copy.wait_recv()
+    width = qkv.shape[1]
+    flip = core == 1
+    for d in range(0, 16, 2):
+        blocks = [
+            jnp.concatenate([untiles(ref[index_of(e)].astype(f32), 6) for e in (d, d + 1)], axis=0)
+            for ref in (piece_full, piece_other)
+        ]
+        first = jnp.where(flip, blocks[1], blocks[0])
+        second = jnp.where(flip, blocks[0], blocks[1])
+        rows = slice(24 * d, 24 * d + 48)
+        wqkv[rows, :] = jnp.concatenate([first[:, :width], second[:, :width]], axis=1).astype(bf16)
+        wproj[rows, :] = jnp.concatenate([first[:, width:], second[:, width:]], axis=1).astype(bf16)
+
+    for n in range(0, 3 * WIDTH, WIDTH):
+        gpacked[:, n : n + WIDTH] = dot(n1[...], wqkv[:, n : n + WIDTH]).astype(bf16)
+    for b in range(images):
+        packed[b, :ROWS] = gpacked[spans[b], :]
+        packed[b, ROWS:] = jnp.zeros((KEYS - ROWS, 3 * WIDTH), bf16)
+    low_half = lax.broadcasted_iota(jnp.int32, (ROWS, 128), 1) < HEAD_DIM
+    key_half = lax.broadcasted_iota(jnp.int32, (KEYS, 128), 1) < HEAD_DIM
+    zero = jnp.zeros((ROWS, 128), bf16)
+    valid = lax.broadcasted_iota(jnp.int32, (16, KEYS), 1) < SEQ
+
+    def section(b, which, pair_of_heads, count=KEYS):
+        start = which * WIDTH + 128 * pair_of_heads
+        return packed[b, :count, start : start + 128]
+
+    def find_scores(b):
+        for p in range(HEADS // 2):
+            query, key = section(b, 0, p, ROWS), section(b, 1, p)
+            score[2 * p] = dot_t(jnp.where(low_half, query, zero), key)
+            score[2 * p + 1] = dot_t(jnp.where(low_half, zero, query), key)
+
+    def attend(b, carry):
+        find_scores(b)
+
+        def rows_step(step, carry):
+            rows = pl.ds(pl.multiple_of(step * 16, 16), 16)
+            scores = [score[h, rows, :] for h in range(HEADS)]
+            found = []
+            for g in range(HEADS):
+                mixed = scores[0] * (pre[g, 0] * 0.125)
+                for h in range(1, HEADS):
+                    mixed = mixed + scores[h] * (pre[g, h] * 0.125)
+                mixed = jnp.where(valid, mixed, -1e30)
+                top = jnp.max(mixed, axis=-1, keepdims=True)
+                raised = jnp.exp(mixed - top)
+                prob = raised * (1.0 / jnp.sum(raised, axis=-1, keepdims=True))
+                probs[b, g, rows, :] = prob
+                found.append(prob)
+            for g in range(HEADS):
+                mixed = found[0] * post[g, 0]
+                for h in range(1, HEADS):
+                    mixed = mixed + found[h] * post[g, h]
+                attn[b, g, rows, :] = mixed.astype(bf16)
+            return carry
+
+        lax.fori_loop(0, ROWS // 16, rows_step, 0, unroll=ROWS // 16)
+        pieces = []
+        for p in range(HEADS // 2):
+            value = section(b, 2, p)
+            pieces.append(
+                jnp.where(low_half, dot(attn[b, 2 * p], value), dot(attn[b, 2 * p + 1], value))
+            )
+        rows = pl.ds(pl.multiple_of(b * ROWS, 16), ROWS)
+        att[rows, :] = jnp.concatenate(pieces, axis=1).astype(bf16)
+        return carry
+
+    lax.fori_loop(0, images, attend, 0)
+    branch = dot(att[...], wproj[...])
+    for b in range(images):
+        middle = inputs[spans[b], :] + (branch[spans[b]] + row(pbias))
+        mid[spans[b], :] = middle
+        centred, r = centre(middle)
+        n2[spans[b], :] = jnp.where(inside, centred * r * row(gain2) + row(bias2), 0.0).astype(bf16)
+
+    def exchange_copy(s):
+        return remote(streams_out.at[s], streams_came.at[s], stream_pair_sems, (s,), pair)
+
+    halvings = [
+        Halving(
+            streams_acc.at[s], [ref.at[s] for ref in streams_landing], stream_sems.at[s, 0],
+            BLOCK_PARTS, s, bits, partners,
+        )
+        for s in range(STREAMS)
+    ]
+    doublings = [
+        Doubling(fulls[s], stream_sems.at[s, 1], BLOCK_PARTS, s, bits, partners)
+        for s in range(STREAMS)
+    ]
+
+    def act(s, step):
+        if step < 0:
+            halvings[s].start(0)
+        elif step < 4:
+            halvings[s].act(step)
+            if step == 3:
+                fulls[s][mine] = streams_acc[(s,) + mine]
+                doublings[s].start()
+        else:
+            doublings[s].act(step - 4)
+
+    def blocks():
+        filters = tiles(gconv[...])
+        empty = jnp.zeros((BLOCK - 104, 128), f32)
+        for d in range(16):
+            yield index_of(d), jnp.concatenate(
+                [
+                    tiles(gqkv[24 * d : 24 * d + 24, :STREAM]),
+                    tiles(hid[16 * d : 16 * d + 16, :WIDTH]),
+                    filters[8 * d : 8 * d + 8],
+                    empty,
+                ],
+                axis=0,
+            )
+
+    def mlp(i, carry):
+        units = pl.ds(
+            pl.multiple_of(lax.rem((1 - core) * STREAMS + i, 2 * STREAMS) * STREAM, STREAM), STREAM
+        )
+        bias_row = conv_full[:, units].astype(f32)[KS * KS : KS * KS + 1]
+        hid[:, :STREAM] = dot(n2[...], fc1_full[:, units]) + bias_row
+        kr, ki = turned[:HALF, units], turned[HALF:, units]
+        cross_r = jnp.zeros((HALF, STREAM), f32)
+        cross_i = jnp.zeros((HALF, STREAM), f32)
+        bias_sum = jnp.zeros((1, STREAM), f32)
+        for b in range(images):
+            activated, slope = gelu_parts(hid[spans[b], :STREAM])
+            hid[spans[b], :STREAM] = slope
+            x = dot(fwd[...], activated.astype(bf16))
+            xr, xi = x[:HALF], x[HALF:]
+            yr, yi = ghat[b, :HALF, units], ghat[b, HALF:, units]
+            ahead = jnp.concatenate([xr * kr - xi * ki, xr * ki + xi * kr], axis=0).astype(bf16)
+            back = jnp.concatenate([yr * kr + yi * ki, yi * kr - yr * ki], axis=0).astype(bf16)
+            cross_r = cross_r + (xr * yr + xi * yi)
+            cross_i = cross_i + (xi * yr - xr * yi)
+            conv_low[spans[b], units] = dot(inv[...], ahead).astype(bf16)
+            ghid = (dot(inv[...], back) * hid[spans[b], :STREAM]).astype(bf16)
+            bias_sum = bias_sum + add_rows(ghid.astype(f32))
+            ghid_low[spans[b], units] = ghid
+        cross = jnp.concatenate([cross_r, cross_i], axis=0)
+        high = cross.astype(bf16)
+        low_part = (cross - high.astype(f32)).astype(bf16)
+        last = lax.broadcasted_iota(jnp.int32, (TAPS, STREAM), 0) == KS * KS
+        gconv[...] = jnp.where(
+            last, bias_sum, dot(bh[...], high) + dot(bl[...], high) + dot(bh[...], low_part)
+        )
+        hid[:STREAM, :WIDTH] = t_dot(conv_low[:, units], cot_pad[...])
+        gqkv[:, :STREAM] = t_dot(n2[...], ghid_low[:, units])
+
+        @pl.when(i < STREAMS)
+        def _():
+            for index, values in blocks():
+                streams_out[(i,) + index] = values.astype(bf16)
+            exchange_copy(i).start()
+
+        @pl.when(i >= STREAMS)
+        def _():
+            s = i - STREAMS
+            exchange_copy(s).wait_recv()
+            for index, values in blocks():
+                came = streams_came[(s,) + index].astype(f32)
+                streams_acc[(s,) + index] = (values + came).astype(bf16)
+
+        for turn, items in enumerate((((0, -1),), ((0, 0), (1, -1)), ((0, 1), (1, 0), (2, -1)))):
+
+            @pl.when(i == STREAMS + turn)
+            def _():
+                for item in items:
+                    act(*item)
+
+        return carry
+
+    lax.fori_loop(0, 2 * STREAMS, mlp, 0)
+    pending = [
+        (2, 0), (1, 1), (0, 2), (2, 1), (1, 2), (0, 3), (2, 2), (1, 3), (0, 4), (2, 3), (1, 4),
+        (0, 5), (2, 4), (1, 5), (0, 6), (2, 5), (1, 6), (0, 7), (2, 6), (1, 7), (2, 7),
+    ]
+
+    def poll(count=1):
+        for _ in range(count):
+            if pending:
+                act(*pending.pop(0))
+
+    hid[:, :WIDTH] = dot_t(ghid_low[...], fc1_full[...])
+    hid[:, WIDTH:] = dot(conv_low[...], fc2_full[...])
+    gain_sum = jnp.zeros((1, WIDTH), f32)
+    bias_sum = jnp.zeros((1, WIDTH), f32)
+    proj_sum = jnp.zeros((1, WIDTH), f32)
+    for b in range(images):
+        middle = mid[spans[b], :]
+        block_out[b] = (middle + (hid[spans[b], WIDTH:] + row(fc2b)))[:SEQ].astype(bf16)
+        centred, r = centre(middle)
+        grad = hid[spans[b], :WIDTH]
+        back, gain_rows = norm_back(centred, r, row(gain2), grad)
+        gain_sum = gain_sum + add_rows(gain_rows)
+        bias_sum = bias_sum + add_rows(grad)
+        whole_grad = gmid[spans[b], :] + back
+        gmid[spans[b], :] = whole_grad
+        rounded = whole_grad.astype(bf16)
+        proj_sum = proj_sum + add_rows(rounded.astype(f32))
+        gmid_low[spans[b], :] = rounded
+    poll()
+    gatt[...] = dot_t(gmid_low[...], wproj[...]).astype(bf16)
+    mix[...] = jnp.zeros_like(mix)
+
+    def fold(values):
+        values = values[:, :128] + values[:, 128:]
+        return values[:8] + values[8:]
+
+    places = 4
+    plan = [[pending.pop(0)] for _ in range(images * places) if pending]
+
+    def poll_at(b, spot):
+        for image_index in range(images):
+            index = image_index * places + spot
+            if index < len(plan):
+
+                @pl.when(b == image_index)
+                def _():
+                    for item in plan[index]:
+                        act(*item)
+
+    def put_weight(g, values):
+        ghat[1, :ROWS, KEYS * g : KEYS * (g + 1)] = values
+
+    def back_image(b, carry):
+        rows_of_image = pl.ds(pl.multiple_of(b * ROWS, 16), ROWS)
+        find_scores(b)
+        for p in range(HEADS // 2):
+            value = section(b, 2, p)
+            ahead = gatt[rows_of_image, 128 * p : 128 * p + 128]
+            put_weight(2 * p, dot_t(jnp.where(low_half, ahead, zero), value))
+            put_weight(2 * p + 1, dot_t(jnp.where(low_half, zero, ahead), value))
+        poll_at(b, 0)
+
+        def back_step(step, carry):
+            rows = pl.ds(pl.multiple_of(step * 16, 16), 16)
+            weights = [ghat[1, rows, KEYS * g : KEYS * (g + 1)] for g in range(HEADS)]
+            mixed = []
+            for h in range(HEADS):
+                prob = probs[b, h, rows, :]
+                ahead = weights[0] * post[0, h]
+                for g in range(1, HEADS):
+                    ahead = ahead + weights[g] * post[g, h]
+                for g in range(HEADS):
+                    mix[HEADS * HEADS + g * HEADS + h] += fold(weights[g] * prob)
+                inner = jnp.sum(prob * ahead, axis=-1, keepdims=True)
+                mixed.append(prob * (ahead - inner))
+            for h in range(HEADS):
+                scores = score[h, rows, :]
+                sums = mixed[0] * pre[0, h]
+                for g in range(1, HEADS):
+                    sums = sums + mixed[g] * pre[g, h]
+                low[h, rows, :] = sums.astype(bf16)
+                for g in range(HEADS):
+                    mix[g * HEADS + h] += fold(mixed[g] * scores)
+            return carry
+
+        lax.fori_loop(0, 7, back_step, 0, unroll=7)
+        poll_at(b, 1)
+        lax.fori_loop(7, ROWS // 16, back_step, 0, unroll=6)
+        poll_at(b, 2)
+        queries, keys, values = [], [], []
+        for p in range(HEADS // 2):
+            query, key = section(b, 0, p, ROWS), section(b, 1, p)
+            ahead = gatt[rows_of_image, 128 * p : 128 * p + 128]
+            even, odd = low[2 * p], low[2 * p + 1]
+            queries.append(jnp.where(low_half, dot(even, key), dot(odd, key)) * 0.125)
+            keys.append(jnp.where(key_half, t_dot(even, query), t_dot(odd, query))[:ROWS] * 0.125)
+            values.append(
+                jnp.where(
+                    key_half, t_dot(attn[b, 2 * p], ahead), t_dot(attn[b, 2 * p + 1], ahead)
+                )[:ROWS]
+            )
+        gpacked[rows_of_image, :] = jnp.concatenate(queries + keys + values, axis=1).astype(bf16)
+        poll_at(b, 3)
+        return carry
+
+    lax.fori_loop(0, images, back_image, 0)
+    gproj[...] = t_dot(att[...], gmid_low[...])
+    for n in range(0, 3 * WIDTH, WIDTH):
+        gqkv[:, n : n + WIDTH] = t_dot(n1[...], gpacked[:, n : n + WIDTH])
+    poll()
+
+    width, proj_width = gqkv.shape[1] // 2, gproj.shape[1] // 2
+
+    def pieces(side):
+        for d in range(16):
+            rows = slice(24 * d, 24 * d + 24)
+            both = jnp.concatenate(
+                [
+                    gqkv[rows, side * width : (side + 1) * width],
+                    gproj[rows, side * proj_width : (side + 1) * proj_width],
+                ],
+                axis=1,
+            )
+            yield index_of(d), tiles(both)
+
+    for side in range(2):
+
+        @pl.when(core == side)
+        def _():
+            for index, values in pieces(1 - side):
+                att_bufs["out"][index] = values.astype(bf16)
+
+    exchange = remote(att_bufs["out"], att_bufs["came"], att_pair_sems, (0,), pair)
+    exchange.start()
+    hid[:, :WIDTH] = dot_t(gpacked[...], wqkv[...])
+    norm_gain = jnp.zeros((1, WIDTH), f32)
+    norm_bias = jnp.zeros((1, WIDTH), f32)
+    attention = Halving(
+        att_bufs["acc"], att_bufs["landing"], att_sems, PIECE_PARTS, 0, bits, partners
+    )
+    for b in range(images):
+        centred, r = centre(inputs[spans[b], :])
+        grad = hid[spans[b], :WIDTH]
+        back, gain_rows = norm_back(centred, r, row(gain1), grad)
+        norm_gain = norm_gain + add_rows(gain_rows)
+        norm_bias = norm_bias + add_rows(grad)
+        gtok_out[b] = (gmid[spans[b], :] + back)[:SEQ]
+        if b == 1:
+            exchange.wait_recv()
+            for side in range(2):
+
+                @pl.when(core == side)
+                def _():
+                    for index, values in pieces(side):
+                        came = att_bufs["came"][index].astype(f32)
+                        att_bufs["acc"][index] = (values + came).astype(bf16)
+
+            attention.start(0)
+            poll()
+    rows_out[...] = jnp.concatenate(
+        [norm_gain, norm_bias, proj_sum, gain_sum, bias_sum, cot_sum, jnp.zeros((2, WIDTH), f32)],
+        axis=0,
+    )
+    for t in range(WIDTH // 128):
+        small_sums[0, 8 * t : 8 * t + 8] = rows_out[:, 128 * t : 128 * t + 128]
+    square[...] = jnp.zeros_like(square)
+    square[: 2 * HEADS * HEADS] = jnp.sum(mix[...], axis=1)
+    sums = add_rows(square[...].T)
+    small_sums[0, 24:] = jnp.concatenate([sums, jnp.zeros((SMALL - 25, 128), f32)], axis=0)
+
+    def small_copy(step):
+        device = pair if step == 0 else partners[4 - step]
+        return remote(
+            small_sums.at[step], small_landed.at[step], att_pair_sems, (1 + step,), device
+        )
+
+    small_copy(0).start()
+    for step in range(4):
+        small_copy(step).wait_recv()
+        small_sums[step + 1] = small_sums[step] + small_landed[step]
+        small_copy(step + 1).start()
+        attention.act(step)
+        poll(2)
+    poll(len(pending))
+    small_copy(4).wait_recv()
+    small_out[...] = small_sums[4] + small_landed[4]
+    piece_out[...] = att_bufs["acc"][mine]
+    for copy in weights_come + forwards + [exchange]:
+        copy.wait_send()
+    for s in range(STREAMS):
+        exchange_copy(s).wait_send()
+    for step in range(5):
+        small_copy(step).wait_send()
+    gather.finish()
+    attention.finish()
+    for s in range(STREAMS):
+        halvings[s].finish()
+        doublings[s].finish()
+
+
+def call_block(
+    pre, post, tok, cot, gain1, bias1, pbias, gain2, bias2, fc2b, qkv, proj, fc1, conv, bias, fc2
+):
+    images, half = tok.shape[0], fc1.shape[1]
+    units, total = 2 * half, images * ROWS
+    forward, inverse, kernel, back, one = fourier()
+    kernel_high, kernel_low = split(kernel)
+    back_high, back_low = split(back)
+    consts = [
+        jnp.asarray(forward.astype(np.float32).astype(bf16)),
+        jnp.asarray(inverse.astype(np.float32).astype(bf16)),
+        jnp.asarray(kernel_high), jnp.asarray(kernel_low),
+        jnp.asarray(back_high), jnp.asarray(back_low),
+        jnp.asarray(one.astype(np.float32)),
+    ]
+    vmem = pl.BlockSpec(memory_space=pltpu.VMEM)
+    smem = pl.BlockSpec(memory_space=pltpu.SMEM)
+    hbm = pl.BlockSpec(memory_space=pl.ANY)
+
+    def bufs(rows):
+        buffer = lambda free: pltpu.VMEM((2,) * free + (rows, 128), bf16)
+        return {
+            "acc": buffer(4), "out": buffer(4), "came": buffer(4),
+            "landing": [buffer(3), buffer(2), buffer(1), buffer(0)],
+        }
+
+    stacked = lambda free: pltpu.VMEM((STREAMS,) + (2,) * free + (BLOCK, 128), bf16)
+    tall = lambda width, dtype: pltpu.VMEM((total, width), dtype)
+    cube = lambda dtype: pltpu.VMEM((HEADS, ROWS, KEYS), dtype)
+    scratch = dict(
+        piece_full=pltpu.VMEM((2, 2, 2, 2, PIECE, 128), bf16),
+        piece_other=pltpu.VMEM((2, 2, 2, 2, PIECE, 128), bf16),
+        taps_pad=pltpu.VMEM((TAPS, half), f32),
+        wqkv=pltpu.VMEM((WIDTH, 3 * WIDTH), bf16),
+        wproj=pltpu.VMEM((WIDTH, WIDTH), bf16),
+        fc1_full=pltpu.VMEM((WIDTH, units), bf16),
+        fc2_full=pltpu.VMEM((units, WIDTH), bf16),
+        conv_full=pltpu.VMEM((TAPS, units), bf16),
+        inputs=tall(WIDTH, f32),
+        cot_pad=tall(WIDTH, bf16),
+        n1=tall(WIDTH, bf16),
+        packed=pltpu.VMEM((images, KEYS, 3 * WIDTH), bf16),
+        score=cube(f32),
+        probs=pltpu.VMEM((images, HEADS, ROWS, KEYS), f32),
+        attn=pltpu.VMEM((images, HEADS, ROWS, KEYS), bf16),
+        att=tall(WIDTH, bf16),
+        mid=tall(WIDTH, f32),
+        n2=tall(WIDTH, bf16),
+        turned=pltpu.VMEM((COEFS, units), f32),
+        ghat=pltpu.VMEM((images, COEFS, units), f32),
+        hid=tall(half, f32),
+        conv_low=tall(units, bf16),
+        ghid_low=tall(units, bf16),
+        gmid=tall(WIDTH, f32),
+        gmid_low=tall(WIDTH, bf16),
+        gatt=tall(WIDTH, bf16),
+        low=cube(bf16),
+        gpacked=tall(3 * WIDTH, bf16),
+        mix=pltpu.VMEM((2 * HEADS * HEADS, 8, 128), f32),
+        rows_out=pltpu.VMEM((8, WIDTH), f32),
+        square=pltpu.VMEM((128, 128), f32),
+        gqkv=pltpu.VMEM((WIDTH, 3 * WIDTH), f32),
+        gproj=pltpu.VMEM((WIDTH, WIDTH), f32),
+        small_sums=pltpu.VMEM((5, SMALL, 128), f32),
+        small_landed=pltpu.VMEM((5, SMALL, 128), f32),
+        streams_out=stacked(4),
+        streams_came=stacked(4),
+        streams_acc=stacked(4),
+        streams_landing=[stacked(free) for free in (3, 2, 1, 0)],
+        gconv=pltpu.VMEM((TAPS, STREAM), f32),
+        att_bufs=bufs(PIECE),
+        local_sems=pltpu.SemaphoreType.DMA((2,)),
+        gather_sems=pltpu.SemaphoreType.DMA((2, 3, 4)),
+        gather_pair_sems=pltpu.SemaphoreType.DMA((2, 16)),
+        stream_pair_sems=pltpu.SemaphoreType.DMA((2, STREAMS)),
+        stream_sems=pltpu.SemaphoreType.DMA((STREAMS, 2, 2, 3, 4)),
+        att_sems=pltpu.SemaphoreType.DMA((2, 3, 4)),
+        att_pair_sems=pltpu.SemaphoreType.DMA((2, 6)),
+    )
+    return pl.pallas_call(
+        block_kernel,
+        in_specs=[smem] * 2 + [vmem] * 10 + [hbm] + [vmem] * 2 + [hbm] + [vmem] * len(consts),
+        out_specs=[vmem] * (4 + STREAMS),
+        out_shape=[
+            jax.ShapeDtypeStruct(tok.shape, bf16),
+            jax.ShapeDtypeStruct(tok.shape, f32),
+        ]
+        + [jax.ShapeDtypeStruct((2, 2, 2, 2, BLOCK, 128), bf16)] * STREAMS
+        + [
+            jax.ShapeDtypeStruct((PIECE, 128), bf16),
+            jax.ShapeDtypeStruct((SMALL, 128), f32),
+        ],
+        scratch_shapes=list(scratch.values()),
+        compiler_params=pltpu.CompilerParams(
+            vmem_limit_bytes=VMEM, collective_id=0, has_side_effects=True
+        ),
+        name="block",
+    )(
+        pre, post, tok, cot, gain1, bias1, pbias, gain2, bias2, fc2b, qkv, proj, fc1, conv, bias,
+        fc2, *consts,
+    )
+
+
+def finish_kernel(
+    t0, t1, t2, piece, small, gfc1, gb1, gconv, gfc2, gqkv, gproj, g1, b1, pb, g2, b2, fb,
+    pre, post, taps, mixes,
+):
+    for s, total in enumerate((t0, t1, t2)):
+        side = slice(s * STREAM, (s + 1) * STREAM)
+        for d in range(16):
+            block = total[index_of(d)].astype(f32)
+            gfc1[24 * d : 24 * d + 24, side] = untiles(block[:48], 2)
+            gfc2[s * STREAM + 16 * d : s * STREAM + 16 * d + 16, :] = untiles(block[48:96], 3)
+            taps[8 * d : 8 * d + 8, :] = block[96:104]
+        filters = untiles(taps[...], 2)
+        gconv[:, side] = filters[: KS * KS]
+        gb1[side] = filters[KS * KS]
+    both = untiles(piece[...].astype(f32), 6)
+    width = gqkv.shape[1]
+    gqkv[...] = both[:, :width]
+    gproj[...] = both[:, width:]
+    rows = untiles(small[:24], 3)
+    for index, ref in enumerate((g1, b1, pb, g2, b2, fb)):
+        ref[...] = rows[index].reshape(ref.shape)
+    line = small[24:25]
+    for index, ref in enumerate((pre, post)):
+        for g in range(HEADS):
+            start = HEADS * HEADS * index + HEADS * g
+            mixes[index, g : g + 1, :HEADS] = line[:, start : start + HEADS]
+    pre[...] = mixes[0, :HEADS, :HEADS] * 0.125
+    post[...] = mixes[1, :HEADS, :HEADS]
+
+
+def call_finish(totals, piece, small, half):
+    vmem = pl.BlockSpec(memory_space=pltpu.VMEM)
+    shape = lambda *dims: jax.ShapeDtypeStruct(dims, f32)
+    return pl.pallas_call(
+        finish_kernel,
+        in_specs=[vmem] * (STREAMS + 2),
+        out_specs=[vmem] * 14,
+        out_shape=[
+            shape(WIDTH, half), shape(half), shape(KS * KS, half), shape(half, WIDTH),
+            shape(24, 3 * WIDTH // 2), shape(24, WIDTH // 2),
+        ]
+        + [shape(WIDTH)] * 6
+        + [shape(HEADS, HEADS)] * 2,
+        scratch_shapes=[pltpu.VMEM((128, 128), f32), pltpu.VMEM((2, 8, 128), f32)],
+        compiler_params=pltpu.CompilerParams(vmem_limit_bytes=VMEM),
+        name="finish",
+    )(*totals, piece, small)
+
+
+def shards_any(
     tokens, norm1_gain, norm1_bias, qkv_weight, mix_pre, mix_post, proj_weight, proj_bias,
     norm2_gain, norm2_bias, fc1_weight, fc1_bias, conv_weight, fc2_weight, fc2_bias, cotangent,
 ):
     gather = lambda v, axis, dim: lax.all_gather(v, axis, axis=dim, tiled=True)
     both = jnp.concatenate([qkv_weight, proj_weight], axis=1)
-    rows = gather(both, "dp", 0)
-    pair = lax.all_gather(rows, "tensor", axis=0)
+    pair = lax.all_gather(gather(both, "dp", 0), "tensor", axis=0)
     columns = qkv_weight.shape[1]
     wqkv = jnp.concatenate([pair[0, :, :columns], pair[1, :, :columns]], axis=1)
     wproj = jnp.concatenate([pair[0, :, columns:], pair[1, :, columns:]], axis=1)
     fc1 = gather(fc1_weight, "tensor", 1)
-    fc1b = gather(fc1_bias, "tensor", 0)
-    conv = gather(conv_weight, "tensor", 1)
+    taps = jnp.concatenate([conv_weight, fc1_bias[None]], axis=0)
+    taps = jnp.pad(gather(taps, "tensor", 1), ((0, TAPS - KS * KS - 1), (0, 0)))
     fc2 = gather(fc2_weight, "tensor", 0)
-    block_out, gtok, gqkv, gproj, gfc1, gb1, gconv, gfc2, gb2, rows, mix = local_block(
+    block_out, gtok, gqkv, gproj, gfc1, gconv, gfc2, small = local_block(
         tokens, norm1_gain, norm1_bias, wqkv, mix_pre, mix_post, wproj, proj_bias, norm2_gain,
-        norm2_bias, fc1, fc1b, conv, fc2, fc2_bias, cotangent,
+        norm2_bias, fc1, taps, fc2, fc2_bias, cotangent,
     )
     scatter = lambda v, axis, dim: lax.psum_scatter(v, axis, scatter_dimension=dim, tiled=True)
-    gqkv = scatter(scatter(gqkv.astype(bf16), "tensor", 1).astype(f32), "dp", 0)
-    gproj = scatter(scatter(gproj.astype(bf16), "tensor", 1).astype(f32), "dp", 0)
-    gfc1 = lax.psum(scatter(gfc1.astype(bf16), "tensor", 1).astype(f32), "dp")
-    gfc2 = lax.psum(scatter(gfc2.astype(bf16), "tensor", 0).astype(f32), "dp")
+    gqkv = scatter(scatter(gqkv, "tensor", 1), "dp", 0)
+    gproj = scatter(scatter(gproj, "tensor", 1), "dp", 0)
+    gfc1 = lax.psum(scatter(gfc1, "tensor", 1), "dp")
+    gfc2 = lax.psum(scatter(gfc2, "tensor", 0), "dp")
     gconv = lax.psum(scatter(gconv, "tensor", 1), "dp")
-    gb1 = lax.psum(scatter(gb1[0], "tensor", 0), "dp")
-    mixes = jnp.sum(mix, axis=1).reshape(2, HEADS, HEADS)
-    rows, gb2, mixes = lax.psum((rows, gb2, mixes), ("dp", "tensor"))
+    small = lax.psum(small, ("dp", "tensor"))
+    rows = jnp.concatenate([small[0:8], small[8:16], small[16:24]], axis=1)
+    mixes = small[24, : 2 * HEADS * HEADS].reshape(2, HEADS, HEADS)
     return (
         block_out, gtok, rows[0], rows[1], gqkv, mixes[0] * 0.125, mixes[1], gproj, rows[2],
-        rows[3], rows[4], gfc1, gb1, gconv, gfc2, gb2[0],
+        rows[3], rows[4], gfc1, gconv[KS * KS], gconv[: KS * KS], gfc2, rows[5],
+    )
+
+
+def shards_sixteen(
+    tokens, norm1_gain, norm1_bias, qkv_weight, mix_pre, mix_post, proj_weight, proj_bias,
+    norm2_gain, norm2_bias, fc1_weight, fc1_bias, conv_weight, fc2_weight, fc2_bias, cotangent,
+):
+    block_out, gtok, t0, t1, t2, piece, small = call_block(
+        mix_pre, mix_post, tokens, cotangent, norm1_gain, norm1_bias, proj_bias, norm2_gain,
+        norm2_bias, fc2_bias, qkv_weight, proj_weight, fc1_weight, conv_weight, fc1_bias,
+        fc2_weight,
+    )
+    gfc1, gb1, gconv, gfc2, gqkv, gproj, g1, b1, pb, g2, b2, fb, pre, post = call_finish(
+        (t0, t1, t2), piece, small, fc1_weight.shape[1]
+    )
+    return (
+        block_out, gtok, g1, b1, gqkv, pre, post, gproj, pb, g2, b2, gfc1, gb1, gconv, gfc2, fb
     )
 
 
@@ -549,4 +1320,6 @@
         spec, spec, P(), P(), P("dp", "tensor"), P(), P(), P("dp", "tensor"), P(), P(), P(),
         P(None, "tensor"), P("tensor"), P(None, "tensor"), P("tensor", None), P(),
     )
-    return jax.shard_map(shards, mesh=mesh, in_specs=in_specs, out_specs=out_specs, check_vma=False)
+    sixteen = mesh.shape["dp"] == 16 and mesh.shape["tensor"] == 2
+    body = shards_sixteen if sixteen else shards_any
+    return jax.shard_map(body, mesh=mesh, in_specs=in_specs, out_specs=out_specs, check_vma=False)

time: 566 us -> 114 us (0.20)
  waiting for transfers between devices: 241 us -> 0 us
  blocking collectives: 209 us -> 0 us
  Pallas kernels: 72.9 us -> 106 us
  between operations: 14.8 us -> 0.85 us
  other arithmetic: 11 us -> 0 us
  local copies, waits for them, and re-layouts: 16.6 us -> 6.5 us
    psum x2 -> x0, blocking collectives: 154 us -> none  [the longest x1 113 us: shards(): gfc1 = lax.psum(scatter(gfc1.astype(bf16), 'tensor', 1).astype(f32), 'dp')]
    unnamed x14 -> x0, waiting for transfers between devices: 137 us -> none
    reduce_scatter x4 -> x0, waiting for transfers between devices: 104 us -> none  [shards(): lax.psum_scatter(v, axis, scatter_dimension=dim, tiled=True)]
    all_gather x3 -> x0, blocking collectives: 52.2 us -> none  [shards(): gather = lambda v, axis, dim: lax.all_gather(v, axis, axis=dim, tiled=True)]
    pallas_call x3 -> x2, Pallas kernels: 72.9 us -> 106 us  [the longest x1 103 us: call_block(): pl.pallas_call(block_kernel, in_specs=[smem] * 2 + [vmem] * 10 + [hbm] +...]
    convert_element_type x6 -> x0, other arithmetic: 7.26 us -> none  [the longest x1 2.97 us: shards(): gfc1 = lax.psum(scatter(gfc1.astype(bf16), 'tensor', 1).astype(f32), 'dp')]
  transfers between devices with their start and end apart: 11 -> 0, of which waited for: 3 -> 0; matrix products, arithmetic and copies ran while one was open for 4% -> 0% of each run, Pallas kernels for 8% -> 0%
where the time goes in v3:
time: 114 us
  Pallas kernels  106 us (93%)
  local copies, waits for them, and re-layouts  6.5 us (6%)
    pallas_call x1, Pallas kernels, call_block(): pl.pallas_call(block_kernel, in_specs=[smem] * 2 + [vmem] * 10 + [hbm] +...  103 us
    unnamed x8, local copies, waits for them, and re-layouts  6.5 us
    pallas_call x1, Pallas kernels, call_finish(): pl.pallas_call(finish_kernel, in_specs=[vmem] * (STREAMS + 2), out_specs=...  2.89 us

profile of v3, /device:TPU:0, one launch (start us, length us, event | category | flops | bytes accessed | tf_op | source)
XLA Modules:
  0.0 113.7 jit_solution(3797186999610408314)
XLA Ops:
  0.6 0.0 copy-start.1
  0.7 2.0 %copy.39.tok = bf16[4,197,384]{2,1,0:T(8,128)(2,1)} copy(bf16[4,197,384]{2,0,1:T(4,128)(2,1)} %param.23) | data formatting | bytes 1210368 | tf_op args[0]
  2.7 0.0 copy-done.1
  2.7 0.9 copy.40.cot
  3.6 103.5 %block.1 = (bf16[4,197,384]{2,1,0:T(8,128)(2,1)}, f32[4,197,384]{2,1,0:T(8,128)}, bf16[2,2,2,2,112,128]{5,4,3,2,1,0:T(8,128)(2,1)}, bf16[2,2,2,2,112,128]{5,4,3,...) custom-call(f32[6,6]{1,0:T(8,128)} %pre.1, ...), custom_call_target="tpu_custom_call" | custom-call | tf_op jit(solution)/shard_map/block/pallas_call | solution.py:1190
  107.1 0.0 copy-start
  107.1 2.2 %copy.41 = bf16[4,197,384]{2,0,1:T(4,128)(2,1)} copy(bf16[4,197,384]{2,1,0:T(8,128)(2,1)} %get-tuple-element.58) | data formatting | bytes 1210368
  109.3 0.0 copy-done
  109.3 1.3 %copy.42 = f32[4,197,384]{2,0,1:T(4,128)} copy(f32[4,197,384]{2,1,0:T(8,128)S(1)} %copy-done) | data formatting | bytes 2420736
  110.7 2.9 %finish.1 = (f32[384,768]{1,0:T(8,128)}, f32[768]{0:T(1024)}, f32[49,768]{1,0:T(8,128)}, f32[768,384]{1,0:T(8,128)}, f32[24,576]{1,0:T(8,128)}, /*index=5*/f32[2...) custom-call(bf16[2,2,2,2,112,128]{5,4,3,2,1,0:T(8,128)(2,1)} %get-tu, ...), custom_call_target="tpu_custom_call" | custom-call | tf_op jit(solution)/shard_map/finish/pallas_call | solution.py:1247
Async XLA Ops:
  0.6 2.0 %copy-start.1 = (bf16[4,197,384]{2,0,1:T(4,128)(2,1)S(1)}, bf16[4,197,384]{2,0,1:T(4,128)(2,1)}, u32[]{:S(2)}) copy-start(bf16[4,197,384]{2,0,1:T(4,128)(2,1)} %param.38) | copy-start | bytes 1815556
  107.1 2.2 %copy-start = (f32[4,197,384]{2,1,0:T(8,128)S(1)}, f32[4,197,384]{2,1,0:T(8,128)}, u32[]{:S(2)}) copy-start(f32[4,197,384]{2,1,0:T(8,128)} %get-tuple-element.59) | copy-start | bytes 3631108

commit v4 on v3

--- a/solution.py
+++ b/solution.py
@@ -515,20 +515,41 @@
 
 
 SIDES = (8, 4, 2, 1)
-ORDERS = ((3, 2, 1, 0), (2, 1, 0, 3), (1, 0, 3, 2))
+DEPTH, PLANE = (0, 1), (2, 3)
+ROUNDS = ((PLANE, DEPTH), (DEPTH, PLANE))
+FLIPS = ((0, 1), (1, 0), (1, 1))
 MESH_IDS = pl.DeviceIdType.MESH
 PIECE = 144
-PIECE_PARTS = ((0, 48), (48, 48), (96, 48))
+PIECE_PARTS = ((0, 96), (96, 48))
 BLOCK = 112
-BLOCK_PARTS = ((0, 48), (48, 32), (80, 32))
+BLOCK_PARTS = ((0, 80), (80, 32))
 STREAMS = 3
 
 
-def place():
-    dp, core = lax.axis_index("dp"), lax.axis_index("tensor")
-    bits = [lax.rem(dp // stride, 2) for stride in SIDES]
-    partners = [(dp + (1 - 2 * bit) * stride, core) for bit, stride in zip(bits, SIDES)]
-    return bits, partners, (dp, 1 - core), core
+class Place:
+    def __init__(self):
+        self.dp, self.core = lax.axis_index("dp"), lax.axis_index("tensor")
+        self.bits = tuple(lax.rem(self.dp // stride, 2) for stride in SIDES)
+        self.pair = (self.dp, 1 - self.core)
+
+    def peer(self, axes, flip):
+        dp = self.dp
+        for axis, turn in zip(axes, flip):
+            if turn:
+                dp = dp + (1 - 2 * self.bits[axis]) * SIDES[axis]
+        return dp, self.core
+
+    def mine(self, axes):
+        return {axis: self.bits[axis] for axis in axes}
+
+    def theirs(self, axes, flip):
+        return {
+            axis: 1 - self.bits[axis] if turn else self.bits[axis] for axis, turn in zip(axes, flip)
+        }
+
+    def everyone(self):
+        peers = [self.peer(axes, flip) for axes in (PLANE, DEPTH) for flip in FLIPS]
+        return peers + [self.pair]
 
 
 def meet(partners):
@@ -549,87 +570,104 @@
     return tuple(fixed.get(axis, slice(None)) for axis in range(4)) + (rows,)
 
 
-def combos(count):
-    return [tuple((i >> (count - 1 - j)) & 1 for j in range(count)) for i in range(2**count)]
-
-
 def index_of(d):
     return tuple((d // stride) % 2 for stride in SIDES)
 
 
-class Halving:
-    def __init__(self, acc, landing, sems, parts, turn, bits, partners):
+class Sum:
+    def __init__(self, acc, landing, sems, parts, where):
         self.acc, self.landing, self.sems = acc, landing, sems
-        self.parts, self.turn, self.bits, self.partners = parts, turn, bits, partners
-
-    def copy(self, part, step):
-        order, rows = ORDERS[(part + self.turn) % 3], pl.ds(*self.parts[part])
-        axis = order[step]
-        fixed = {a: self.bits[a] for a in order[:step]}
-        fixed[axis] = 1 - self.bits[axis]
-        dst = self.landing[step].at[(slice(None),) * (3 - step) + (rows,)]
+        self.parts, self.where = parts, where
+
+    def copy(self, part, turn, peer):
+        rows, axes, flip = pl.ds(*self.parts[part]), ROUNDS[part][turn], FLIPS[peer]
+        fixed = self.where.theirs(axes, flip)
+        if turn == 0:
+            dst = self.landing[0].at[peer, :, :, rows]
+        else:
+            fixed.update(self.where.mine(ROUNDS[part][0]))
+            dst = self.landing[1].at[peer, rows]
         return remote(
-            self.acc.at[region(fixed, rows)], dst, self.sems, (part, step), self.partners[axis]
+            self.acc.at[region(fixed, rows)], dst, self.sems, (part, turn, peer),
+            self.where.peer(axes, flip),
         )
 
-    def start(self, step):
-        for part in range(3):
-            self.copy(part, step).start()
-
-    def act(self, step):
-        for part in range(3):
-            order, rows = ORDERS[(part + self.turn) % 3], pl.ds(*self.parts[part])
-            self.copy(part, step).wait_recv()
-            fixed = {a: self.bits[a] for a in order[: step + 1]}
-            free = [a for a in range(4) if a not in fixed]
-            for combo in combos(len(free)):
-                where = region({**fixed, **dict(zip(free, combo))}, rows)
-                came = self.landing[step][combo + (rows,)]
-                self.acc[where] = (self.acc[where].astype(f32) + came.astype(f32)).astype(bf16)
-            if step < 3:
-                self.copy(part, step + 1).start()
+    def start(self):
+        for part in range(2):
+            for peer in range(3):
+                self.copy(part, 0, peer).start()
+
+    def act(self, turn):
+        for part in range(2):
+            rows = pl.ds(*self.parts[part])
+            first, second = ROUNDS[part]
+            for peer in range(3):
+                self.copy(part, turn, peer).wait_recv()
+            for near in (0, 1) if turn == 0 else (None,):
+                for far in (0, 1) if turn == 0 else (None,):
+                    fixed = self.where.mine(first)
+                    if turn == 0:
+                        fixed.update({second[0]: near, second[1]: far})
+                        came = [self.landing[0][peer, near, far, rows] for peer in range(3)]
+                    else:
+                        fixed.update(self.where.mine(second))
+                        came = [self.landing[1][peer, rows] for peer in range(3)]
+                    spot = region(fixed, rows)
+                    total = self.acc[spot].astype(f32)
+                    for values in came:
+                        total = total + values.astype(f32)
+                    self.acc[spot] = total.astype(bf16)
+            if turn == 0:
+                for peer in range(3):
+                    self.copy(part, 1, peer).start()
 
     def finish(self):
-        for step in range(4):
-            for part in range(3):
-                self.copy(part, step).wait_send()
-
-
-class Doubling:
-    def __init__(self, full, sems, parts, turn, bits, partners):
-        self.full, self.sems = full, sems
-        self.parts, self.turn, self.bits, self.partners = parts, turn, bits, partners
-
-    def come(self, part, step):
-        order, rows = ORDERS[(part + self.turn) % 3][::-1], pl.ds(*self.parts[part])
-        fixed = {a: self.bits[a] for a in order[step + 1 :]}
-        fixed[order[step]] = 1 - self.bits[order[step]]
-        return region(fixed, rows)
-
-    def copy(self, part, step):
-        order, rows = ORDERS[(part + self.turn) % 3][::-1], pl.ds(*self.parts[part])
-        held = region({a: self.bits[a] for a in order[step:]}, rows)
+        for part in range(2):
+            for turn in range(2):
+                for peer in range(3):
+                    self.copy(part, turn, peer).wait_send()
+
+
+class Gather:
+    def __init__(self, full, sems, parts, where):
+        self.full, self.sems, self.parts, self.where = full, sems, parts, where
+
+    def spot(self, part, turn, flip):
+        first, second = ROUNDS[part][::-1]
+        if turn == 0:
+            fixed = {**self.where.mine(second), **self.where.theirs(first, flip)}
+        else:
+            fixed = self.where.theirs(second, flip)
+        return region(fixed, pl.ds(*self.parts[part]))
+
+    def copy(self, part, turn, peer):
+        axes, held = ROUNDS[part][::-1][turn], self.spot(part, turn, (0, 0))
         return remote(
-            self.full.at[held], self.full.at[held], self.sems, (part, step),
-            self.partners[order[step]],
+            self.full.at[held], self.full.at[held], self.sems, (part, turn, peer),
+            self.where.peer(axes, FLIPS[peer]),
         )
 
     def start(self):
-        for part in range(3):
-            self.copy(part, 0).start()
-
-    def act(self, step, then=None):
-        for part in range(3):
-            self.copy(part, step).wait_recv()
-            if step < 3:
-                self.copy(part, step + 1).start()
+        for part in range(2):
+            for peer in range(3):
+                self.copy(part, 0, peer).start()
+
+    def act(self, turn, then=None):
+        for part in range(2):
+            for peer in range(3):
+                self.copy(part, turn, peer).wait_recv()
+            if turn == 0:
+                for peer in range(3):
+                    self.copy(part, 1, peer).start()
             if then is not None:
-                then(part, step)
+                for peer in range(3):
+                    then(part, turn, peer)
 
     def finish(self):
-        for step in range(4):
-            for part in range(3):
-                self.copy(part, step).wait_send()
+        for part in range(2):
+            for turn in range(2):
+                for peer in range(3):
+                    self.copy(part, turn, peer).wait_send()
 
 
 def tiles(values):
@@ -660,8 +698,8 @@
     images = tok.shape[0]
     total = images * ROWS
     half = fc1.shape[1]
-    bits, partners, pair, core = place()
-    mine = tuple(bits)
+    where = Place()
+    pair, core, mine = where.pair, where.core, where.bits
     mine_start = pl.multiple_of(core * half, 128)
     other_start = pl.multiple_of((1 - core) * half, 128)
     cols, rows_of = pl.ds(mine_start, half), pl.ds(mine_start, half)
@@ -675,8 +713,8 @@
     taps_pad[: KS * KS] = conv[...].astype(f32)
     taps_pad[KS * KS : KS * KS + 1] = bias[...].astype(f32).reshape(1, half)
     conv_full[:, cols] = taps_pad[...].astype(bf16)
-    meet(partners + [pair])
-    gather = Doubling(piece_full, gather_sems, PIECE_PARTS, 0, bits, partners)
+    meet(where.everyone())
+    gather = Gather(piece_full, gather_sems, PIECE_PARTS, where)
     gather.start()
     weights_come = [
         remote(conv_full.at[:, cols], conv_full.at[:, cols], gather_pair_sems, (0,), pair),
@@ -693,11 +731,11 @@
     for copy in weights_come + forwards + local:
         copy.start()
 
-    def forward(part, step):
-        where = gather.come(part, step)
+    def forward(part, turn, peer):
+        spot = gather.spot(part, turn, FLIPS[peer])
         copy = remote(
-            piece_full.at[where], piece_other.at[where], gather_pair_sems,
-            (4 + 3 * step + part,), pair,
+            piece_full.at[spot], piece_other.at[spot], gather_pair_sems,
+            (4 + 6 * part + 3 * turn + peer,), pair,
         )
         copy.start()
         forwards.append(copy)
@@ -710,7 +748,6 @@
         grads = gmid[spans[b], :]
         cot_sum = cot_sum + add_rows(grads)
         cot_pad[spans[b], :] = grads.astype(bf16)
-    gather.act(0, forward)
     for b in range(images):
         centred, r = centre(inputs[spans[b], :])
         n1[spans[b], :] = jnp.where(inside, centred * r * row(gain1) + row(bias1), 0.0).astype(bf16)
@@ -723,15 +760,14 @@
         for b in range(images):
             ghat[b, :, units] = dot(fwd[...], hid[spans[b], :].astype(bf16))
 
-    gather.act(1, forward)
+    gather.act(0, forward)
     for copy in local:
         copy.wait()
     prepare(mine_start)
-    gather.act(2, forward)
     for copy in weights_come:
         copy.wait_recv()
     prepare(other_start)
-    gather.act(3, forward)
+    gather.act(1, forward)
     for copy in forwards:
         copy.wait_recv()
     width = qkv.shape[1]
@@ -813,28 +849,25 @@
     def exchange_copy(s):
         return remote(streams_out.at[s], streams_came.at[s], stream_pair_sems, (s,), pair)
 
-    halvings = [
-        Halving(
+    sums = [
+        Sum(
             streams_acc.at[s], [ref.at[s] for ref in streams_landing], stream_sems.at[s, 0],
-            BLOCK_PARTS, s, bits, partners,
+            BLOCK_PARTS, where,
         )
         for s in range(STREAMS)
     ]
-    doublings = [
-        Doubling(fulls[s], stream_sems.at[s, 1], BLOCK_PARTS, s, bits, partners)
-        for s in range(STREAMS)
-    ]
+    gathers = [Gather(fulls[s], stream_sems.at[s, 1], BLOCK_PARTS, where) for s in range(STREAMS)]
 
     def act(s, step):
         if step < 0:
-            halvings[s].start(0)
-        elif step < 4:
-            halvings[s].act(step)
-            if step == 3:
+            sums[s].start()
+        elif step < 2:
+            sums[s].act(step)
+            if step == 1:
                 fulls[s][mine] = streams_acc[(s,) + mine]
-                doublings[s].start()
+                gathers[s].start()
         else:
-            doublings[s].act(step - 4)
+            gathers[s].act(step - 2)
 
     def blocks():
         filters = tiles(gconv[...])
@@ -851,9 +884,9 @@
             )
 
     def mlp(i, carry):
-        units = pl.ds(
-            pl.multiple_of(lax.rem((1 - core) * STREAMS + i, 2 * STREAMS) * STREAM, STREAM), STREAM
-        )
+        s, own = i // 2, lax.rem(i, 2)
+        owner = (1 - core) * (1 - own) + core * own
+        units = pl.ds(pl.multiple_of((owner * STREAMS + s) * STREAM, STREAM), STREAM)
         bias_row = conv_full[:, units].astype(f32)[KS * KS : KS * KS + 1]
         hid[:, :STREAM] = dot(n2[...], fc1_full[:, units]) + bias_row
         kr, ki = turned[:HALF, units], turned[HALF:, units]
@@ -884,23 +917,23 @@
         hid[:STREAM, :WIDTH] = t_dot(conv_low[:, units], cot_pad[...])
         gqkv[:, :STREAM] = t_dot(n2[...], ghid_low[:, units])
 
-        @pl.when(i < STREAMS)
+        @pl.when(own == 0)
         def _():
             for index, values in blocks():
-                streams_out[(i,) + index] = values.astype(bf16)
-            exchange_copy(i).start()
-
-        @pl.when(i >= STREAMS)
+                streams_out[(s,) + index] = values.astype(bf16)
+            exchange_copy(s).start()
+
+        @pl.when(own == 1)
         def _():
-            s = i - STREAMS
             exchange_copy(s).wait_recv()
             for index, values in blocks():
                 came = streams_came[(s,) + index].astype(f32)
                 streams_acc[(s,) + index] = (values + came).astype(bf16)
 
-        for turn, items in enumerate((((0, -1),), ((0, 0), (1, -1)), ((0, 1), (1, 0), (2, -1)))):
-
-            @pl.when(i == STREAMS + turn)
+        plan = {1: ((0, -1),), 3: ((0, 0), (1, -1)), 4: ((0, 1),), 5: ((2, -1), (1, 0), (0, 2))}
+        for turn, items in plan.items():
+
+            @pl.when(i == turn)
             def _():
                 for item in items:
                     act(*item)
@@ -908,15 +941,6 @@
         return carry
 
     lax.fori_loop(0, 2 * STREAMS, mlp, 0)
-    pending = [
-        (2, 0), (1, 1), (0, 2), (2, 1), (1, 2), (0, 3), (2, 2), (1, 3), (0, 4), (2, 3), (1, 4),
-        (0, 5), (2, 4), (1, 5), (0, 6), (2, 5), (1, 6), (0, 7), (2, 6), (1, 7), (2, 7),
-    ]
-
-    def poll(count=1):
-        for _ in range(count):
-            if pending:
-                act(*pending.pop(0))
 
     hid[:, :WIDTH] = dot_t(ghid_low[...], fc1_full[...])
     hid[:, WIDTH:] = dot(conv_low[...], fc2_full[...])
@@ -936,7 +960,7 @@
         rounded = whole_grad.astype(bf16)
         proj_sum = proj_sum + add_rows(rounded.astype(f32))
         gmid_low[spans[b], :] = rounded
-    poll()
+    act(1, 1)
     gatt[...] = dot_t(gmid_low[...], wproj[...]).astype(bf16)
     mix[...] = jnp.zeros_like(mix)
 
@@ -944,17 +968,15 @@
         values = values[:, :128] + values[:, 128:]
         return values[:8] + values[8:]
 
-    places = 4
-    plan = [[pending.pop(0)] for _ in range(images * places) if pending]
+    plan = {(0, 3): ((1, 2), (2, 0)), (1, 3): ((2, 1),), (2, 3): ((2, 2),)}
 
     def poll_at(b, spot):
-        for image_index in range(images):
-            index = image_index * places + spot
-            if index < len(plan):
+        for (image_index, at), items in plan.items():
+            if at == spot:
 
                 @pl.when(b == image_index)
                 def _():
-                    for item in plan[index]:
+                    for item in items:
                         act(*item)
 
     def put_weight(g, values):
@@ -1017,7 +1039,6 @@
     gproj[...] = t_dot(att[...], gmid_low[...])
     for n in range(0, 3 * WIDTH, WIDTH):
         gqkv[:, n : n + WIDTH] = t_dot(n1[...], gpacked[:, n : n + WIDTH])
-    poll()
 
     width, proj_width = gqkv.shape[1] // 2, gproj.shape[1] // 2
 
@@ -1043,11 +1064,19 @@
     exchange = remote(att_bufs["out"], att_bufs["came"], att_pair_sems, (0,), pair)
     exchange.start()
     hid[:, :WIDTH] = dot_t(gpacked[...], wqkv[...])
+    attention = Sum(att_bufs["acc"], att_bufs["landing"], att_sems, PIECE_PARTS, where)
+    exchange.wait_recv()
+    for side in range(2):
+
+        @pl.when(core == side)
+        def _():
+            for index, values in pieces(side):
+                came = att_bufs["came"][index].astype(f32)
+                att_bufs["acc"][index] = (values + came).astype(bf16)
+
+    attention.start()
     norm_gain = jnp.zeros((1, WIDTH), f32)
     norm_bias = jnp.zeros((1, WIDTH), f32)
-    attention = Halving(
-        att_bufs["acc"], att_bufs["landing"], att_sems, PIECE_PARTS, 0, bits, partners
-    )
     for b in range(images):
         centred, r = centre(inputs[spans[b], :])
         grad = hid[spans[b], :WIDTH]
@@ -1055,18 +1084,6 @@
         norm_gain = norm_gain + add_rows(gain_rows)
         norm_bias = norm_bias + add_rows(grad)
         gtok_out[b] = (gmid[spans[b], :] + back)[:SEQ]
-        if b == 1:
-            exchange.wait_recv()
-            for side in range(2):
-
-                @pl.when(core == side)
-                def _():
-                    for index, values in pieces(side):
-                        came = att_bufs["came"][index].astype(f32)
-                        att_bufs["acc"][index] = (values + came).astype(bf16)
-
-            attention.start(0)
-            poll()
     rows_out[...] = jnp.concatenate(
         [norm_gain, norm_bias, proj_sum, gain_sum, bias_sum, cot_sum, jnp.zeros((2, WIDTH), f32)],
         axis=0,
@@ -1075,37 +1092,55 @@
         small_sums[0, 8 * t : 8 * t + 8] = rows_out[:, 128 * t : 128 * t + 128]
     square[...] = jnp.zeros_like(square)
     square[: 2 * HEADS * HEADS] = jnp.sum(mix[...], axis=1)
-    sums = add_rows(square[...].T)
-    small_sums[0, 24:] = jnp.concatenate([sums, jnp.zeros((SMALL - 25, 128), f32)], axis=0)
-
-    def small_copy(step):
-        device = pair if step == 0 else partners[4 - step]
+    line = add_rows(square[...].T)
+    small_sums[0, 24:] = jnp.concatenate([line, jnp.zeros((SMALL - 25, 128), f32)], axis=0)
+
+    def small_copy(turn, peer):
+        if turn == 0:
+            device = pair
+        else:
+            device = where.peer((PLANE, DEPTH)[turn - 1], FLIPS[peer])
+        index = 0 if turn == 0 else 3 * turn - 2 + peer
         return remote(
-            small_sums.at[step], small_landed.at[step], att_pair_sems, (1 + step,), device
+            small_sums.at[turn], small_landed.at[index], att_pair_sems, (1 + index,), device
         )
 
-    small_copy(0).start()
-    for step in range(4):
-        small_copy(step).wait_recv()
-        small_sums[step + 1] = small_sums[step] + small_landed[step]
-        small_copy(step + 1).start()
-        attention.act(step)
-        poll(2)
-    poll(len(pending))
-    small_copy(4).wait_recv()
-    small_out[...] = small_sums[4] + small_landed[4]
+    small_counts = (1, 3, 3)
+
+    def small_start(turn):
+        for peer in range(small_counts[turn]):
+            small_copy(turn, peer).start()
+
+    def small_take(turn):
+        total = small_sums[turn]
+        for peer in range(small_counts[turn]):
+            small_copy(turn, peer).wait_recv()
+            total = total + small_landed[0 if turn == 0 else 3 * turn - 2 + peer]
+        return total
+
+    small_start(0)
+    small_sums[1] = small_take(0)
+    small_start(1)
+    attention.act(0)
+    small_sums[2] = small_take(1)
+    small_start(2)
+    for s in range(STREAMS):
+        act(s, 3)
+    small_out[...] = small_take(2)
+    attention.act(1)
     piece_out[...] = att_bufs["acc"][mine]
     for copy in weights_come + forwards + [exchange]:
         copy.wait_send()
+    for turn in range(3):
+        for peer in range(small_counts[turn]):
+            small_copy(turn, peer).wait_send()
     for s in range(STREAMS):
         exchange_copy(s).wait_send()
-    for step in range(5):
-        small_copy(step).wait_send()
     gather.finish()
     attention.finish()
     for s in range(STREAMS):
-        halvings[s].finish()
-        doublings[s].finish()
+        sums[s].finish()
+        gathers[s].finish()
 
 
 def call_block(
@@ -1131,7 +1166,9 @@
         buffer = lambda free: pltpu.VMEM((2,) * free + (rows, 128), bf16)
         return {
             "acc": buffer(4), "out": buffer(4), "came": buffer(4),
-            "landing": [buffer(3), buffer(2), buffer(1), buffer(0)],
+            "landing": [
+                pltpu.VMEM((3, 2, 2, rows, 128), bf16), pltpu.VMEM((3, rows, 128), bf16),
+            ],
         }
 
     stacked = lambda free: pltpu.VMEM((STREAMS,) + (2,) * free + (BLOCK, 128), bf16)
@@ -1171,21 +1208,24 @@
         square=pltpu.VMEM((128, 128), f32),
         gqkv=pltpu.VMEM((WIDTH, 3 * WIDTH), f32),
         gproj=pltpu.VMEM((WIDTH, WIDTH), f32),
-        small_sums=pltpu.VMEM((5, SMALL, 128), f32),
-        small_landed=pltpu.VMEM((5, SMALL, 128), f32),
+        small_sums=pltpu.VMEM((3, SMALL, 128), f32),
+        small_landed=pltpu.VMEM((7, SMALL, 128), f32),
         streams_out=stacked(4),
         streams_came=stacked(4),
         streams_acc=stacked(4),
-        streams_landing=[stacked(free) for free in (3, 2, 1, 0)],
+        streams_landing=[
+            pltpu.VMEM((STREAMS, 3, 2, 2, BLOCK, 128), bf16),
+            pltpu.VMEM((STREAMS, 3, BLOCK, 128), bf16),
+        ],
         gconv=pltpu.VMEM((TAPS, STREAM), f32),
         att_bufs=bufs(PIECE),
         local_sems=pltpu.SemaphoreType.DMA((2,)),
-        gather_sems=pltpu.SemaphoreType.DMA((2, 3, 4)),
+        gather_sems=pltpu.SemaphoreType.DMA((2, 2, 2, 3)),
         gather_pair_sems=pltpu.SemaphoreType.DMA((2, 16)),
         stream_pair_sems=pltpu.SemaphoreType.DMA((2, STREAMS)),
-        stream_sems=pltpu.SemaphoreType.DMA((STREAMS, 2, 2, 3, 4)),
-        att_sems=pltpu.SemaphoreType.DMA((2, 3, 4)),
-        att_pair_sems=pltpu.SemaphoreType.DMA((2, 6)),
+        stream_sems=pltpu.SemaphoreType.DMA((STREAMS, 2, 2, 2, 2, 3)),
+        att_sems=pltpu.SemaphoreType.DMA((2, 2, 2, 3)),
+        att_pair_sems=pltpu.SemaphoreType.DMA((2, 8)),
     )
     return pl.pallas_call(
         block_kernel,

time: 114 us -> 103 us (0.904)
  Pallas kernels: 106 us -> 94.9 us
    pallas_call x1, Pallas kernels: 103 us -> 92 us  [call_block(): pl.pallas_call(block_kernel, in_specs=[smem] * 2 + [vmem] * 10 + [hbm] +...]
where the time goes in v4:
time: 103 us; the launch traced here: 102 us
  Pallas kernels  94.9 us (92%)
  local copies, waits for them, and re-layouts  6.5 us (6%)
    pallas_call x1, Pallas kernels, call_block(): pl.pallas_call(block_kernel, in_specs=[smem] * 2 + [vmem] * 10 + [hbm] +...  92 us
    unnamed x8, local copies, waits for them, and re-layouts  6.5 us
    pallas_call x1, Pallas kernels, call_finish(): pl.pallas_call(finish_kernel, in_specs=[vmem] * (STREAMS + 2), out_specs=...  2.89 us

profile of v4, /device:TPU:0, one launch (start us, length us, event | category | flops | bytes accessed | tf_op | source)
XLA Modules:
  0.0 102.3 jit_solution(7278536488465589407)
XLA Ops:
  0.6 0.0 copy-start.1
  0.7 2.0 %copy.39.tok = bf16[4,197,384]{2,1,0:T(8,128)(2,1)} copy(bf16[4,197,384]{2,0,1:T(4,128)(2,1)} %param.23) | data formatting | bytes 1210368 | tf_op args[0]
  2.7 0.0 copy-done.1
  2.7 0.9 copy.40.cot
  3.6 92.0 %block.1 = (bf16[4,197,384]{2,1,0:T(8,128)(2,1)}, f32[4,197,384]{2,1,0:T(8,128)}, bf16[2,2,2,2,112,128]{5,4,3,2,1,0:T(8,128)(2,1)}, bf16[2,2,2,2,112,128]{5,4,3,...) custom-call(f32[6,6]{1,0:T(8,128)} %pre.1, ...), custom_call_target="tpu_custom_call" | custom-call | tf_op jit(solution)/shard_map/block/pallas_call | solution.py:1230
  95.6 0.0 copy-start
  95.7 2.2 %copy.41 = bf16[4,197,384]{2,0,1:T(4,128)(2,1)} copy(bf16[4,197,384]{2,1,0:T(8,128)(2,1)} %get-tuple-element.58) | data formatting | bytes 1210368
  97.9 0.0 copy-done
  97.9 1.3 %copy.42 = f32[4,197,384]{2,0,1:T(4,128)} copy(f32[4,197,384]{2,1,0:T(8,128)S(1)} %copy-done) | data formatting | bytes 2420736
  99.2 2.9 %finish.1 = (f32[384,768]{1,0:T(8,128)}, f32[768]{0:T(1024)}, f32[49,768]{1,0:T(8,128)}, f32[768,384]{1,0:T(8,128)}, f32[24,576]{1,0:T(8,128)}, /*index=5*/f32[2...) custom-call(bf16[2,2,2,2,112,128]{5,4,3,2,1,0:T(8,128)(2,1)} %get-tu, ...), custom_call_target="tpu_custom_call" | custom-call | tf_op jit(solution)/shard_map/finish/pallas_call | solution.py:1287
Async XLA Ops:
  0.6 2.0 %copy-start.1 = (bf16[4,197,384]{2,0,1:T(4,128)(2,1)S(1)}, bf16[4,197,384]{2,0,1:T(4,128)(2,1)}, u32[]{:S(2)}) copy-start(bf16[4,197,384]{2,0,1:T(4,128)(2,1)} %param.38) | copy-start | bytes 1815556
  95.6 2.2 %copy-start = (f32[4,197,384]{2,1,0:T(8,128)S(1)}, f32[4,197,384]{2,1,0:T(8,128)}, u32[]{:S(2)}) copy-start(f32[4,197,384]{2,1,0:T(8,128)} %get-tuple-element.59) | copy-start | bytes 3631108

commit v5 on v4

--- a/solution.py
+++ b/solution.py
@@ -524,6 +524,11 @@
 BLOCK = 112
 BLOCK_PARTS = ((0, 80), (80, 32))
 STREAMS = 3
+MLP_PLAN = {(1, 4): ((0, -1),), (3, 4): ((1, -1), (0, 0)), (5, 4): ((2, -1), (0, 1), (1, 0))}
+BACK_PLAN = {
+    (0, 3): ((0, 2), (1, 1)), (1, 3): ((2, 0),), (2, 0): ((1, 2),), (2, 3): ((2, 1),),
+    (3, 3): ((2, 2),),
+}
 
 
 class Place:
@@ -684,18 +689,18 @@
 def block_kernel(
     pre, post, tok, cot, gain1, bias1, pbias, gain2, bias2, fc2b,
     qkv, proj, fc1, conv, bias, fc2, fwd, inv, kh, kl, bh, bl, one,
-    block_out, gtok_out, *rest,
+    block_out, gtok_out, fulls_out, piece_out, small_out, *rest,
 ):
-    fulls, (piece_out, small_out), rest = rest[:STREAMS], rest[STREAMS : STREAMS + 2], rest[STREAMS + 2 :]
     (
+        tok_held, cot_held, out_held, gtok_held, fulls_held,
         piece_full, piece_other, taps_pad, wqkv, wproj, fc1_full, fc2_full, conv_full,
         inputs, cot_pad, n1, packed, score, probs, attn, att, mid, n2,
         turned, ghat, hid, conv_low, ghid_low, gmid, gmid_low, gatt, low, gpacked, mix,
         rows_out, square, gqkv, gproj, small_sums, small_landed,
         streams_out, streams_came, streams_acc, streams_landing, gconv, att_bufs,
-        local_sems, gather_sems, gather_pair_sems, stream_pair_sems, stream_sems, att_sems, att_pair_sems,
+        local_sems, leave_sems, gather_sems, gather_pair_sems, stream_pair_sems, stream_sems, att_sems, att_pair_sems,
     ) = rest
-    images = tok.shape[0]
+    images = tok.shape[1]
     total = images * ROWS
     half = fc1.shape[1]
     where = Place()
@@ -706,6 +711,18 @@
     span = lambda b: slice(b * ROWS, (b + 1) * ROWS)
     spans = [span(b) for b in range(images)]
     inside = row_mask((ROWS, WIDTH))
+    fulls = [fulls_held.at[s] for s in range(STREAMS)]
+    local = [
+        pltpu.make_async_copy(src, dst, local_sems.at[index])
+        for index, (src, dst) in enumerate(
+            (
+                (tok, tok_held), (cot, cot_held), (fc2, fc2_full.at[rows_of]),
+                (fc1, fc1_full.at[:, cols]),
+            )
+        )
+    ]
+    for copy in local:
+        copy.start()
 
     both = jnp.concatenate([qkv[...].astype(f32), proj[...].astype(f32)], axis=1)
     piece_full[mine] = tiles(both).astype(bf16)
@@ -724,11 +741,7 @@
     forwards = [
         remote(piece_full.at[mine], piece_other.at[mine], gather_pair_sems, (3,), pair)
     ]
-    local = [
-        pltpu.make_async_copy(fc2, fc2_full.at[rows_of], local_sems.at[0]),
-        pltpu.make_async_copy(fc1, fc1_full.at[:, cols], local_sems.at[1]),
-    ]
-    for copy in weights_come + forwards + local:
+    for copy in weights_come + forwards:
         copy.start()
 
     def forward(part, turn, peer):
@@ -741,10 +754,14 @@
         forwards.append(copy)
 
     cot_sum = jnp.zeros((1, WIDTH), f32)
+    local[0].wait()
+    local[1].wait()
+    for source, ref in ((tok_held, inputs), (cot_held, gmid)):
+        flat = source[...].reshape(SEQ, images * WIDTH)
+        for b in range(images):
+            ref[b * ROWS + SEQ - 5 : (b + 1) * ROWS] = jnp.zeros((ROWS - SEQ + 5, WIDTH), f32)
+            ref[b * ROWS : b * ROWS + SEQ] = flat[:, b * WIDTH : (b + 1) * WIDTH].astype(f32)
     for b in range(images):
-        for source, ref in ((tok, inputs), (cot, gmid)):
-            ref[b * ROWS + SEQ - 5 : (b + 1) * ROWS] = jnp.zeros((ROWS - SEQ + 5, WIDTH), f32)
-            ref[b * ROWS : b * ROWS + SEQ] = source[b].astype(f32)
         grads = gmid[spans[b], :]
         cot_sum = cot_sum + add_rows(grads)
         cot_pad[spans[b], :] = grads.astype(bf16)
@@ -761,7 +778,7 @@
             ghat[b, :, units] = dot(fwd[...], hid[spans[b], :].astype(bf16))
 
     gather.act(0, forward)
-    for copy in local:
+    for copy in local[2:]:
         copy.wait()
     prepare(mine_start)
     for copy in weights_come:
@@ -869,6 +886,15 @@
         else:
             gathers[s].act(step - 2)
 
+    def poll(plan, index, spot):
+        for (turn, at), items in plan.items():
+            if at == spot:
+
+                @pl.when(index == turn)
+                def _():
+                    for item in items:
+                        act(*item)
+
     def blocks():
         filters = tiles(gconv[...])
         empty = jnp.zeros((BLOCK - 104, 128), f32)
@@ -893,20 +919,40 @@
         cross_r = jnp.zeros((HALF, STREAM), f32)
         cross_i = jnp.zeros((HALF, STREAM), f32)
         bias_sum = jnp.zeros((1, STREAM), f32)
-        for b in range(images):
+        held = {}
+
+        def stage_act(b):
             activated, slope = gelu_parts(hid[spans[b], :STREAM])
             hid[spans[b], :STREAM] = slope
-            x = dot(fwd[...], activated.astype(bf16))
+            held["act", b] = activated.astype(bf16)
+
+        def stage_turn(b):
+            held["x", b] = dot(fwd[...], held.pop(("act", b)))
+
+        def stage_mix(b):
+            x = held.pop(("x", b))
             xr, xi = x[:HALF], x[HALF:]
             yr, yi = ghat[b, :HALF, units], ghat[b, HALF:, units]
-            ahead = jnp.concatenate([xr * kr - xi * ki, xr * ki + xi * kr], axis=0).astype(bf16)
-            back = jnp.concatenate([yr * kr + yi * ki, yi * kr - yr * ki], axis=0).astype(bf16)
-            cross_r = cross_r + (xr * yr + xi * yi)
-            cross_i = cross_i + (xi * yr - xr * yi)
+            ahead = jnp.concatenate([xr * kr - xi * ki, xr * ki + xi * kr], axis=0)
+            back = jnp.concatenate([yr * kr + yi * ki, yi * kr - yr * ki], axis=0)
+            held["r"] = held["r"] + (xr * yr + xi * yi)
+            held["i"] = held["i"] + (xi * yr - xr * yi)
+            held["mix", b] = (ahead.astype(bf16), back.astype(bf16))
+
+        def stage_back(b):
+            ahead, back = held.pop(("mix", b))
             conv_low[spans[b], units] = dot(inv[...], ahead).astype(bf16)
             ghid = (dot(inv[...], back) * hid[spans[b], :STREAM]).astype(bf16)
-            bias_sum = bias_sum + add_rows(ghid.astype(f32))
+            held["bias"] = held["bias"] + add_rows(ghid.astype(f32))
             ghid_low[spans[b], units] = ghid
+
+        held["r"], held["i"], held["bias"] = cross_r, cross_i, bias_sum
+        stages = (stage_act, stage_turn, stage_mix, stage_back)
+        for beat in range(images + len(stages) - 1):
+            for depth in reversed(range(len(stages))):
+                if 0 <= beat - depth < images:
+                    stages[depth](beat - depth)
+        cross_r, cross_i, bias_sum = held["r"], held["i"], held["bias"]
         cross = jnp.concatenate([cross_r, cross_i], axis=0)
         high = cross.astype(bf16)
         low_part = (cross - high.astype(f32)).astype(bf16)
@@ -930,26 +976,17 @@
                 came = streams_came[(s,) + index].astype(f32)
                 streams_acc[(s,) + index] = (values + came).astype(bf16)
 
-        plan = {1: ((0, -1),), 3: ((0, 0), (1, -1)), 4: ((0, 1),), 5: ((2, -1), (1, 0), (0, 2))}
-        for turn, items in plan.items():
-
-            @pl.when(i == turn)
-            def _():
-                for item in items:
-                    act(*item)
-
+        poll(MLP_PLAN, i, images)
         return carry
 
     lax.fori_loop(0, 2 * STREAMS, mlp, 0)
 
     hid[:, :WIDTH] = dot_t(ghid_low[...], fc1_full[...])
-    hid[:, WIDTH:] = dot(conv_low[...], fc2_full[...])
     gain_sum = jnp.zeros((1, WIDTH), f32)
     bias_sum = jnp.zeros((1, WIDTH), f32)
     proj_sum = jnp.zeros((1, WIDTH), f32)
     for b in range(images):
         middle = mid[spans[b], :]
-        block_out[b] = (middle + (hid[spans[b], WIDTH:] + row(fc2b)))[:SEQ].astype(bf16)
         centred, r = centre(middle)
         grad = hid[spans[b], :WIDTH]
         back, gain_rows = norm_back(centred, r, row(gain2), grad)
@@ -960,24 +997,12 @@
         rounded = whole_grad.astype(bf16)
         proj_sum = proj_sum + add_rows(rounded.astype(f32))
         gmid_low[spans[b], :] = rounded
-    act(1, 1)
     gatt[...] = dot_t(gmid_low[...], wproj[...]).astype(bf16)
     mix[...] = jnp.zeros_like(mix)
 
     def fold(values):
         values = values[:, :128] + values[:, 128:]
         return values[:8] + values[8:]
-
-    plan = {(0, 3): ((1, 2), (2, 0)), (1, 3): ((2, 1),), (2, 3): ((2, 2),)}
-
-    def poll_at(b, spot):
-        for (image_index, at), items in plan.items():
-            if at == spot:
-
-                @pl.when(b == image_index)
-                def _():
-                    for item in items:
-                        act(*item)
 
     def put_weight(g, values):
         ghat[1, :ROWS, KEYS * g : KEYS * (g + 1)] = values
@@ -990,7 +1015,7 @@
             ahead = gatt[rows_of_image, 128 * p : 128 * p + 128]
             put_weight(2 * p, dot_t(jnp.where(low_half, ahead, zero), value))
             put_weight(2 * p + 1, dot_t(jnp.where(low_half, zero, ahead), value))
-        poll_at(b, 0)
+        poll(BACK_PLAN, b, 0)
 
         def back_step(step, carry):
             rows = pl.ds(pl.multiple_of(step * 16, 16), 16)
@@ -1016,9 +1041,9 @@
             return carry
 
         lax.fori_loop(0, 7, back_step, 0, unroll=7)
-        poll_at(b, 1)
+        poll(BACK_PLAN, b, 1)
         lax.fori_loop(7, ROWS // 16, back_step, 0, unroll=6)
-        poll_at(b, 2)
+        poll(BACK_PLAN, b, 2)
         queries, keys, values = [], [], []
         for p in range(HEADS // 2):
             query, key = section(b, 0, p, ROWS), section(b, 1, p)
@@ -1032,7 +1057,7 @@
                 )[:ROWS]
             )
         gpacked[rows_of_image, :] = jnp.concatenate(queries + keys + values, axis=1).astype(bf16)
-        poll_at(b, 3)
+        poll(BACK_PLAN, b, 3)
         return carry
 
     lax.fori_loop(0, images, back_image, 0)
@@ -1075,6 +1100,13 @@
                 att_bufs["acc"][index] = (values + came).astype(bf16)
 
     attention.start()
+    hid[:, WIDTH:] = dot(conv_low[...], fc2_full[...])
+    for b in range(images):
+        result = mid[spans[b], :] + (hid[spans[b], WIDTH:] + row(fc2b))
+        gtok_held[:, b, :] = result[:SEQ]
+    out_held[...] = gtok_held[...].astype(bf16)
+    leaving = [pltpu.make_async_copy(out_held, block_out, leave_sems.at[0])]
+    leaving[0].start()
     norm_gain = jnp.zeros((1, WIDTH), f32)
     norm_bias = jnp.zeros((1, WIDTH), f32)
     for b in range(images):
@@ -1083,7 +1115,9 @@
         back, gain_rows = norm_back(centred, r, row(gain1), grad)
         norm_gain = norm_gain + add_rows(gain_rows)
         norm_bias = norm_bias + add_rows(grad)
-        gtok_out[b] = (gmid[spans[b], :] + back)[:SEQ]
+        gtok_held[:, b, :] = (gmid[spans[b], :] + back)[:SEQ]
+    leaving.append(pltpu.make_async_copy(gtok_held, gtok_out, leave_sems.at[1]))
+    leaving[1].start()
     rows_out[...] = jnp.concatenate(
         [norm_gain, norm_bias, proj_sum, gain_sum, bias_sum, cot_sum, jnp.zeros((2, WIDTH), f32)],
         axis=0,
@@ -1126,9 +1160,13 @@
     small_start(2)
     for s in range(STREAMS):
         act(s, 3)
+    leaving.append(pltpu.make_async_copy(fulls_held, fulls_out, leave_sems.at[2]))
+    leaving[2].start()
     small_out[...] = small_take(2)
     attention.act(1)
     piece_out[...] = att_bufs["acc"][mine]
+    for copy in leaving:
+        copy.wait()
     for copy in weights_come + forwards + [exchange]:
         copy.wait_send()
     for turn in range(3):
@@ -1146,7 +1184,7 @@
 def call_block(
     pre, post, tok, cot, gain1, bias1, pbias, gain2, bias2, fc2b, qkv, proj, fc1, conv, bias, fc2
 ):
-    images, half = tok.shape[0], fc1.shape[1]
+    images, half = tok.shape[1], fc1.shape[1]
     units, total = 2 * half, images * ROWS
     forward, inverse, kernel, back, one = fourier()
     kernel_high, kernel_low = split(kernel)
@@ -1175,6 +1213,11 @@
     tall = lambda width, dtype: pltpu.VMEM((total, width), dtype)
     cube = lambda dtype: pltpu.VMEM((HEADS, ROWS, KEYS), dtype)
     scratch = dict(
+        tok_held=pltpu.VMEM(tok.shape, bf16),
+        cot_held=pltpu.VMEM(tok.shape, bf16),
+        out_held=pltpu.VMEM(tok.shape, bf16),
+        gtok_held=pltpu.VMEM(tok.shape, f32),
+        fulls_held=stacked(4),
         piece_full=pltpu.VMEM((2, 2, 2, 2, PIECE, 128), bf16),
         piece_other=pltpu.VMEM((2, 2, 2, 2, PIECE, 128), bf16),
         taps_pad=pltpu.VMEM((TAPS, half), f32),
@@ -1219,7 +1262,8 @@
         ],
         gconv=pltpu.VMEM((TAPS, STREAM), f32),
         att_bufs=bufs(PIECE),
-        local_sems=pltpu.SemaphoreType.DMA((2,)),
+        local_sems=pltpu.SemaphoreType.DMA((10,)),
+        leave_sems=pltpu.SemaphoreType.DMA((3,)),
         gather_sems=pltpu.SemaphoreType.DMA((2, 2, 2, 3)),
         gather_pair_sems=pltpu.SemaphoreType.DMA((2, 16)),
         stream_pair_sems=pltpu.SemaphoreType.DMA((2, STREAMS)),
@@ -1229,14 +1273,14 @@
     )
     return pl.pallas_call(
         block_kernel,
-        in_specs=[smem] * 2 + [vmem] * 10 + [hbm] + [vmem] * 2 + [hbm] + [vmem] * len(consts),
-        out_specs=[vmem] * (4 + STREAMS),
+        in_specs=[smem] * 2 + [hbm] * 2 + [vmem] * 8 + [hbm] + [vmem] * 2 + [hbm] + [vmem] * len(consts),
+        out_specs=[hbm] * 3 + [vmem] * 2,
         out_shape=[
             jax.ShapeDtypeStruct(tok.shape, bf16),
             jax.ShapeDtypeStruct(tok.shape, f32),
         ]
-        + [jax.ShapeDtypeStruct((2, 2, 2, 2, BLOCK, 128), bf16)] * STREAMS
         + [
+            jax.ShapeDtypeStruct((STREAMS, 2, 2, 2, 2, BLOCK, 128), bf16),
             jax.ShapeDtypeStruct((PIECE, 128), bf16),
             jax.ShapeDtypeStruct((SMALL, 128), f32),
         ],
@@ -1252,19 +1296,26 @@
 
 
 def finish_kernel(
-    t0, t1, t2, piece, small, gfc1, gb1, gconv, gfc2, gqkv, gproj, g1, b1, pb, g2, b2, fb,
-    pre, post, taps, mixes,
+    totals_in, piece, small, out_in, gtok_in, gfc1_out, gb1, gconv, gfc2_out, gqkv, gproj, g1, b1,
+    pb, g2, b2, fb, pre, post, out, gtok, totals, out_held, gtok_held, gfc1, gfc2, taps, mixes,
+    sems,
 ):
-    for s, total in enumerate((t0, t1, t2)):
-        side = slice(s * STREAM, (s + 1) * STREAM)
-        for d in range(16):
-            block = total[index_of(d)].astype(f32)
-            gfc1[24 * d : 24 * d + 24, side] = untiles(block[:48], 2)
-            gfc2[s * STREAM + 16 * d : s * STREAM + 16 * d + 16, :] = untiles(block[48:96], 3)
-            taps[8 * d : 8 * d + 8, :] = block[96:104]
-        filters = untiles(taps[...], 2)
-        gconv[:, side] = filters[: KS * KS]
-        gb1[side] = filters[KS * KS]
+    coming = [
+        pltpu.make_async_copy(totals_in.at[s], totals.at[s], sems.at[s]) for s in range(STREAMS)
+    ]
+    coming += [
+        pltpu.make_async_copy(gtok_in, gtok_held, sems.at[STREAMS]),
+        pltpu.make_async_copy(out_in, out_held, sems.at[STREAMS + 1]),
+    ]
+    for copy in coming:
+        copy.start()
+    leaving = []
+
+    def leave(src, dst):
+        copy = pltpu.make_async_copy(src, dst, sems.at[STREAMS + 2 + len(leaving)])
+        copy.start()
+        leaving.append(copy)
+
     both = untiles(piece[...].astype(f32), 6)
     width = gqkv.shape[1]
     gqkv[...] = both[:, :width]
@@ -1279,25 +1330,53 @@
             mixes[index, g : g + 1, :HEADS] = line[:, start : start + HEADS]
     pre[...] = mixes[0, :HEADS, :HEADS] * 0.125
     post[...] = mixes[1, :HEADS, :HEADS]
-
-
-def call_finish(totals, piece, small, half):
+    for s in range(STREAMS):
+        side = slice(s * STREAM, (s + 1) * STREAM)
+        coming[s].wait()
+        for d in range(16):
+            block = totals[(s,) + index_of(d)].astype(f32)
+            gfc1[24 * d : 24 * d + 24, side] = untiles(block[:48], 2)
+            gfc2[s * STREAM + 16 * d : s * STREAM + 16 * d + 16, :] = untiles(block[48:96], 3)
+            taps[8 * d : 8 * d + 8, :] = block[96:104]
+        leave(gfc2.at[side], gfc2_out.at[side])
+        leave(gfc1.at[:, side], gfc1_out.at[:, side])
+        filters = untiles(taps[...], 2)
+        gconv[:, side] = filters[: KS * KS]
+        gb1[side] = filters[KS * KS]
+        if s == 0:
+            coming[STREAMS].wait()
+            leave(gtok_held, gtok)
+            coming[STREAMS + 1].wait()
+            leave(out_held, out)
+    for copy in leaving:
+        copy.wait()
+
+
+def call_finish(totals, piece, small, block_out, gtok, half):
+    hbm = pl.BlockSpec(memory_space=pl.ANY)
     vmem = pl.BlockSpec(memory_space=pltpu.VMEM)
     shape = lambda *dims: jax.ShapeDtypeStruct(dims, f32)
     return pl.pallas_call(
         finish_kernel,
-        in_specs=[vmem] * (STREAMS + 2),
-        out_specs=[vmem] * 14,
+        in_specs=[hbm] + [vmem] * 2 + [hbm] * 2,
+        out_specs=[hbm] + [vmem] * 2 + [hbm] + [vmem] * 10 + [hbm] * 2,
         out_shape=[
             shape(WIDTH, half), shape(half), shape(KS * KS, half), shape(half, WIDTH),
             shape(24, 3 * WIDTH // 2), shape(24, WIDTH // 2),
         ]
         + [shape(WIDTH)] * 6
-        + [shape(HEADS, HEADS)] * 2,
-        scratch_shapes=[pltpu.VMEM((128, 128), f32), pltpu.VMEM((2, 8, 128), f32)],
+        + [shape(HEADS, HEADS)] * 2
+        + [jax.ShapeDtypeStruct(v.shape, v.dtype) for v in (block_out, gtok)],
+        scratch_shapes=[
+            pltpu.VMEM(totals.shape, bf16),
+            pltpu.VMEM(block_out.shape, bf16), pltpu.VMEM(gtok.shape, f32),
+            pltpu.VMEM((WIDTH, half), f32), pltpu.VMEM((half, WIDTH), f32),
+            pltpu.VMEM((128, 128), f32), pltpu.VMEM((2, 8, 128), f32),
+            pltpu.SemaphoreType.DMA((STREAMS + 2 + 2 * STREAMS + 2,)),
+        ],
         compiler_params=pltpu.CompilerParams(vmem_limit_bytes=VMEM),
         name="finish",
-    )(*totals, piece, small)
+    )(totals, piece, small, block_out, gtok)
 
 
 def shards_any(
@@ -1337,14 +1416,16 @@
     tokens, norm1_gain, norm1_bias, qkv_weight, mix_pre, mix_post, proj_weight, proj_bias,
     norm2_gain, norm2_bias, fc1_weight, fc1_bias, conv_weight, fc2_weight, fc2_bias, cotangent,
 ):
-    block_out, gtok, t0, t1, t2, piece, small = call_block(
-        mix_pre, mix_post, tokens, cotangent, norm1_gain, norm1_bias, proj_bias, norm2_gain,
+    turn = lambda v: jnp.transpose(v, (1, 0, 2))
+    block_out, gtok, totals, piece, small = call_block(
+        mix_pre, mix_post, turn(tokens), turn(cotangent), norm1_gain, norm1_bias, proj_bias, norm2_gain,
         norm2_bias, fc2_bias, qkv_weight, proj_weight, fc1_weight, conv_weight, fc1_bias,
         fc2_weight,
     )
-    gfc1, gb1, gconv, gfc2, gqkv, gproj, g1, b1, pb, g2, b2, fb, pre, post = call_finish(
-        (t0, t1, t2), piece, small, fc1_weight.shape[1]
-    )
+    (
+        gfc1, gb1, gconv, gfc2, gqkv, gproj, g1, b1, pb, g2, b2, fb, pre, post, block_out, gtok
+    ) = call_finish(totals, piece, small, block_out, gtok, fc1_weight.shape[1])
+    block_out, gtok = turn(block_out), turn(gtok)
     return (
         block_out, gtok, g1, b1, gqkv, pre, post, gproj, pb, g2, b2, gfc1, gb1, gconv, gfc2, fb
     )

time: 103 us -> 91.1 us (0.88)
  local copies, waits for them, and re-layouts: 6.5 us -> 0 us
  Pallas kernels: 94.9 us -> 90 us
    unnamed x8 -> x0, local copies, waits for them, and re-layouts: 6.5 us -> none
    pallas_call x2, Pallas kernels: 94.9 us -> 90 us  [the longest x1 84.9 us: call_block(): pl.pallas_call(block_kernel, in_specs=[smem] * 2 + [hbm] * 2 + [vmem] * 8...]
where the time goes in v5:
time: 91.1 us; the launch traced here: 90.8 us
  Pallas kernels  90 us (99%)
    pallas_call x1, Pallas kernels, call_block(): pl.pallas_call(block_kernel, in_specs=[smem] * 2 + [hbm] * 2 + [vmem] * 8...  84.9 us
    pallas_call x1, Pallas kernels, call_finish(): pl.pallas_call(finish_kernel, in_specs=[hbm] + [vmem] * 2 + [hbm] * 2, ou...  5.05 us

profile of v5, /device:TPU:0, one launch (start us, length us, event | category | flops | bytes accessed | tf_op | source)
XLA Modules:
  0.0 90.8 jit_solution(815304672944117174)
XLA Ops:
  0.7 84.9 %block.1 = (bf16[197,4,384]{2,1,0:T(4,128)(2,1)}, f32[197,4,384]{2,1,0:T(4,128)}, bf16[3,2,2,2,2,112,128]{6,5,4,3,2,1,0:T(8,128)(2,1)}, bf16[144,128]{1,0:T(8,128)(2,1)}, f32[32,128]{1,0:T(8,128)}) custom-call(f32[6,6]{1,0:T(8,128)} %pre.1, f32[6,6]{1,0:T(8,128)} %post.1, bf16[197,4,384]{2,1,0:T(4,128)(2,1)} %bitcast.4, bf16[197,4,384]{2,1,0:T(4,128)(2,1)} %bitcast.5, ...), custom_call_target="tpu_custom_call" | custom-call | tf_op jit(solution)/shard_map/block/pallas_call | solution.py:1274
  85.6 5.1 %finish.1 = (f32[384,768]{1,0:T(8,128)}, f32[768]{0:T(1024)}, f32[49,768]{1,0:T(8,128)}, f32[768,384]{1,0:T(8,128)}, f32[24,576]{1,0:T(8,128)}, /*index=5*/f32[2...) custom-call(bf16[3,2,2,2,2,112,128]{6,5,4,3,2,1,0:T(8,128)(2,1)} %ge, ...), custom_call_target="tpu_custom_call" | custom-call | tf_op jit(solution)/shard_map/finish/pallas_call | solution.py:1359

commit v6 on v5

--- a/solution.py
+++ b/solution.py
@@ -18,7 +18,7 @@
 TAPS = 64
 KEYS = 256
 WIDTH = 384
-HALF = 152
+HALF = 160
 COEFS = 2 * HALF
 CLASS_ROW = 145
 CHUNK = 512
@@ -526,9 +526,9 @@
 STREAMS = 3
 MLP_PLAN = {(1, 4): ((0, -1),), (3, 4): ((1, -1), (0, 0)), (5, 4): ((2, -1), (0, 1), (1, 0))}
 BACK_PLAN = {
-    (0, 3): ((0, 2), (1, 1)), (1, 3): ((2, 0),), (2, 0): ((1, 2),), (2, 3): ((2, 1),),
-    (3, 3): ((2, 2),),
+    (0, 3): ((0, 2), (1, 1)), (1, 1): ((2, 0),), (1, 2): ((1, 2),), (1, 3): ((2, 1),),
 }
+TAIL_PLAN = ()
 
 
 class Place:
@@ -557,11 +557,11 @@
         return peers + [self.pair]
 
 
-def meet(partners):
+def greet(partners):
     barrier = pltpu.get_barrier_semaphore()
     for partner in partners:
         pl.semaphore_signal(barrier, inc=1, device_id=partner, device_id_type=MESH_IDS)
-    pl.semaphore_wait(barrier, len(partners))
+    return lambda: pl.semaphore_wait(barrier, len(partners))
 
 
 def remote(src, dst, sems, index, device):
@@ -681,6 +681,12 @@
     )
 
 
+def weave(*lists):
+    steps = [((k + 0.5) / len(one), step) for one in lists for k, step in enumerate(one)]
+    for _, step in sorted(steps, key=lambda item: item[0]):
+        step()
+
+
 def untiles(values, count):
     rows = values.shape[0] // count
     return jnp.concatenate([values[t * rows : (t + 1) * rows] for t in range(count)], axis=1)
@@ -688,16 +694,16 @@
 
 def block_kernel(
     pre, post, tok, cot, gain1, bias1, pbias, gain2, bias2, fc2b,
-    qkv, proj, fc1, conv, bias, fc2, fwd, inv, kh, kl, bh, bl, one,
+    qkv, proj, fc1, conv, bias, fc2, fwd_in, inv_in, kh_in, kl_in, bh_in, bl_in, one,
     block_out, gtok_out, fulls_out, piece_out, small_out, *rest,
 ):
     (
-        tok_held, cot_held, out_held, gtok_held, fulls_held,
-        piece_full, piece_other, taps_pad, wqkv, wproj, fc1_full, fc2_full, conv_full,
-        inputs, cot_pad, n1, packed, score, probs, attn, att, mid, n2,
-        turned, ghat, hid, conv_low, ghid_low, gmid, gmid_low, gatt, low, gpacked, mix,
+        tok_held, cot_held, out_held, gtok_held, out_wide, fwd, inv, kh, kl, bh, bl,
+        piece_full, piece_other, taps_pad, wqkv, wproj, fc1_blocks, fc2_full, conv_full,
+        cot_pad, n1, packed, score, weight, probs, attn, att, mid, n2,
+        turned, ghat, hid, hidden, slope, acted, weights, conv_low, ghid_low, gmid, gmid_low, gatt, low, gpacked, mix,
         rows_out, square, gqkv, gproj, small_sums, small_landed,
-        streams_out, streams_came, streams_acc, streams_landing, gconv, att_bufs,
+        streams_out, streams_came, streams_acc, streams_landing, gconv, made, ahead, behind, cross, att_bufs,
         local_sems, leave_sems, gather_sems, gather_pair_sems, stream_pair_sems, stream_sems, att_sems, att_pair_sems,
     ) = rest
     images = tok.shape[1]
@@ -705,19 +711,22 @@
     half = fc1.shape[1]
     where = Place()
     pair, core, mine = where.pair, where.core, where.bits
+    met = greet(where.everyone())
     mine_start = pl.multiple_of(core * half, 128)
-    other_start = pl.multiple_of((1 - core) * half, 128)
     cols, rows_of = pl.ds(mine_start, half), pl.ds(mine_start, half)
     span = lambda b: slice(b * ROWS, (b + 1) * ROWS)
     spans = [span(b) for b in range(images)]
     inside = row_mask((ROWS, WIDTH))
-    fulls = [fulls_held.at[s] for s in range(STREAMS)]
+    fulls = [streams_came.at[s] for s in range(STREAMS)]
+    sides = [(s, pl.ds(s * STREAM, STREAM)) for s in range(STREAMS)]
     local = [
         pltpu.make_async_copy(src, dst, local_sems.at[index])
         for index, (src, dst) in enumerate(
             (
                 (tok, tok_held), (cot, cot_held), (fc2, fc2_full.at[rows_of]),
-                (fc1, fc1_full.at[:, cols]),
+                (fwd_in, fwd), (kh_in, kh), (kl_in, kl),
+                *((fc1.at[:, side], fc1_blocks.at[core * STREAMS + s]) for s, side in sides),
+                (inv_in, inv), (bh_in, bh), (bl_in, bl),
             )
         )
     ]
@@ -730,16 +739,23 @@
     taps_pad[: KS * KS] = conv[...].astype(f32)
     taps_pad[KS * KS : KS * KS + 1] = bias[...].astype(f32).reshape(1, half)
     conv_full[:, cols] = taps_pad[...].astype(bf16)
-    meet(where.everyone())
+    met()
     gather = Gather(piece_full, gather_sems, PIECE_PARTS, where)
     gather.start()
     weights_come = [
         remote(conv_full.at[:, cols], conv_full.at[:, cols], gather_pair_sems, (0,), pair),
         remote(fc2, fc2_full.at[rows_of], gather_pair_sems, (1,), pair),
-        remote(fc1, fc1_full.at[:, cols], gather_pair_sems, (2,), pair),
+        *(
+            remote(
+                fc1.at[:, side], fc1_blocks.at[core * STREAMS + s], gather_pair_sems, (2 + s,), pair
+            )
+            for s, side in sides
+        ),
     ]
     forwards = [
-        remote(piece_full.at[mine], piece_other.at[mine], gather_pair_sems, (3,), pair)
+        remote(
+            piece_full.at[mine], piece_other.at[mine], gather_pair_sems, (2 + STREAMS,), pair
+        )
     ]
     for copy in weights_come + forwards:
         copy.start()
@@ -748,7 +764,7 @@
         spot = gather.spot(part, turn, FLIPS[peer])
         copy = remote(
             piece_full.at[spot], piece_other.at[spot], gather_pair_sems,
-            (4 + 6 * part + 3 * turn + peer,), pair,
+            (3 + STREAMS + 6 * part + 3 * turn + peer,), pair,
         )
         copy.start()
         forwards.append(copy)
@@ -756,7 +772,7 @@
     cot_sum = jnp.zeros((1, WIDTH), f32)
     local[0].wait()
     local[1].wait()
-    for source, ref in ((tok_held, inputs), (cot_held, gmid)):
+    for source, ref in ((tok_held, mid), (cot_held, gmid)):
         flat = source[...].reshape(SEQ, images * WIDTH)
         for b in range(images):
             ref[b * ROWS + SEQ - 5 : (b + 1) * ROWS] = jnp.zeros((ROWS - SEQ + 5, WIDTH), f32)
@@ -766,24 +782,29 @@
         cot_sum = cot_sum + add_rows(grads)
         cot_pad[spans[b], :] = grads.astype(bf16)
     for b in range(images):
-        centred, r = centre(inputs[spans[b], :])
+        centred, r = centre(mid[spans[b], :])
         n1[spans[b], :] = jnp.where(inside, centred * r * row(gain1) + row(bias1), 0.0).astype(bf16)
 
-    def prepare(start):
-        units = pl.ds(start, half)
-        taps = conv_full[:, units]
-        turned[:, units] = dot(kh[...], taps) + dot(kl[...], taps) + one[...]
-        hid[...] = dot_t(cot_pad[...], fc2_full[units, :])
-        for b in range(images):
-            ghat[b, :, units] = dot(fwd[...], hid[spans[b], :].astype(bf16))
+    def prepare(side):
+        def prepare_unit(s, carry):
+            block = side * STREAMS + s
+            units = pl.ds(pl.multiple_of(block * STREAM, STREAM), STREAM)
+            taps = conv_full[:, units]
+            turned[block] = dot(kh[...], taps) + dot(kl[...], taps) + one[...]
+            grads = dot_t(cot_pad[...], fc2_full[units, :]).astype(bf16)
+            for b in range(images):
+                ghat[block, b] = dot(fwd[...], grads[spans[b]]).astype(bf16)
+            return carry
+
+        lax.fori_loop(0, STREAMS, prepare_unit, 0)
 
     gather.act(0, forward)
     for copy in local[2:]:
         copy.wait()
-    prepare(mine_start)
+    prepare(core)
     for copy in weights_come:
         copy.wait_recv()
-    prepare(other_start)
+    prepare(1 - core)
     gather.act(1, forward)
     for copy in forwards:
         copy.wait_recv()
@@ -803,62 +824,85 @@
     for n in range(0, 3 * WIDTH, WIDTH):
         gpacked[:, n : n + WIDTH] = dot(n1[...], wqkv[:, n : n + WIDTH]).astype(bf16)
     for b in range(images):
-        packed[b, :ROWS] = gpacked[spans[b], :]
-        packed[b, ROWS:] = jnp.zeros((KEYS - ROWS, 3 * WIDTH), bf16)
+        packed[b % 2][b // 2, :ROWS] = gpacked[spans[b], :]
+        packed[b % 2][b // 2, ROWS:] = jnp.zeros((KEYS - ROWS, 3 * WIDTH), bf16)
     low_half = lax.broadcasted_iota(jnp.int32, (ROWS, 128), 1) < HEAD_DIM
     key_half = lax.broadcasted_iota(jnp.int32, (KEYS, 128), 1) < HEAD_DIM
     zero = jnp.zeros((ROWS, 128), bf16)
     valid = lax.broadcasted_iota(jnp.int32, (16, KEYS), 1) < SEQ
 
-    def section(b, which, pair_of_heads, count=KEYS):
+    def section(q, side, which, pair_of_heads, count=KEYS):
         start = which * WIDTH + 128 * pair_of_heads
-        return packed[b, :count, start : start + 128]
-
-    def find_scores(b):
-        for p in range(HEADS // 2):
-            query, key = section(b, 0, p, ROWS), section(b, 1, p)
-            score[2 * p] = dot_t(jnp.where(low_half, query, zero), key)
-            score[2 * p + 1] = dot_t(jnp.where(low_half, zero, query), key)
-
-    def attend(b, carry):
-        find_scores(b)
-
-        def rows_step(step, carry):
-            rows = pl.ds(pl.multiple_of(step * 16, 16), 16)
-            scores = [score[h, rows, :] for h in range(HEADS)]
-            found = []
-            for g in range(HEADS):
-                mixed = scores[0] * (pre[g, 0] * 0.125)
-                for h in range(1, HEADS):
-                    mixed = mixed + scores[h] * (pre[g, h] * 0.125)
-                mixed = jnp.where(valid, mixed, -1e30)
-                top = jnp.max(mixed, axis=-1, keepdims=True)
-                raised = jnp.exp(mixed - top)
-                prob = raised * (1.0 / jnp.sum(raised, axis=-1, keepdims=True))
-                probs[b, g, rows, :] = prob
-                found.append(prob)
-            for g in range(HEADS):
-                mixed = found[0] * post[g, 0]
-                for h in range(1, HEADS):
-                    mixed = mixed + found[h] * post[g, h]
-                attn[b, g, rows, :] = mixed.astype(bf16)
-            return carry
-
-        lax.fori_loop(0, ROWS // 16, rows_step, 0, unroll=ROWS // 16)
-        pieces = []
-        for p in range(HEADS // 2):
-            value = section(b, 2, p)
-            pieces.append(
-                jnp.where(low_half, dot(attn[b, 2 * p], value), dot(attn[b, 2 * p + 1], value))
+        return packed[side][q, :count, start : start + 128]
+
+    def rows_at(q, side):
+        return pl.ds(pl.multiple_of((2 * q + side) * ROWS, 16), ROWS)
+
+    def skewed(q, stages, after=None):
+        for beat in range(2 + max(depth for depth, _ in stages)):
+            weave(
+                *[
+                    [functools.partial(step, q, beat - depth) for step in steps]
+                    for depth, steps in stages
+                    if 0 <= beat - depth < 2
+                ]
             )
-        rows = pl.ds(pl.multiple_of(b * ROWS, 16), ROWS)
-        att[rows, :] = jnp.concatenate(pieces, axis=1).astype(bf16)
+            if after is not None:
+                after(beat)
+
+    pairs = range(HEADS // 2)
+    row_blocks = [slice(r, r + 16) for r in range(0, ROWS, 16)]
+
+    def products(left, right, target, p):
+        target[2 * p] = dot_t(jnp.where(low_half, left, zero), right)
+        target[2 * p + 1] = dot_t(jnp.where(low_half, zero, left), right)
+
+    def score_step(p, q, side):
+        products(section(q, side, 0, p, ROWS), section(q, side, 1, p), score[side], p)
+
+    def softmax_rows(rows, q, side):
+        scores = [score[side][h, rows, :] for h in range(HEADS)]
+        found = []
+        for g in range(HEADS):
+            mixed = scores[0] * (pre[g, 0] * 0.125)
+            for h in range(1, HEADS):
+                mixed = mixed + scores[h] * (pre[g, h] * 0.125)
+            mixed = jnp.where(valid, mixed, -1e30)
+            top = jnp.max(mixed, axis=-1, keepdims=True)
+            raised = jnp.exp(mixed - top)
+            prob = raised * (1.0 / jnp.sum(raised, axis=-1, keepdims=True))
+            probs[side][q, g, rows, :] = prob
+            found.append(prob)
+        for g in range(HEADS):
+            mixed = found[0] * post[g, 0]
+            for h in range(1, HEADS):
+                mixed = mixed + found[h] * post[g, h]
+            attn[side][q, g, rows, :] = mixed.astype(bf16)
+
+    def out_step(p, q, side):
+        value = section(q, side, 2, p)
+        even, odd = dot(attn[side][q, 2 * p], value), dot(attn[side][q, 2 * p + 1], value)
+        att[rows_at(q, side), 128 * p : 128 * p + 128] = jnp.where(low_half, even, odd).astype(
+            bf16
+        )
+
+    def each(function, items):
+        return [functools.partial(function, item) for item in items]
+
+    def attend(q, carry):
+        skewed(
+            q,
+            (
+                (0, each(score_step, pairs)), (1, each(softmax_rows, row_blocks)),
+                (2, each(out_step, pairs)),
+            ),
+        )
         return carry
 
-    lax.fori_loop(0, images, attend, 0)
-    branch = dot(att[...], wproj[...])
+    lax.fori_loop(0, images // 2, attend, 0)
+    hid[...] = dot(att[...], wproj[...])
     for b in range(images):
-        middle = inputs[spans[b], :] + (branch[spans[b]] + row(pbias))
+        middle = mid[spans[b], :] + (hid[spans[b], :] + row(pbias))
         mid[spans[b], :] = middle
         centred, r = centre(middle)
         n2[spans[b], :] = jnp.where(inside, centred * r * row(gain2) + row(bias2), 0.0).astype(bf16)
@@ -902,7 +946,7 @@
             yield index_of(d), jnp.concatenate(
                 [
                     tiles(gqkv[24 * d : 24 * d + 24, :STREAM]),
-                    tiles(hid[16 * d : 16 * d + 16, :WIDTH]),
+                    tiles(hid[16 * d : 16 * d + 16]),
                     filters[8 * d : 8 * d + 8],
                     empty,
                 ],
@@ -912,56 +956,80 @@
     def mlp(i, carry):
         s, own = i // 2, lax.rem(i, 2)
         owner = (1 - core) * (1 - own) + core * own
-        units = pl.ds(pl.multiple_of((owner * STREAMS + s) * STREAM, STREAM), STREAM)
+        unit = owner * STREAMS + s
+        units = pl.ds(pl.multiple_of(unit * STREAM, STREAM), STREAM)
         bias_row = conv_full[:, units].astype(f32)[KS * KS : KS * KS + 1]
-        hid[:, :STREAM] = dot(n2[...], fc1_full[:, units]) + bias_row
-        kr, ki = turned[:HALF, units], turned[HALF:, units]
-        cross_r = jnp.zeros((HALF, STREAM), f32)
-        cross_i = jnp.zeros((HALF, STREAM), f32)
-        bias_sum = jnp.zeros((1, STREAM), f32)
-        held = {}
-
-        def stage_act(b):
-            activated, slope = gelu_parts(hid[spans[b], :STREAM])
-            hid[spans[b], :STREAM] = slope
-            held["act", b] = activated.astype(bf16)
-
-        def stage_turn(b):
-            held["x", b] = dot(fwd[...], held.pop(("act", b)))
-
-        def stage_mix(b):
-            x = held.pop(("x", b))
-            xr, xi = x[:HALF], x[HALF:]
-            yr, yi = ghat[b, :HALF, units], ghat[b, HALF:, units]
-            ahead = jnp.concatenate([xr * kr - xi * ki, xr * ki + xi * kr], axis=0)
-            back = jnp.concatenate([yr * kr + yi * ki, yi * kr - yr * ki], axis=0)
-            held["r"] = held["r"] + (xr * yr + xi * yi)
-            held["i"] = held["i"] + (xi * yr - xr * yi)
-            held["mix", b] = (ahead.astype(bf16), back.astype(bf16))
-
-        def stage_back(b):
-            ahead, back = held.pop(("mix", b))
-            conv_low[spans[b], units] = dot(inv[...], ahead).astype(bf16)
-            ghid = (dot(inv[...], back) * hid[spans[b], :STREAM]).astype(bf16)
-            held["bias"] = held["bias"] + add_rows(ghid.astype(f32))
-            ghid_low[spans[b], units] = ghid
-
-        held["r"], held["i"], held["bias"] = cross_r, cross_i, bias_sum
-        stages = (stage_act, stage_turn, stage_mix, stage_back)
+        weights[...] = fc1_blocks[unit]
+        sums_of = {"bias": jnp.zeros((8, STREAM), f32)}
+
+        def first(b, start, count):
+            rows = slice(b * ROWS + start, b * ROWS + start + count)
+            hidden[b % 2][start : start + count] = dot(n2[rows, :], weights[...]) + bias_row
+
+        def activate(b, start):
+            rows = slice(start, start + 16)
+            activated, slopes = gelu_parts(hidden[b % 2][rows])
+            slope[b][rows] = slopes
+            acted[b % 2][rows] = activated.astype(bf16)
+
+        def transform(b, start, count):
+            made[b % 2][start : start + count] = dot(
+                fwd[start : start + count], acted[b % 2][...]
+            )
+
+        def multiply(b, start):
+            real, imag = slice(start, start + 16), slice(HALF + start, HALF + start + 16)
+            xr, xi = made[b % 2][real], made[b % 2][imag]
+            yr, yi = ghat[unit, b, real].astype(f32), ghat[unit, b, imag].astype(f32)
+            kr, ki = turned[unit, real], turned[unit, imag]
+            ahead[b % 2][real] = (xr * kr - xi * ki).astype(bf16)
+            ahead[b % 2][imag] = (xr * ki + xi * kr).astype(bf16)
+            behind[b % 2][real] = (yr * kr + yi * ki).astype(bf16)
+            behind[b % 2][imag] = (yi * kr - yr * ki).astype(bf16)
+            cross_r, cross_i = xr * yr + xi * yi, xi * yr - xr * yi
+            if b > 0:
+                cross_r, cross_i = cross[real] + cross_r, cross[imag] + cross_i
+            cross[real], cross[imag] = cross_r, cross_i
+
+        def invert(b, start, count):
+            near = slice(start, start + count)
+            rows = slice(b * ROWS + start, b * ROWS + start + count)
+            part = inv[near]
+            conv_low[unit, rows] = dot(part, ahead[b % 2][...]).astype(bf16)
+            ghid = (dot(part, behind[b % 2][...]) * slope[b][near]).astype(bf16)
+            ghid_low[unit, rows] = ghid
+            rounded = ghid.astype(f32)
+            total = sums_of["bias"]
+            for r in range(0, count, 8):
+                total = total + rounded[r : r + 8]
+            sums_of["bias"] = total
+
+        stages = (
+            lambda b: [functools.partial(first, b, 0, ROWS)],
+            lambda b: [functools.partial(activate, b, start) for start in range(0, ROWS, 16)],
+            lambda b: [
+                functools.partial(transform, b, start, HALF) for start in (0, HALF)
+            ],
+            lambda b: [functools.partial(multiply, b, start) for start in range(0, HALF, 16)],
+            lambda b: [functools.partial(invert, b, *block) for block in ((0, 112), (112, 96))],
+        )
         for beat in range(images + len(stages) - 1):
-            for depth in reversed(range(len(stages))):
-                if 0 <= beat - depth < images:
-                    stages[depth](beat - depth)
-        cross_r, cross_i, bias_sum = held["r"], held["i"], held["bias"]
-        cross = jnp.concatenate([cross_r, cross_i], axis=0)
-        high = cross.astype(bf16)
-        low_part = (cross - high.astype(f32)).astype(bf16)
+            weave(
+                *[
+                    stage(beat - depth)
+                    for depth, stage in enumerate(stages)
+                    if 0 <= beat - depth < images
+                ]
+            )
+        bias_sum = add_rows(sums_of["bias"])
+        high = cross[...].astype(bf16)
+        low_part = (cross[...] - high.astype(f32)).astype(bf16)
         last = lax.broadcasted_iota(jnp.int32, (TAPS, STREAM), 0) == KS * KS
         gconv[...] = jnp.where(
             last, bias_sum, dot(bh[...], high) + dot(bl[...], high) + dot(bh[...], low_part)
         )
-        hid[:STREAM, :WIDTH] = t_dot(conv_low[:, units], cot_pad[...])
-        gqkv[:, :STREAM] = t_dot(n2[...], ghid_low[:, units])
+        hid[:STREAM] = t_dot(conv_low[unit], cot_pad[...])
+        gqkv[:, :STREAM] = t_dot(n2[...], ghid_low[unit])
 
         @pl.when(own == 0)
         def _():
@@ -981,14 +1049,17 @@
 
     lax.fori_loop(0, 2 * STREAMS, mlp, 0)
 
-    hid[:, :WIDTH] = dot_t(ghid_low[...], fc1_full[...])
+    every = range(2 * STREAMS)
+    joined = lambda ref, *rows: jnp.concatenate([ref[(u,) + rows] for u in every], axis=1)
+    for b in range(images):
+        hid[spans[b], :] = dot_t(joined(ghid_low, spans[b]), joined(fc1_blocks))
     gain_sum = jnp.zeros((1, WIDTH), f32)
     bias_sum = jnp.zeros((1, WIDTH), f32)
     proj_sum = jnp.zeros((1, WIDTH), f32)
     for b in range(images):
         middle = mid[spans[b], :]
         centred, r = centre(middle)
-        grad = hid[spans[b], :WIDTH]
+        grad = hid[spans[b], :]
         back, gain_rows = norm_back(centred, r, row(gain2), grad)
         gain_sum = gain_sum + add_rows(gain_rows)
         bias_sum = bias_sum + add_rows(grad)
@@ -998,70 +1069,71 @@
         proj_sum = proj_sum + add_rows(rounded.astype(f32))
         gmid_low[spans[b], :] = rounded
     gatt[...] = dot_t(gmid_low[...], wproj[...]).astype(bf16)
+    gproj[...] = t_dot(att[...], gmid_low[...])
     mix[...] = jnp.zeros_like(mix)
 
     def fold(values):
         values = values[:, :128] + values[:, 128:]
         return values[:8] + values[8:]
 
-    def put_weight(g, values):
-        ghat[1, :ROWS, KEYS * g : KEYS * (g + 1)] = values
-
-    def back_image(b, carry):
-        rows_of_image = pl.ds(pl.multiple_of(b * ROWS, 16), ROWS)
-        find_scores(b)
-        for p in range(HEADS // 2):
-            value = section(b, 2, p)
-            ahead = gatt[rows_of_image, 128 * p : 128 * p + 128]
-            put_weight(2 * p, dot_t(jnp.where(low_half, ahead, zero), value))
-            put_weight(2 * p + 1, dot_t(jnp.where(low_half, zero, ahead), value))
-        poll(BACK_PLAN, b, 0)
-
-        def back_step(step, carry):
-            rows = pl.ds(pl.multiple_of(step * 16, 16), 16)
-            weights = [ghat[1, rows, KEYS * g : KEYS * (g + 1)] for g in range(HEADS)]
-            mixed = []
-            for h in range(HEADS):
-                prob = probs[b, h, rows, :]
-                ahead = weights[0] * post[0, h]
-                for g in range(1, HEADS):
-                    ahead = ahead + weights[g] * post[g, h]
-                for g in range(HEADS):
-                    mix[HEADS * HEADS + g * HEADS + h] += fold(weights[g] * prob)
-                inner = jnp.sum(prob * ahead, axis=-1, keepdims=True)
-                mixed.append(prob * (ahead - inner))
-            for h in range(HEADS):
-                scores = score[h, rows, :]
-                sums = mixed[0] * pre[0, h]
-                for g in range(1, HEADS):
-                    sums = sums + mixed[g] * pre[g, h]
-                low[h, rows, :] = sums.astype(bf16)
-                for g in range(HEADS):
-                    mix[g * HEADS + h] += fold(mixed[g] * scores)
-            return carry
-
-        lax.fori_loop(0, 7, back_step, 0, unroll=7)
-        poll(BACK_PLAN, b, 1)
-        lax.fori_loop(7, ROWS // 16, back_step, 0, unroll=6)
-        poll(BACK_PLAN, b, 2)
-        queries, keys, values = [], [], []
-        for p in range(HEADS // 2):
-            query, key = section(b, 0, p, ROWS), section(b, 1, p)
-            ahead = gatt[rows_of_image, 128 * p : 128 * p + 128]
-            even, odd = low[2 * p], low[2 * p + 1]
-            queries.append(jnp.where(low_half, dot(even, key), dot(odd, key)) * 0.125)
-            keys.append(jnp.where(key_half, t_dot(even, query), t_dot(odd, query))[:ROWS] * 0.125)
-            values.append(
-                jnp.where(
-                    key_half, t_dot(attn[b, 2 * p], ahead), t_dot(attn[b, 2 * p + 1], ahead)
-                )[:ROWS]
-            )
-        gpacked[rows_of_image, :] = jnp.concatenate(queries + keys + values, axis=1).astype(bf16)
-        poll(BACK_PLAN, b, 3)
+    def weight_step(p, q, side):
+        ahead_p = gatt[rows_at(q, side), 128 * p : 128 * p + 128]
+        products(ahead_p, section(q, side, 2, p), weight[side], p)
+
+    def back_rows(rows, q, side):
+        given = [weight[side][g, rows, :] for g in range(HEADS)]
+        mixed = []
+        for h in range(HEADS):
+            prob = probs[side][q, h, rows, :]
+            ahead_h = given[0] * post[0, h]
+            for g in range(1, HEADS):
+                ahead_h = ahead_h + given[g] * post[g, h]
+            for g in range(HEADS):
+                mix[HEADS * HEADS + g * HEADS + h] += fold(given[g] * prob)
+            inner = jnp.sum(prob * ahead_h, axis=-1, keepdims=True)
+            mixed.append(prob * (ahead_h - inner))
+        for h in range(HEADS):
+            scores = score[side][h, rows, :]
+            total = mixed[0] * pre[0, h]
+            for g in range(1, HEADS):
+                total = total + mixed[g] * pre[g, h]
+            low[side][h, rows, :] = total.astype(bf16)
+            for g in range(HEADS):
+                mix[g * HEADS + h] += fold(mixed[g] * scores)
+
+    def value_step(p, q, side):
+        rows, lanes = rows_at(q, side), 2 * WIDTH + 128 * p
+        ahead_p = gatt[rows, 128 * p : 128 * p + 128]
+        even, odd = t_dot(attn[side][q, 2 * p], ahead_p), t_dot(attn[side][q, 2 * p + 1], ahead_p)
+        gpacked[rows, lanes : lanes + 128] = jnp.where(key_half, even, odd)[:ROWS].astype(bf16)
+
+    def query_step(p, q, side):
+        key = section(q, side, 1, p)
+        even, odd = dot(low[side][2 * p], key), dot(low[side][2 * p + 1], key)
+        gpacked[rows_at(q, side), 128 * p : 128 * p + 128] = (
+            jnp.where(low_half, even, odd) * 0.125
+        ).astype(bf16)
+
+    def key_step(p, q, side):
+        query, lanes = section(q, side, 0, p, ROWS), WIDTH + 128 * p
+        even, odd = t_dot(low[side][2 * p], query), t_dot(low[side][2 * p + 1], query)
+        gpacked[rows_at(q, side), lanes : lanes + 128] = (
+            jnp.where(key_half, even, odd)[:ROWS] * 0.125
+        ).astype(bf16)
+
+    def back_couple(q, carry):
+        skewed(
+            q,
+            (
+                (0, each(score_step, pairs) + each(weight_step, pairs)),
+                (1, each(back_rows, row_blocks)), (1, each(value_step, pairs)),
+                (2, each(query_step, pairs) + each(key_step, pairs)),
+            ),
+            lambda beat: poll(BACK_PLAN, q, beat),
+        )
         return carry
 
-    lax.fori_loop(0, images, back_image, 0)
-    gproj[...] = t_dot(att[...], gmid_low[...])
+    lax.fori_loop(0, images // 2, back_couple, 0)
     for n in range(0, 3 * WIDTH, WIDTH):
         gqkv[:, n : n + WIDTH] = t_dot(n1[...], gpacked[:, n : n + WIDTH])
 
@@ -1079,16 +1151,20 @@
             )
             yield index_of(d), tiles(both)
 
+    gather.finish()
+    for copy in forwards:
+        copy.wait_send()
     for side in range(2):
 
         @pl.when(core == side)
         def _():
             for index, values in pieces(1 - side):
-                att_bufs["out"][index] = values.astype(bf16)
-
-    exchange = remote(att_bufs["out"], att_bufs["came"], att_pair_sems, (0,), pair)
+                piece_full[index] = values.astype(bf16)
+
+    exchange = remote(piece_full, piece_other, att_pair_sems, (0,), pair)
     exchange.start()
-    hid[:, :WIDTH] = dot_t(gpacked[...], wqkv[...])
+    for b in range(images):
+        hid[spans[b], :] = dot_t(gpacked[spans[b], :], wqkv[...])
     attention = Sum(att_bufs["acc"], att_bufs["landing"], att_sems, PIECE_PARTS, where)
     exchange.wait_recv()
     for side in range(2):
@@ -1096,28 +1172,26 @@
         @pl.when(core == side)
         def _():
             for index, values in pieces(side):
-                came = att_bufs["came"][index].astype(f32)
+                came = piece_other[index].astype(f32)
                 att_bufs["acc"][index] = (values + came).astype(bf16)
 
     attention.start()
-    hid[:, WIDTH:] = dot(conv_low[...], fc2_full[...])
-    for b in range(images):
-        result = mid[spans[b], :] + (hid[spans[b], WIDTH:] + row(fc2b))
-        gtok_held[:, b, :] = result[:SEQ]
-    out_held[...] = gtok_held[...].astype(bf16)
-    leaving = [pltpu.make_async_copy(out_held, block_out, leave_sems.at[0])]
-    leaving[0].start()
+
+    for item in TAIL_PLAN:
+        act(*item)
     norm_gain = jnp.zeros((1, WIDTH), f32)
     norm_bias = jnp.zeros((1, WIDTH), f32)
+    flat = tok_held[...].reshape(SEQ, images * WIDTH)
     for b in range(images):
-        centred, r = centre(inputs[spans[b], :])
-        grad = hid[spans[b], :WIDTH]
+        rows = slice(b * ROWS, b * ROWS + SEQ)
+        centred, r = centre(flat[:, b * WIDTH : (b + 1) * WIDTH].astype(f32))
+        grad = hid[rows, :]
         back, gain_rows = norm_back(centred, r, row(gain1), grad)
         norm_gain = norm_gain + add_rows(gain_rows)
         norm_bias = norm_bias + add_rows(grad)
-        gtok_held[:, b, :] = (gmid[spans[b], :] + back)[:SEQ]
-    leaving.append(pltpu.make_async_copy(gtok_held, gtok_out, leave_sems.at[1]))
-    leaving[1].start()
+        gtok_held[:, b, :] = gmid[rows, :] + back
+    leaving = [pltpu.make_async_copy(gtok_held, gtok_out, leave_sems.at[1])]
+    leaving[0].start()
     rows_out[...] = jnp.concatenate(
         [norm_gain, norm_bias, proj_sum, gain_sum, bias_sum, cot_sum, jnp.zeros((2, WIDTH), f32)],
         axis=0,
@@ -1152,29 +1226,41 @@
             total = total + small_landed[0 if turn == 0 else 3 * turn - 2 + peer]
         return total
 
+    def second_projection(b):
+        second = dot(joined(conv_low, spans[b]), fc2_full[...])
+        result = mid[spans[b], :] + (second + row(fc2b))
+        out_wide[:, b, :] = result[:SEQ]
+
     small_start(0)
+    for b in range(images // 2):
+        second_projection(b)
     small_sums[1] = small_take(0)
     small_start(1)
+    act(2, 2)
     attention.act(0)
+    for b in range(images // 2, images):
+        second_projection(b)
+    out_held[...] = out_wide[...].astype(bf16)
+    leaving.append(pltpu.make_async_copy(out_held, block_out, leave_sems.at[0]))
+    leaving[1].start()
     small_sums[2] = small_take(1)
     small_start(2)
     for s in range(STREAMS):
         act(s, 3)
-    leaving.append(pltpu.make_async_copy(fulls_held, fulls_out, leave_sems.at[2]))
+    leaving.append(pltpu.make_async_copy(streams_came, fulls_out, leave_sems.at[2]))
     leaving[2].start()
     small_out[...] = small_take(2)
     attention.act(1)
     piece_out[...] = att_bufs["acc"][mine]
     for copy in leaving:
         copy.wait()
-    for copy in weights_come + forwards + [exchange]:
+    for copy in weights_come + [exchange]:
         copy.wait_send()
     for turn in range(3):
         for peer in range(small_counts[turn]):
             small_copy(turn, peer).wait_send()
     for s in range(STREAMS):
         exchange_copy(s).wait_send()
-    gather.finish()
     attention.finish()
     for s in range(STREAMS):
         sums[s].finish()
@@ -1203,7 +1289,7 @@
     def bufs(rows):
         buffer = lambda free: pltpu.VMEM((2,) * free + (rows, 128), bf16)
         return {
-            "acc": buffer(4), "out": buffer(4), "came": buffer(4),
+            "acc": buffer(4),
             "landing": [
                 pltpu.VMEM((3, 2, 2, rows, 128), bf16), pltpu.VMEM((3, rows, 128), bf16),
             ],
@@ -1211,40 +1297,48 @@
 
     stacked = lambda free: pltpu.VMEM((STREAMS,) + (2,) * free + (BLOCK, 128), bf16)
     tall = lambda width, dtype: pltpu.VMEM((total, width), dtype)
-    cube = lambda dtype: pltpu.VMEM((HEADS, ROWS, KEYS), dtype)
+    two = lambda shape, dtype, count=2: [pltpu.VMEM(shape, dtype) for _ in range(count)]
     scratch = dict(
         tok_held=pltpu.VMEM(tok.shape, bf16),
         cot_held=pltpu.VMEM(tok.shape, bf16),
         out_held=pltpu.VMEM(tok.shape, bf16),
         gtok_held=pltpu.VMEM(tok.shape, f32),
-        fulls_held=stacked(4),
+        out_wide=pltpu.VMEM(tok.shape, f32),
+        **{
+            name: pltpu.VMEM(value.shape, bf16)
+            for name, value in zip(("fwd", "inv", "kh", "kl", "bh", "bl"), consts)
+        },
         piece_full=pltpu.VMEM((2, 2, 2, 2, PIECE, 128), bf16),
         piece_other=pltpu.VMEM((2, 2, 2, 2, PIECE, 128), bf16),
         taps_pad=pltpu.VMEM((TAPS, half), f32),
         wqkv=pltpu.VMEM((WIDTH, 3 * WIDTH), bf16),
         wproj=pltpu.VMEM((WIDTH, WIDTH), bf16),
-        fc1_full=pltpu.VMEM((WIDTH, units), bf16),
+        fc1_blocks=pltpu.VMEM((2 * STREAMS, WIDTH, STREAM), bf16),
         fc2_full=pltpu.VMEM((units, WIDTH), bf16),
         conv_full=pltpu.VMEM((TAPS, units), bf16),
-        inputs=tall(WIDTH, f32),
         cot_pad=tall(WIDTH, bf16),
         n1=tall(WIDTH, bf16),
-        packed=pltpu.VMEM((images, KEYS, 3 * WIDTH), bf16),
-        score=cube(f32),
-        probs=pltpu.VMEM((images, HEADS, ROWS, KEYS), f32),
-        attn=pltpu.VMEM((images, HEADS, ROWS, KEYS), bf16),
+        packed=two((images // 2, KEYS, 3 * WIDTH), bf16),
+        score=two((HEADS, ROWS, KEYS), f32),
+        weight=two((HEADS, ROWS, KEYS), f32),
+        probs=two((images // 2, HEADS, ROWS, KEYS), f32),
+        attn=two((images // 2, HEADS, ROWS, KEYS), bf16),
         att=tall(WIDTH, bf16),
         mid=tall(WIDTH, f32),
         n2=tall(WIDTH, bf16),
-        turned=pltpu.VMEM((COEFS, units), f32),
-        ghat=pltpu.VMEM((images, COEFS, units), f32),
-        hid=tall(half, f32),
-        conv_low=tall(units, bf16),
-        ghid_low=tall(units, bf16),
+        turned=pltpu.VMEM((2 * STREAMS, COEFS, STREAM), f32),
+        ghat=pltpu.VMEM((2 * STREAMS, images, COEFS, STREAM), bf16),
+        hid=tall(WIDTH, f32),
+        hidden=two((ROWS, STREAM), f32),
+        slope=two((ROWS, STREAM), f32, images),
+        acted=two((ROWS, STREAM), bf16),
+        weights=pltpu.VMEM((WIDTH, STREAM), bf16),
+        conv_low=pltpu.VMEM((2 * STREAMS, total, STREAM), bf16),
+        ghid_low=pltpu.VMEM((2 * STREAMS, total, STREAM), bf16),
         gmid=tall(WIDTH, f32),
         gmid_low=tall(WIDTH, bf16),
         gatt=tall(WIDTH, bf16),
-        low=cube(bf16),
+        low=two((HEADS, ROWS, KEYS), bf16),
         gpacked=tall(3 * WIDTH, bf16),
         mix=pltpu.VMEM((2 * HEADS * HEADS, 8, 128), f32),
         rows_out=pltpu.VMEM((8, WIDTH), f32),
@@ -1261,11 +1355,15 @@
             pltpu.VMEM((STREAMS, 3, BLOCK, 128), bf16),
         ],
         gconv=pltpu.VMEM((TAPS, STREAM), f32),
+        made=two((COEFS, STREAM), f32),
+        ahead=two((COEFS, STREAM), bf16),
+        behind=two((COEFS, STREAM), bf16),
+        cross=pltpu.VMEM((COEFS, STREAM), f32),
         att_bufs=bufs(PIECE),
-        local_sems=pltpu.SemaphoreType.DMA((10,)),
+        local_sems=pltpu.SemaphoreType.DMA((9 + STREAMS,)),
         leave_sems=pltpu.SemaphoreType.DMA((3,)),
         gather_sems=pltpu.SemaphoreType.DMA((2, 2, 2, 3)),
-        gather_pair_sems=pltpu.SemaphoreType.DMA((2, 16)),
+        gather_pair_sems=pltpu.SemaphoreType.DMA((2, 15 + STREAMS)),
         stream_pair_sems=pltpu.SemaphoreType.DMA((2, STREAMS)),
         stream_sems=pltpu.SemaphoreType.DMA((STREAMS, 2, 2, 2, 2, 3)),
         att_sems=pltpu.SemaphoreType.DMA((2, 2, 2, 3)),
@@ -1273,7 +1371,7 @@
     )
     return pl.pallas_call(
         block_kernel,
-        in_specs=[smem] * 2 + [hbm] * 2 + [vmem] * 8 + [hbm] + [vmem] * 2 + [hbm] + [vmem] * len(consts),
+        in_specs=[smem] * 2 + [hbm] * 2 + [vmem] * 8 + [hbm] + [vmem] * 2 + [hbm] * 7 + [vmem],
         out_specs=[hbm] * 3 + [vmem] * 2,
         out_shape=[
             jax.ShapeDtypeStruct(tok.shape, bf16),
@@ -1295,11 +1393,10 @@
     )
 
 
-def finish_kernel(
-    totals_in, piece, small, out_in, gtok_in, gfc1_out, gb1, gconv, gfc2_out, gqkv, gproj, g1, b1,
-    pb, g2, b2, fb, pre, post, out, gtok, totals, out_held, gtok_held, gfc1, gfc2, taps, mixes,
-    sems,
-):
+def finish_kernel(totals_in, piece, small, out_in, gtok_in, *rest):
+    outs, rest = rest[:16], rest[16:]
+    held, (totals, out_held, gtok_held, taps, mixes, sems) = rest[:14], rest[14:]
+    gfc1, gb1, gconv, gfc2, gqkv, gproj, g1, b1, pb, g2, b2, fb, pre, post = held
     coming = [
         pltpu.make_async_copy(totals_in.at[s], totals.at[s], sems.at[s]) for s in range(STREAMS)
     ]
@@ -1330,6 +1427,8 @@
             mixes[index, g : g + 1, :HEADS] = line[:, start : start + HEADS]
     pre[...] = mixes[0, :HEADS, :HEADS] * 0.125
     post[...] = mixes[1, :HEADS, :HEADS]
+    for index in range(4, 14):
+        leave(held[index], outs[index])
     for s in range(STREAMS):
         side = slice(s * STREAM, (s + 1) * STREAM)
         coming[s].wait()
@@ -1338,16 +1437,18 @@
             gfc1[24 * d : 24 * d + 24, side] = untiles(block[:48], 2)
             gfc2[s * STREAM + 16 * d : s * STREAM + 16 * d + 16, :] = untiles(block[48:96], 3)
             taps[8 * d : 8 * d + 8, :] = block[96:104]
-        leave(gfc2.at[side], gfc2_out.at[side])
-        leave(gfc1.at[:, side], gfc1_out.at[:, side])
+        leave(gfc2.at[side], outs[3].at[side])
+        leave(gfc1.at[:, side], outs[0].at[:, side])
         filters = untiles(taps[...], 2)
         gconv[:, side] = filters[: KS * KS]
         gb1[side] = filters[KS * KS]
         if s == 0:
             coming[STREAMS].wait()
-            leave(gtok_held, gtok)
+            leave(gtok_held, outs[15])
             coming[STREAMS + 1].wait()
-            leave(out_held, out)
+            leave(out_held, outs[14])
+    leave(gconv, outs[2])
+    leave(gb1, outs[1])
     for copy in leaving:
         copy.wait()
 
@@ -1355,24 +1456,23 @@
 def call_finish(totals, piece, small, block_out, gtok, half):
     hbm = pl.BlockSpec(memory_space=pl.ANY)
     vmem = pl.BlockSpec(memory_space=pltpu.VMEM)
-    shape = lambda *dims: jax.ShapeDtypeStruct(dims, f32)
+    shapes = [
+        (WIDTH, half), (half,), (KS * KS, half), (half, WIDTH), (24, 3 * WIDTH // 2),
+        (24, WIDTH // 2),
+    ]
+    shapes += [(WIDTH,)] * 6 + [(HEADS, HEADS)] * 2
     return pl.pallas_call(
         finish_kernel,
         in_specs=[hbm] + [vmem] * 2 + [hbm] * 2,
-        out_specs=[hbm] + [vmem] * 2 + [hbm] + [vmem] * 10 + [hbm] * 2,
-        out_shape=[
-            shape(WIDTH, half), shape(half), shape(KS * KS, half), shape(half, WIDTH),
-            shape(24, 3 * WIDTH // 2), shape(24, WIDTH // 2),
-        ]
-        + [shape(WIDTH)] * 6
-        + [shape(HEADS, HEADS)] * 2
+        out_specs=[hbm] * 16,
+        out_shape=[jax.ShapeDtypeStruct(shape, f32) for shape in shapes]
         + [jax.ShapeDtypeStruct(v.shape, v.dtype) for v in (block_out, gtok)],
-        scratch_shapes=[
+        scratch_shapes=[pltpu.VMEM(shape, f32) for shape in shapes]
+        + [
             pltpu.VMEM(totals.shape, bf16),
             pltpu.VMEM(block_out.shape, bf16), pltpu.VMEM(gtok.shape, f32),
-            pltpu.VMEM((WIDTH, half), f32), pltpu.VMEM((half, WIDTH), f32),
             pltpu.VMEM((128, 128), f32), pltpu.VMEM((2, 8, 128), f32),
-            pltpu.SemaphoreType.DMA((STREAMS + 2 + 2 * STREAMS + 2,)),
+            pltpu.SemaphoreType.DMA((STREAMS + 2 + 2 * STREAMS + 14,)),
         ],
         compiler_params=pltpu.CompilerParams(vmem_limit_bytes=VMEM),
         name="finish",

time: 91.1 us -> 86.9 us (0.954)
  Pallas kernels: 90 us -> 85.8 us
    pallas_call x1, Pallas kernels: 84.9 us -> 81.2 us  [call_block(): pl.pallas_call(block_kernel, in_specs=[smem] * 2 + [hbm] * 2 + [vmem] * 8...]
where the time goes in v6:
time: 86.9 us; the launch traced here: 86.6 us
  Pallas kernels  85.8 us (99%)
    pallas_call x1, Pallas kernels, call_block(): pl.pallas_call(block_kernel, in_specs=[smem] * 2 + [hbm] * 2 + [vmem] * 8...  81.2 us
    pallas_call x1, Pallas kernels, call_finish(): pl.pallas_call(finish_kernel, in_specs=[hbm] + [vmem] * 2 + [hbm] * 2, ou...  4.53 us

profile of v6, /device:TPU:0, one launch (start us, length us, event | category | flops | bytes accessed | tf_op | source)
XLA Modules:
  0.0 86.6 jit_solution(10219256829684732815)
XLA Ops:
  0.7 81.2 %block.1 = (bf16[197,4,384]{2,1,0:T(4,128)(2,1)}, f32[197,4,384]{2,1,0:T(4,128)}, bf16[3,2,2,2,2,112,128]{6,5,4,3,2,1,0:T(8,128)(2,1)}, bf16[144,128]{1,0:T(8,128)(2,1)}, f32[32,128]{1,0:T(8,128)}) custom-call(f32[6,6]{1,0:T(8,128)} %pre.1, f32[6,6]{1,0:T(8,128)} %post.1, bf16[197,4,384]{2,1,0:T(4,128)(2,1)} %bitcast.4, bf16[197,4,384]{2,1,0:T(4,128)(2,1)} %bitcast.5, ...), custom_call_target="tpu_custom_call" | custom-call | tf_op jit(solution)/shard_map/block/pallas_call | solution.py:1372
  81.9 4.5 %finish.1 = (f32[384,768]{1,0:T(8,128)}, f32[768]{0:T(1024)}, f32[49,768]{1,0:T(8,128)}, f32[768,384]{1,0:T(8,128)}, f32[24,576]{1,0:T(8,128)}, /*index=5*/f32[2...) custom-call(bf16[3,2,2,2,2,112,128]{6,5,4,3,2,1,0:T(8,128)(2,1)} %ge, ...), custom_call_target="tpu_custom_call" | custom-call | tf_op jit(solution)/shard_map/finish/pallas_call | solution.py:1464

commit v7 on v6

--- a/solution.py
+++ b/solution.py
@@ -785,7 +785,7 @@
         centred, r = centre(mid[spans[b], :])
         n1[spans[b], :] = jnp.where(inside, centred * r * row(gain1) + row(bias1), 0.0).astype(bf16)
 
-    def prepare(side):
+    def prepare(side, begin, end):
         def prepare_unit(s, carry):
             block = side * STREAMS + s
             units = pl.ds(pl.multiple_of(block * STREAM, STREAM), STREAM)
@@ -796,16 +796,17 @@
                 ghat[block, b] = dot(fwd[...], grads[spans[b]]).astype(bf16)
             return carry
 
-        lax.fori_loop(0, STREAMS, prepare_unit, 0)
+        lax.fori_loop(begin, end, prepare_unit, 0)
 
     gather.act(0, forward)
     for copy in local[2:]:
         copy.wait()
-    prepare(core)
+    prepare(core, 0, STREAMS)
     for copy in weights_come:
         copy.wait_recv()
-    prepare(1 - core)
+    prepare(1 - core, 0, STREAMS - 1)
     gather.act(1, forward)
+    prepare(1 - core, STREAMS - 1, STREAMS)
     for copy in forwards:
         copy.wait_recv()
     width = qkv.shape[1]

time: 86.9 us -> 87.8 us (1.010)
  Pallas kernels: 85.8 us -> 86.7 us
    pallas_call x1, Pallas kernels: 81.2 us -> 82.1 us  [call_block(): pl.pallas_call(block_kernel, in_specs=[smem] * 2 + [hbm] * 2 + [vmem] * 8...]
where the time goes in v7:
time: 87.8 us; the launch traced here: 87.5 us
  Pallas kernels  86.7 us (99%)
    pallas_call x1, Pallas kernels, call_block(): pl.pallas_call(block_kernel, in_specs=[smem] * 2 + [hbm] * 2 + [vmem] * 8...  82.1 us
    pallas_call x1, Pallas kernels, call_finish(): pl.pallas_call(finish_kernel, in_specs=[hbm] + [vmem] * 2 + [hbm] * 2, ou...  4.53 us

profile of v7, /device:TPU:0, one launch (start us, length us, event | category | flops | bytes accessed | tf_op | source)
XLA Modules:
  0.0 87.5 jit_solution(10655270507952223203)
XLA Ops:
  0.7 82.1 %block.1 = (bf16[197,4,384]{2,1,0:T(4,128)(2,1)}, f32[197,4,384]{2,1,0:T(4,128)}, bf16[3,2,2,2,2,112,128]{6,5,4,3,2,1,0:T(8,128)(2,1)}, bf16[144,128]{1,0:T(8,128)(2,1)}, f32[32,128]{1,0:T(8,128)}) custom-call(f32[6,6]{1,0:T(8,128)} %pre.1, f32[6,6]{1,0:T(8,128)} %post.1, bf16[197,4,384]{2,1,0:T(4,128)(2,1)} %bitcast.4, bf16[197,4,384]{2,1,0:T(4,128)(2,1)} %bitcast.5, ...), custom_call_target="tpu_custom_call" | custom-call | tf_op jit(solution)/shard_map/block/pallas_call | solution.py:1373
  82.8 4.5 %finish.1 = (f32[384,768]{1,0:T(8,128)}, f32[768]{0:T(1024)}, f32[49,768]{1,0:T(8,128)}, f32[768,384]{1,0:T(8,128)}, f32[24,576]{1,0:T(8,128)}, /*index=5*/f32[2...) custom-call(bf16[3,2,2,2,2,112,128]{6,5,4,3,2,1,0:T(8,128)(2,1)} %ge, ...), custom_call_target="tpu_custom_call" | custom-call | tf_op jit(solution)/shard_map/finish/pallas_call | solution.py:1465
